TPU v7x, 512 devices: a whole 4x8x8 slice. The times are simulated.
512 devices in a mesh: sx: 8 (over y), sy: 4 (over z_hi), vel: 16 (over x, z_lo, core).
Axes of the slice: x: 4, y: 8, z: 8 (z_hi: 4, z_lo: 2; z = z_hi * 2 + z_lo), core: 2. Of those that a mesh axis runs over, the one named last changes fastest.
Arguments:
- distribution: float32 [128, 128, 13824], P('sx', 'sy', 'vel'), as said below
- cell_kind: int32 [128, 128], P('sx', 'sy'), may hold values from 0 to 2, as said below
- local_knudsen: float32 [128, 128], P('sx', 'sy'), may hold values from 0.3 to 30
Outputs:
- evolved: float32 [128, 128, 13824], P('sx', 'sy', 'vel')
Inputs may be any that keep to these rules, and one draw needn't show every extreme that they name: `cell_kind`: 0 marks a gas cell, 1 a wall cell, 2 an inflow cell. `distribution`: every entry is positive.
All inputs are finite; a program needn't handle non-finite values.
Results may differ from a plain program's by a relative error of at most 0.0003.
Values sent between devices are 32-bit elements; how exact they have to be, the bound alone decides.
No kernel may reach another device: no remote copies, remote signals or barrier semaphores. Data moves between devices by JAX's collectives and lax.ppermute only.
A program may use at most 128 MiB of HBM per device.

v0:
```python
import math

import jax
import jax.numpy as jnp
from jax import lax
from jax.sharding import PartitionSpec as P

NVX = 24
STEPS = 2


VEL_LIMIT = 4.8
CLOCK_ADVANCE = 0.09
VISCOUS_RATIO = 2.0 / 3.0
WALL_TEMP = 1.0
INFLOW_DENSITY = 12.0
INFLOW_SPEED = 0.5
INFLOW_TEMP = 1.0


def extended(shard, sides, width):
    for axis, dim in sides:
        devices, length = (lax.axis_size(axis), shard.shape[dim])
        up = [(i, (i + 1) % devices) for i in range(devices)]
        down = [(j, i) for i, j in up]
        last = lax.slice_in_dim(shard, length - width, length, axis=dim)
        initial = lax.slice_in_dim(shard, 0, width, axis=dim)
        before = lax.ppermute(last, axis, up)
        after = lax.ppermute(initial, axis, down)
        shard = jnp.concatenate([before, shard, after], axis=dim)
    return shard


def widen_last_index(value):
    return value[..., None]


def line_value(points):
    spacing = 2.0 * VEL_LIMIT / NVX
    return (
        ((points // 2).astype(jnp.float32) + 0.5)
        * spacing
        * (2 * (points % 2) - 1).astype(jnp.float32)
    )


def conserved_integrals(quadrature_totals):
    molecule_crowding = quadrature_totals[0]
    mean_motion_x = quadrature_totals[1] / molecule_crowding
    mean_motion_y = quadrature_totals[2] / molecule_crowding
    mean_motion_z = quadrature_totals[3] / molecule_crowding
    molecular_agitation = (
        quadrature_totals[4] / molecule_crowding
        - (
            mean_motion_x * mean_motion_x
            + mean_motion_y * mean_motion_y
            + mean_motion_z * mean_motion_z
        )
    ) / 3.0
    return (molecule_crowding, mean_motion_x, mean_motion_y, mean_motion_z, molecular_agitation)


def relax(present_state, macro_integrals, local_knudsen, cell_kind, speed_x, speed_y, speed_z):
    (
        molecule_crowding,
        mean_motion_x,
        mean_motion_y,
        mean_motion_z,
        molecular_agitation,
        conduction_x,
        conduction_y,
        conduction_z,
    ) = macro_integrals
    relative_motion_component = speed_x - widen_last_index(mean_motion_x)
    drift_y = speed_y - widen_last_index(mean_motion_y)
    drift_z = speed_z - widen_last_index(mean_motion_z)
    relative_motion_norm = (
        relative_motion_component * relative_motion_component
        + drift_y * drift_y
        + drift_z * drift_z
    )
    maxwell_profile = widen_last_index(
        molecule_crowding / (2.0 * math.pi * molecular_agitation) ** 1.5
    ) * jnp.exp(-relative_motion_norm / widen_last_index(2.0 * molecular_agitation))
    thermal_dot_offset = (
        relative_motion_component * widen_last_index(conduction_x)
        + drift_y * widen_last_index(conduction_y)
        + drift_z * widen_last_index(conduction_z)
    )
    leading_coefficient = (
        (1.0 - VISCOUS_RATIO)
        * thermal_dot_offset
        / widen_last_index(5.0 * molecule_crowding * molecular_agitation * molecular_agitation)
        * (relative_motion_norm / widen_last_index(molecular_agitation) - 5.0)
    )
    shakhov_closure_model = maxwell_profile * (1.0 + leading_coefficient)
    remaining_indicator = jnp.exp(
        -CLOCK_ADVANCE * molecule_crowding * jnp.sqrt(molecular_agitation) / local_knudsen
    )
    medium_cells = shakhov_closure_model + (
        present_state - shakhov_closure_model
    ) * widen_last_index(remaining_indicator)
    speed_sq = speed_x * speed_x + speed_y * speed_y + speed_z * speed_z
    wall = widen_last_index(molecule_crowding / (2.0 * math.pi * WALL_TEMP) ** 1.5) * jnp.exp(
        -speed_sq / (2.0 * WALL_TEMP)
    )
    shifted = speed_x - INFLOW_SPEED
    inflow = (
        INFLOW_DENSITY
        / (2.0 * math.pi * INFLOW_TEMP) ** 1.5
        * jnp.exp(
            -(shifted * shifted + speed_y * speed_y + speed_z * speed_z) / (2.0 * INFLOW_TEMP)
        )
    )
    return jnp.where(
        widen_last_index(cell_kind == 1),
        wall,
        jnp.where(widen_last_index(cell_kind == 2), inflow, medium_cells),
    )


def minmod(left, right):
    return 0.5 * (jnp.sign(left) + jnp.sign(right)) * jnp.minimum(jnp.abs(left), jnp.abs(right))


def sweep_strip(strip, speed, axis):
    length = strip.shape[axis]
    diff = lax.slice_in_dim(strip, 1, length, axis=axis) - lax.slice_in_dim(
        strip, 0, length - 1, axis=axis
    )
    slope = minmod(
        lax.slice_in_dim(diff, 0, length - 2, axis=axis),
        lax.slice_in_dim(diff, 1, length - 1, axis=axis),
    )
    cells = lax.slice_in_dim(strip, 1, length - 1, axis=axis)
    forward = jnp.maximum(speed, 0.0)
    backward = jnp.minimum(speed, 0.0)
    right = forward * (
        lax.slice_in_dim(cells, 0, length - 3, axis=axis)
        + 0.5 * lax.slice_in_dim(slope, 0, length - 3, axis=axis)
    ) + backward * (
        lax.slice_in_dim(cells, 1, length - 2, axis=axis)
        - 0.5 * lax.slice_in_dim(slope, 1, length - 2, axis=axis)
    )
    return lax.slice_in_dim(right, 1, length - 3, axis=axis) - lax.slice_in_dim(
        right, 0, length - 4, axis=axis
    )


def transport(strip_x, strip_y, speed_x, speed_y):
    centre = strip_x[2:-2]
    change = sweep_strip(strip_x, speed_x, 0) + sweep_strip(strip_y, speed_y, 1)
    return centre - CLOCK_ADVANCE * change


def face_strips(values):
    padded = extended(values, (("sx", 0), ("sy", 1)), 2)
    return (padded[:, 2:-2], padded[2:-2, :])


def moments(present_state, speed_x, speed_y, speed_z, weight):
    ones = jnp.ones_like(speed_x)
    speed_sq = speed_x * speed_x + speed_y * speed_y + speed_z * speed_z
    basis = jnp.stack([ones, speed_x, speed_y, speed_z, speed_sq]) * weight
    local = jnp.einsum("kv,xyv->kxy", basis, present_state, precision=lax.Precision.HIGHEST)
    quadrature_totals = lax.psum(local, "vel")
    molecule_crowding, mean_motion_x, mean_motion_y, mean_motion_z, molecular_agitation = (
        conserved_integrals(quadrature_totals)
    )
    relative_motion_component = speed_x - widen_last_index(mean_motion_x)
    drift_y = speed_y - widen_last_index(mean_motion_y)
    drift_z = speed_z - widen_last_index(mean_motion_z)
    relative_motion_norm = (
        relative_motion_component * relative_motion_component
        + drift_y * drift_y
        + drift_z * drift_z
    )
    weighted = relative_motion_norm * present_state
    partial_heat = jnp.stack(
        [
            jnp.sum(relative_motion_component * weighted, axis=-1),
            jnp.sum(drift_y * weighted, axis=-1),
            jnp.sum(drift_z * weighted, axis=-1),
        ]
    ) * (0.5 * weight)
    conduction_triple = lax.psum(partial_heat, "vel")
    conduction_x, conduction_y, conduction_z = (
        conduction_triple[0],
        conduction_triple[1],
        conduction_triple[2],
    )
    return (
        molecule_crowding,
        mean_motion_x,
        mean_motion_y,
        mean_motion_z,
        molecular_agitation,
        conduction_x,
        conduction_y,
        conduction_z,
    )


def body(distribution, cell_kind, local_knudsen):
    count = distribution.shape[2]
    index = lax.axis_index("vel") * count + jnp.arange(count, dtype=jnp.int32)
    spacing = 2.0 * VEL_LIMIT / NVX
    speed_x = line_value(index % NVX)
    speed_y = line_value(index // NVX % NVX)
    speed_z = line_value(index // (NVX * NVX))
    weight = spacing**3
    present_state = distribution
    for section_index in range(STEPS):
        macro_integrals = moments(present_state, speed_x, speed_y, speed_z, weight)
        relaxed = relax(
            present_state, macro_integrals, local_knudsen, cell_kind, speed_x, speed_y, speed_z
        )
        strip_x, strip_y = face_strips(relaxed)
        present_state = transport(strip_x, strip_y, speed_x, speed_y)
    return present_state


def solution(mesh):
    return jax.shard_map(
        body,
        mesh=mesh,
        in_specs=(P("sx", "sy", "vel"), P("sx", "sy"), P("sx", "sy")),
        out_specs=P("sx", "sy", "vel"),
        check_vma=False,
    )
```

profile of v0, /device:TPU:8, one launch (start us, length us, event | category | flops | bytes accessed | tf_op | source)
XLA Modules:
  0.0 306.2 jit_solution(1381958763231719990)
XLA Ops:
  0.0 0.1 fusion.121
  0.1 0.2 fusion.129
  0.5 5.8 %fusion.66 = f32[5,16,32]{2,0,1:T(8,128)S(1)} fusion(f32[16,32,864]{2,1,0:T(8,128)} %param.3, f32[5,864]{1,0:T(8,128)S(1)} %stack.36), kind=kOutput, calls=%fused_computation.130 | convolution fusion | flops 26546400 | bytes 1796992 | tf_op jit(solution)/shard_map/kv,xyv->kxy/dot_general | solution.py:165
  6.2 56.8 %psum.28 = f32[5,16,32]{2,0,1:T(8,128)S(1)} all-reduce(f32[5,16,32]{2,0,1:T(8,128)S(1)} %fusion.66), channel_id=1, replica_groups=mesh['sx'=8,'sy'=4,'vel'=16] {'vel'}, use_global_device_ids=true, to_apply=%region_0.1 | all-reduce | flops 2560 | bytes 20480 | tf_op jit(solution)/shard_map/psum | solution.py:166
  63.1 1.3 fusion.22
  64.4 52.9 %psum.29 = f32[3,16,32]{2,1,0:T(8,128)S(1)} all-reduce(f32[3,16,32]{2,1,0:T(8,128)S(1)} %maximum_multiply_fusion), channel_id=1, replica_groups=mesh['sx'=8,'sy'=4,'vel'=16] {'vel'}, use_global_device_ids=true, to_apply=%region_4.5 | all-reduce | flops 1536 | bytes 12288 | tf_op jit(solution)/shard_map/psum | solution.py:186
  117.4 2.6 select_select_fusion.1
  120.1 3.8 %collective-permute-start.1 = (f32[2,32,864]{2,1,0:T(8,128)S(1)}, f32[2,32,864]{2,1,0:T(8,128)S(1)}, u32[]{:S(2)}, u32[]{:S(2)}) collective-permute-start(f32[2,32,864]{2,1,0:T(8,128)S(1)} %get-tuple-element.28), channel_id=1, source_target_pairs={{64,0},{128,64},{192,128},{256,192},{320,256},{384,320},{448,384},... | collective-permute-start | bytes 663560 | tf_op jit(solution)/shard_map/ppermute | solution.py:29
  123.9 2.0 collective-permute-start
  126.0 2.0 collective-permute-done.1
  128.0 3.8 %collective-permute-done = f32[2,32,864]{2,1,0:T(8,128)S(1)} collective-permute-done((f32[2,32,864]{2,1,0:T(8,128)S(1)}, f32[2,32,864]{2,1,0:T(8,128)S(1)}, u32[]{:S(2)}, u32[]{:S(2)}) %collective-permute-start) | collective-permute-done | bytes 221216 | tf_op jit(solution)/shard_map/ppermute | solution.py:28
  131.8 0.1 pad_maximum_fusion.23
  132.0 10.0 %collective-permute-start.3 = (f32[20,2,864]{2,0,1:T(8,128)S(1)}, f32[20,2,864]{2,0,1:T(8,128)S(1)}, u32[]{:S(2)}, u32[]{:S(2)}) collective-permute-start(f32[20,2,864]{2,0,1:T(8,128)S(1)} %copy.44), channel_id=1, source_target_pairs={{16,0},{32,16},{48,32},{0,48},{17,1},{33,17},{49,33},{1,49},{18,2}... | collective-permute-start | bytes 414728 | tf_op jit(solution)/shard_map/ppermute | solution.py:29
  142.0 2.1 collective-permute-start.2
  144.1 0.2 pad_maximum_fusion.14
  144.3 0.2 slice_subtract_fusion.3
  144.4 0.8 minimum_multiply_fusion.3
  145.3 0.4 fusion.17
  145.7 0.1 copy.46
  145.8 5.6 %collective-permute-done.2 = f32[20,2,864]{2,0,1:T(8,128)S(1)} collective-permute-done((f32[20,2,864]{2,0,1:T(8,128)S(1)}, f32[20,2,864]{2,0,1:T(8,128)S(1)}, u32[]{:S(2)}, u32[]{:S(2)}) %collective-permute-start.2) | collective-permute-done | bytes 138272 | tf_op jit(solution)/shard_map/ppermute | solution.py:28
  151.5 0.3 pad_maximum_fusion
  151.8 0.2 slice_subtract_fusion.1
  152.1 1.6 minimum_multiply_fusion.1
  153.7 1.4 fusion.7
  155.2 3.1 %fusion.63 = f32[16,32,864]{2,1,0:T(8,128)S(1)} fusion(f32[16,33,864]{2,1,0:T(8,128)S(1)} %fusion.7, f32[17,32,864]{2,1,0:T(8,128)S(1)} %fusion.17, f32[16,32]{1,0:T(8,128)S(1)} %get-tuple-element.44, f32[16,32,864]{2,1,0:T(8,128)S(1)} %copy-done.1, f32[16,32]{1,0:T(8,128)S(1)} %get-tuple-element.51, f32[16,32]{1,0:T(8,128)S(1)} %get-tuple-element.43, ...), kind=kLoop, calls=%fused_computation.120 | loop fusion | flops 15040512 | bytes 10659712 | tf_op jit(solution)/shard_map/sub | solution.py:153
  158.3 4.2 %fusion.64 = f32[5,16,32]{2,0,1:T(8,128)S(1)} fusion(f32[16,32,864]{2,1,0:T(8,128)S(1)} %fusion.63, f32[5,864]{1,0:T(8,128)S(1)} %stack.36), kind=kOutput, calls=%fused_computation.128 | convolution fusion | flops 26546400 | bytes 1796992 | tf_op jit(solution)/shard_map/kv,xyv->kxy/dot_general | solution.py:165
  162.5 53.8 %psum.30 = f32[5,16,32]{2,1,0:T(8,128)S(1)} all-reduce(f32[5,16,32]{2,1,0:T(8,128)S(1)} %copy.48), channel_id=1, replica_groups=mesh['sx'=8,'sy'=4,'vel'=16] {'vel'}, use_global_device_ids=true, to_apply=%region_5.6 | all-reduce | flops 2560 | bytes 20480 | tf_op jit(solution)/shard_map/psum | solution.py:166
  216.4 1.3 fusion.41
  217.7 52.9 %psum.31 = f32[3,16,32]{2,1,0:T(8,128)S(1)} all-reduce(f32[3,16,32]{2,1,0:T(8,128)S(1)} %maximum_multiply_fusion.1), channel_id=1, replica_groups=mesh['sx'=8,'sy'=4,'vel'=16] {'vel'}, use_global_device_ids=true, to_apply=%region_9.10 | all-reduce | flops 1536 | bytes 12288 | tf_op jit(solution)/shard_map/psum | solution.py:186
  270.6 2.6 select_select_fusion
  273.2 5.4 %collective-permute-start.5 = (f32[2,32,864]{2,1,0:T(8,128)S(1)}, f32[2,32,864]{2,1,0:T(8,128)S(1)}, u32[]{:S(2)}, u32[]{:S(2)}) collective-permute-start(f32[2,32,864]{2,1,0:T(8,128)S(1)} %get-tuple-element.26), channel_id=1, source_target_pairs={{64,0},{128,64},{192,128},{256,192},{320,256},{384,320},{448,384},... | collective-permute-start | bytes 663560 | tf_op jit(solution)/shard_map/ppermute | solution.py:29
  278.6 2.1 collective-permute-start.4
  280.8 1.4 collective-permute-done.5
  282.1 4.4 %collective-permute-done.4 = f32[2,32,864]{2,1,0:T(8,128)S(1)} collective-permute-done((f32[2,32,864]{2,1,0:T(8,128)S(1)}, f32[2,32,864]{2,1,0:T(8,128)S(1)}, u32[]{:S(2)}, u32[]{:S(2)}) %collective-permute-start.4) | collective-permute-done | bytes 221216 | tf_op jit(solution)/shard_map/ppermute | solution.py:28
  286.5 0.1 pad_maximum_fusion.21
  286.7 2.3 collective-permute-start.7
  289.0 4.4 %collective-permute-start.6 = (f32[20,2,864]{2,0,1:T(8,128)S(1)}, f32[20,2,864]{2,0,1:T(8,128)S(1)}, u32[]{:S(2)}, u32[]{:S(2)}) collective-permute-start(f32[20,2,864]{2,0,1:T(8,128)S(1)} %copy.49), channel_id=1, source_target_pairs={{0,16},{16,32},{32,48},{48,0},{1,17},{17,33},{33,49},{49,1},{2,18}... | collective-permute-start | bytes 414728 | tf_op jit(solution)/shard_map/ppermute | solution.py:28
  293.4 0.2 pad_maximum_fusion.15
  293.6 0.2 slice_subtract_fusion.2
  293.8 0.8 minimum_multiply_fusion.2
  294.6 0.4 fusion.12
  295.1 0.1 copy.53
  295.1 3.3 %collective-permute-done.6 = f32[20,2,864]{2,0,1:T(8,128)S(1)} collective-permute-done((f32[20,2,864]{2,0,1:T(8,128)S(1)}, f32[20,2,864]{2,0,1:T(8,128)S(1)}, u32[]{:S(2)}, u32[]{:S(2)}) %collective-permute-start.6) | collective-permute-done | bytes 138272 | tf_op jit(solution)/shard_map/ppermute | solution.py:28
  298.5 0.3 pad_maximum_fusion.1
  298.8 0.2 slice_subtract_fusion
  299.1 1.6 minimum_multiply_fusion
  300.7 1.4 fusion.2
  302.1 4.1 %fusion.60 = f32[16,32,864]{2,1,0:T(8,128)} fusion(f32[16,33,864]{2,1,0:T(8,128)S(1)} %fusion.2, f32[17,32,864]{2,1,0:T(8,128)S(1)} %fusion.12, f32[16,32]{1,0:T(8,128)S(1)} %get-tuple-element.35, f32[16,32,864]{2,1,0:T(8,128)S(1)} %fusion.63, f32[16,32]{1,0:T(8,128)S(1)} %get-tuple-element.46, f32[16,32]{1,0:T(8,128)S(1)} %get-tuple-element.34, ...), kind=kLoop, calls=%fused_computation.115 | loop fusion | flops 15040512 | bytes 10659712 | tf_op jit(solution)/shard_map/sub | solution.py:153
  (36 shorter events, 0.7 us)
Async XLA Ops:
  0.0 63.1 %copy-start = (f32[16,32,864]{2,1,0:T(8,128)S(1)}, f32[16,32,864]{2,1,0:T(8,128)}, u32[]{:S(2)}) copy-start(f32[16,32,864]{2,1,0:T(8,128)} %param.3) | copy-start | bytes 5308420
  0.5 116.9 %copy-start.3 = (s32[16,32]{1,0:T(8,128)S(1)}, s32[16,32]{1,0:T(8,128)}, u32[]{:S(2)}) copy-start(s32[16,32]{1,0:T(8,128)} %param.4) | copy-start | bytes 6148
  0.5 116.9 %copy-start.2 = (f32[16,32]{1,0:T(8,128)S(1)}, f32[16,32]{1,0:T(8,128)}, u32[]{:S(2)}) copy-start(f32[16,32]{1,0:T(8,128)} %param.5) | copy-start | bytes 6148
  120.1 7.9 %collective-permute-start.1 = (f32[2,32,864]{2,1,0:T(8,128)S(1)}, f32[2,32,864]{2,1,0:T(8,128)S(1)}, u32[]{:S(2)}, u32[]{:S(2)}) collective-permute-start(f32[2,32,864]{2,1,0:T(8,128)S(1)} %get-tuple-element.28), channel_id=1, source_target_pairs={{64,0},{128,64},{192,128},{256,192},{320,256},{384,320},{448,384},... | collective-permute-start | bytes 663560 | tf_op jit(solution)/shard_map/ppermute | solution.py:29
  123.9 7.9 %collective-permute-start = (f32[2,32,864]{2,1,0:T(8,128)S(1)}, f32[2,32,864]{2,1,0:T(8,128)S(1)}, u32[]{:S(2)}, u32[]{:S(2)}) collective-permute-start(f32[2,32,864]{2,1,0:T(8,128)S(1)} %get-tuple-element.27), channel_id=1, source_target_pairs={{0,64},{64,128},{128,192},{192,256},{256,320},{320,384},{384,448},... | collective-permute-start | bytes 663560 | tf_op jit(solution)/shard_map/ppermute | solution.py:28
  132.0 13.8 %collective-permute-start.3 = (f32[20,2,864]{2,0,1:T(8,128)S(1)}, f32[20,2,864]{2,0,1:T(8,128)S(1)}, u32[]{:S(2)}, u32[]{:S(2)}) collective-permute-start(f32[20,2,864]{2,0,1:T(8,128)S(1)} %copy.44), channel_id=1, source_target_pairs={{16,0},{32,16},{48,32},{0,48},{17,1},{33,17},{49,33},{1,49},{18,2}... | collective-permute-start | bytes 414728 | tf_op jit(solution)/shard_map/ppermute | solution.py:29
  142.0 9.4 %collective-permute-start.2 = (f32[20,2,864]{2,0,1:T(8,128)S(1)}, f32[20,2,864]{2,0,1:T(8,128)S(1)}, u32[]{:S(2)}, u32[]{:S(2)}) collective-permute-start(f32[20,2,864]{2,0,1:T(8,128)S(1)} %copy.42), channel_id=1, source_target_pairs={{0,16},{16,32},{32,48},{48,0},{1,17},{17,33},{33,49},{49,1},{2,18}... | collective-permute-start | bytes 414728 | tf_op jit(solution)/shard_map/ppermute | solution.py:28
  153.7 1.5 copy-start.1
  273.2 8.9 %collective-permute-start.5 = (f32[2,32,864]{2,1,0:T(8,128)S(1)}, f32[2,32,864]{2,1,0:T(8,128)S(1)}, u32[]{:S(2)}, u32[]{:S(2)}) collective-permute-start(f32[2,32,864]{2,1,0:T(8,128)S(1)} %get-tuple-element.26), channel_id=1, source_target_pairs={{64,0},{128,64},{192,128},{256,192},{320,256},{384,320},{448,384},... | collective-permute-start | bytes 663560 | tf_op jit(solution)/shard_map/ppermute | solution.py:29
  278.6 7.9 %collective-permute-start.4 = (f32[2,32,864]{2,1,0:T(8,128)S(1)}, f32[2,32,864]{2,1,0:T(8,128)S(1)}, u32[]{:S(2)}, u32[]{:S(2)}) collective-permute-start(f32[2,32,864]{2,1,0:T(8,128)S(1)} %get-tuple-element.25), channel_id=1, source_target_pairs={{0,64},{64,128},{128,192},{192,256},{256,320},{320,384},{384,448},... | collective-permute-start | bytes 663560 | tf_op jit(solution)/shard_map/ppermute | solution.py:28
  286.7 8.4 %collective-permute-start.7 = (f32[20,2,864]{2,0,1:T(8,128)S(1)}, f32[20,2,864]{2,0,1:T(8,128)S(1)}, u32[]{:S(2)}, u32[]{:S(2)}) collective-permute-start(f32[20,2,864]{2,0,1:T(8,128)S(1)} %copy.51), channel_id=1, source_target_pairs={{16,0},{32,16},{48,32},{0,48},{17,1},{33,17},{49,33},{1,49},{18,2}... | collective-permute-start | bytes 414728 | tf_op jit(solution)/shard_map/ppermute | solution.py:29
  289.0 9.4 %collective-permute-start.6 = (f32[20,2,864]{2,0,1:T(8,128)S(1)}, f32[20,2,864]{2,0,1:T(8,128)S(1)}, u32[]{:S(2)}, u32[]{:S(2)}) collective-permute-start(f32[20,2,864]{2,0,1:T(8,128)S(1)} %copy.49), channel_id=1, source_target_pairs={{0,16},{16,32},{32,48},{48,0},{1,17},{17,33},{33,49},{49,1},{2,18}... | collective-permute-start | bytes 414728 | tf_op jit(solution)/shard_map/ppermute | solution.py:28
where the time goes:
time: 307 us; the launch traced here: 306 us
  blocking collectives  216 us (70%)
  starting transfers between devices  32.2 us (10%)
  other arithmetic  26.1 us (9%)
  waiting for transfers between devices  20.5 us (7%)
  matrix products  9.9 us (3%)
    psum x2, blocking collectives, moments(): quadrature_totals = lax.psum(local, 'vel')  111 us
    psum x2, blocking collectives, moments(): conduction_triple = lax.psum(partial_heat, 'vel')  106 us
    ppermute x4, starting transfers between devices, extended(): after = lax.ppermute(initial, axis, down)  21.5 us
    ppermute x4, waiting for transfers between devices, extended(): before = lax.ppermute(last, axis, up)  17.1 us
    ppermute x4, starting transfers between devices, extended(): before = lax.ppermute(last, axis, up)  10.7 us
    dot_general x2, matrix products, moments(): jnp.einsum('kv,xyv->kxy', basis, present_state, precision=lax.Precision.H...  9.9 us
    sub x2, other arithmetic, transport(): return centre - CLOCK_ADVANCE * change  7.19 us
  transfers between devices with their start and end apart: 8, of which 6 were waited for; matrix products, arithmetic and copies ran while one was open for 1% of the time, Pallas kernels for 0%

commit v1 on v0

v1 whole, which is shorter than its diff:
```python
import functools
import math

import jax
import jax.numpy as jnp
from jax import lax
from jax.experimental import pallas as pl
from jax.experimental.pallas import tpu as pltpu
from jax.sharding import PartitionSpec as P

NVX = 24
STEPS = 2

VEL_LIMIT = 4.8
CLOCK_ADVANCE = 0.09
VISCOUS_RATIO = 2.0 / 3.0
WALL_TEMP = 1.0
INFLOW_DENSITY = 12.0
INFLOW_SPEED = 0.5
INFLOW_TEMP = 1.0

SPACING = 2.0 * VEL_LIMIT / NVX
WEIGHT = SPACING**3
LOG2E = 1.0 / math.log(2.0)

LANE = 128
REACH = 2 * STEPS
MOMENTS = 13
COEFFICIENTS = 32
CHUNKS = 8
F32 = jnp.float32
BF16 = jnp.bfloat16


def lattice(first, velocities, lanes):
    lane = lax.broadcasted_iota(jnp.int32, (1, lanes), 1)
    held = lane < velocities
    index = jnp.where(held, first + lane, 0).astype(F32)

    def split(value, by):
        over = jnp.floor((value + 0.5) * (1.0 / by))
        return over, value - by * over

    def line(points):
        half, odd = split(points, 2.0)
        return jnp.where(odd > 0.5, half, -half - 1.0)

    index, a = split(index, float(NVX))
    c, b = split(index, float(NVX))
    return line(a), line(b), line(c), held, lane


def tables_kernel(velocities, first_ref, moment_ref, relax_ref, courant_ref, turn_ref):
    lanes = courant_ref.shape[1]
    a, b, c, held, lane = lattice(first_ref[0], velocities, lanes)
    zero, one = jnp.zeros((1, lanes), F32), jnp.ones((1, lanes), F32)
    square = a * a + b * b + c * c
    cubic = [a * square, b * square, c * square]
    high = [v.astype(BF16).astype(F32) for v in cubic]
    low = [v - h for v, h in zip(cubic, high)]
    rows = [one, a, b, c, a * a, b * b, c * c, a * b, a * c, b * c, *high, *low]
    rows = [jnp.where(held, v, 0.0) for v in rows]
    rows += [jnp.where(lane == velocities + i, 1.0, 0.0) for i in range(2)]
    turn_ref[...] = jnp.zeros_like(turn_ref)
    for i, value in enumerate(rows):
        turn_ref[i : i + 1, :] = value
    for start in range(0, lanes, LANE):
        turned = turn_ref[:, start : start + LANE].T
        moment_ref[start : start + LANE, :] = turned.astype(BF16)

    half = 0.5 * (square + a + b + c)
    turn_ref[...] = jnp.zeros_like(turn_ref)
    for i, value in enumerate((one, a, b, c, half)):
        for j in range(3):
            turn_ref[3 * i + j : 3 * i + j + 1, :] = jnp.where(held, value, 0.0)
    for i, value in enumerate((one, a, b, c)):
        for j in range(2):
            at = COEFFICIENTS + 15 + 2 * i + j
            turn_ref[at : at + 1, :] = jnp.where(held, value, 0.0)
    for start in range(0, lanes, LANE):
        for i in range(2):
            part = turn_ref[i * COEFFICIENTS : (i + 1) * COEFFICIENTS, start : start + LANE]
            at = 2 * start + i * LANE
            relax_ref[:, at : at + LANE] = part.astype(BF16)
    row = lax.broadcasted_iota(jnp.int32, (COEFFICIENTS, LANE), 0)
    for i in range(2):
        at = 2 * lanes + i * LANE
        picked = jnp.where((row >= 23 + 3 * i) & (row < 26 + 3 * i), 1.0, 0.0)
        relax_ref[:, at : at + LANE] = picked.astype(BF16)

    speeds = [jnp.where(held, CLOCK_ADVANCE * SPACING * (v + 0.5), 0.0) for v in (a, b)]
    signs = [jnp.where(v >= 0.0, 0.5, -0.5) for v in (a, b)]
    for i, value in enumerate([*speeds, *signs, zero, zero, zero, zero]):
        courant_ref[i : i + 1, :] = value


def cell_columns(kind_ref, knudsen_ref):
    nx, ny = kind_ref.shape
    both = jnp.concatenate([knudsen_ref[...], kind_ref[...].astype(F32)], axis=0)
    return jnp.concatenate([both, jnp.zeros((2 * nx, LANE - ny), F32)], axis=1).T


def widen(state, columns, x, nx, velocities, out_ref, at):
    ny, lanes = state.shape[0], out_ref.shape[1]
    full = velocities // LANE * LANE
    out_ref[at : at + ny, :full] = state[:, :full]
    last = jnp.concatenate(
        [state[:, full:], jnp.zeros((ny, lanes - velocities), F32)], axis=1
    )
    lane = lax.broadcasted_iota(jnp.int32, (ny, LANE), 1) + full
    last = jnp.where(lane == velocities, columns[:ny, x : x + 1], last)
    last = jnp.where(lane == velocities + 1, columns[:ny, nx + x : nx + x + 1], last)
    out_ref[at : at + ny, full:] = last


def sides_kernel(velocities, kind_ref, knudsen_ref, first_ref, last_ref, low_ref, high_ref):
    nx, ny = kind_ref.shape
    columns = cell_columns(kind_ref, knudsen_ref)
    for i in range(REACH):
        widen(last_ref[i], columns, nx - REACH + i, nx, velocities, low_ref, i * ny)
        widen(first_ref[i], columns, i, nx, velocities, high_ref, i * ny)


def own_kernel(velocities, kind_ref, knudsen_ref, state_ref, own_ref):
    nx, ny = kind_ref.shape
    columns = cell_columns(kind_ref, knudsen_ref)
    for x in range(nx):
        widen(state_ref[x], columns, x, nx, velocities, own_ref, x * ny)


def edges_kernel(own_ref, low_x_ref, high_x_ref, low_ref, high_ref):
    ny = low_x_ref.shape[0] // REACH
    at = 0
    for source in (low_x_ref, own_ref, high_x_ref):
        for start in range(0, source.shape[0], ny):
            low_ref[at : at + REACH, :] = source[start + ny - REACH : start + ny, :]
            high_ref[at : at + REACH, :] = source[start : start + REACH, :]
            at += REACH


def pieces(value, count):
    out = []
    for _ in range(count - 1):
        high = value.astype(BF16).astype(F32)
        out.append(high)
        value = value - high
    return out + [value]


def moment_rows(rows_ref, cells, basis_ref, sums_ref, block_ref, totals_ref, aux_ref):
    step = 160
    for start in range(0, cells, step):
        rows = rows_ref[start : start + step, :]
        high = rows.astype(BF16)
        low = (rows - high.astype(F32)).astype(BF16)
        basis = basis_ref[...]
        sums_ref[start : start + step, :] = jnp.dot(
            high, basis, preferred_element_type=F32
        ) + jnp.dot(low, basis, preferred_element_type=F32)
    sums_ref[cells:, :] = jnp.zeros((CHUNKS * LANE - cells, LANE), F32)
    for chunk in range(CHUNKS):
        turned = sums_ref[chunk * LANE : (chunk + 1) * LANE, :].T
        block_ref[pl.ds(chunk, 24, stride=CHUNKS), :] = turned[:24, :]
    totals_ref[: 10 * CHUNKS, :] = block_ref[: 10 * CHUNKS, :]
    totals_ref[10 * CHUNKS :, :] = (
        block_ref[10 * CHUNKS : 13 * CHUNKS, :] + block_ref[13 * CHUNKS : 16 * CHUNKS, :]
    )
    aux_ref[...] = block_ref[16 * CHUNKS : 18 * CHUNKS, :]


def coefficients(gathered_ref, aux_ref, block_ref):
    total = gathered_ref[0]
    for device in range(1, gathered_ref.shape[0]):
        total = total + gathered_ref[device]
    n, nx, ny, nz, xx, yy, zz, xy, xz, yz, cx, cy, cz = (
        total[i * CHUNKS : (i + 1) * CHUNKS, :] for i in range(MOMENTS)
    )
    knudsen = aux_ref[:CHUNKS, :]
    kind = aux_ref[CHUNKS:, :]
    inverse = 1.0 / n
    ux, uy, uz = nx * inverse, ny * inverse, nz * inverse
    uu = ux * ux + uy * uy + uz * uz
    trace = xx + yy + zz
    spread = (trace * inverse - uu) / 3.0
    temperature = SPACING * SPACING * spread
    density = WEIGHT * n
    qx = cx - ux * trace - 2.0 * (ux * xx + uy * xy + uz * xz) + 2.0 * ux * uu * n
    qy = cy - uy * trace - 2.0 * (ux * xy + uy * yy + uz * yz) + 2.0 * uy * uu * n
    qz = cz - uz * trace - 2.0 * (ux * xz + uy * yz + uz * zz) + 2.0 * uz * uu * n
    root = jnp.sqrt(temperature)
    keep = jnp.exp(-CLOCK_ADVANCE * density * root / knudsen)
    scale = (1.0 - keep) * density / ((2.0 * math.pi) ** 1.5 * temperature * root)
    heat = (
        scale
        * ((1.0 - VISCOUS_RATIO) * -2.0 * math.log(2.0) / 10.0)
        / (n * spread * spread)
    )

    wall, inflow = kind == 1.0, kind == 2.0
    solid = wall | inflow
    ux = jnp.where(inflow, INFLOW_SPEED / SPACING - 0.5, jnp.where(wall, -0.5, ux))
    uy = jnp.where(solid, -0.5, uy)
    uz = jnp.where(solid, -0.5, uz)
    spread = jnp.where(
        inflow,
        INFLOW_TEMP / SPACING**2,
        jnp.where(wall, WALL_TEMP / SPACING**2, spread),
    )
    scale = jnp.where(
        inflow,
        INFLOW_DENSITY / (2.0 * math.pi * INFLOW_TEMP) ** 1.5,
        jnp.where(wall, density / (2.0 * math.pi * WALL_TEMP) ** 1.5, scale),
    )
    keep = jnp.where(solid, 0.0, keep)
    qx = jnp.where(solid, 0.0, heat * qx)
    qy = jnp.where(solid, 0.0, heat * qy)
    qz = jnp.where(solid, 0.0, heat * qz)
    rate = (0.5 * LOG2E) / spread

    rows = []
    rows += pieces(-rate * (ux * ux + uy * uy + uz * uz), 3)
    for u in (ux, uy, uz):
        rows += pieces(rate * (2.0 * u + 1.0), 3)
    rows += pieces(-2.0 * rate, 3)
    for q in (-(qx * ux + qy * uy + qz * uz), qx, qy, qz):
        rows += pieces(q, 2)
    rows += pieces(keep, 3)
    rows += pieces(scale, 3)
    rows += [jnp.zeros_like(n)] * (COEFFICIENTS - len(rows))
    for i, value in enumerate(rows):
        block_ref[i * CHUNKS : (i + 1) * CHUNKS, :] = value


def relaxed_rows(rows_ref, cells, lanes, velocities, basis_ref, block_ref, out_ref):
    tail = 2 * lanes
    for chunk in range(-(-cells // LANE)):
        start, size = chunk * LANE, min(LANE, cells - chunk * LANE)
        here = slice(start, start + size)
        left = block_ref[pl.ds(chunk, COEFFICIENTS, stride=CHUNKS), :].T
        left = left[:size, :].astype(BF16)
        pair = jnp.dot(left, basis_ref[:, tail : tail + 2 * LANE], preferred_element_type=F32)
        keep, scale = pair[:, :LANE], pair[:, LANE:]
        for lane in range(0, lanes, LANE):
            pair = jnp.dot(
                left, basis_ref[:, 2 * lane : 2 * lane + 2 * LANE], preferred_element_type=F32
            )
            power, linear = pair[:, :LANE], pair[:, LANE:]
            state = rows_ref[here, lane : lane + LANE]
            value = state * keep + jnp.exp2(power) * (
                scale + linear * (power + 2.5 * LOG2E)
            )
            if lane + LANE > velocities:
                held = lax.broadcasted_iota(jnp.int32, value.shape, 1) < velocities - lane
                value = jnp.where(held, value, state)
            out_ref[here, lane : lane + LANE] = value


def limited(left, right):
    least, most = jnp.minimum(left, right), jnp.maximum(left, right)
    return jnp.maximum(least, 0.0) + jnp.minimum(most, 0.0)


def transported_rows(rows_ref, count, row, lanes, courant_ref, write):
    for lane in range(0, lanes, LANE):
        along = slice(lane, lane + LANE)
        speed_x, speed_y = courant_ref[0:1, along], courant_ref[1:2, along]
        half_x, half_y = courant_ref[2:3, along], courant_ref[3:4, along]
        positive_x = jnp.broadcast_to(half_x, (row, LANE)) > 0.0
        positive_y = jnp.broadcast_to(half_y, (row, LANE)) > 0.0

        def load(x):
            return rows_ref[x * row : (x + 1) * row, along]

        before, centre = load(0), load(1)
        slope_before = centre - before
        edge_before = face_before = centre_before = None
        for x in range(1, count - 1):
            after = load(x + 1)
            slope_after = after - centre
            edge = centre + half_x * limited(slope_before, slope_after)
            face = None if edge_before is None else edge - edge_before
            if face_before is not None:
                middle = centre_before
                rise = pltpu.roll(middle, row - 1, 0) - middle
                edge_y = middle + half_y * limited(pltpu.roll(rise, 1, 0), rise)
                face_y = pltpu.roll(edge_y, row - 1, 0) - edge_y
                change_x = jnp.where(positive_x, face_before, face)
                change_y = jnp.where(positive_y, pltpu.roll(face_y, 1, 0), face_y)
                write(x - 3, lane, middle - speed_x * change_x - speed_y * change_y)
            centre_before, centre = centre, after
            slope_before = slope_after
            edge_before, face_before = edge, face


def first_kernel(
    own_ref, low_x_ref, high_x_ref, low_y_ref, high_y_ref, basis_ref,
    rows_ref, totals_ref, aux_ref, sums_ref, block_ref,
):
    ny = low_x_ref.shape[0] // REACH
    nx = own_ref.shape[0] // ny
    row = ny + 2 * REACH
    for x in range(nx + 2 * REACH):
        if x < REACH:
            source, at = low_x_ref, x
        elif x < nx + REACH:
            source, at = own_ref, x - REACH
        else:
            source, at = high_x_ref, x - nx - REACH
        rows_ref[x * row : x * row + ny, :] = source[at * ny : (at + 1) * ny, :]
        rows_ref[x * row + ny : x * row + ny + REACH, :] = high_y_ref[x * REACH : (x + 1) * REACH, :]
        rows_ref[x * row + ny + REACH : (x + 1) * row, :] = low_y_ref[x * REACH : (x + 1) * REACH, :]
    cells = (nx + 2 * REACH) * row
    moment_rows(rows_ref, cells, basis_ref, sums_ref, block_ref, totals_ref, aux_ref)


def middle_kernel(
    velocities, row, gathered_ref, aux_in_ref, rows_in_ref, relax_ref, courant_ref, basis_ref,
    rows_ref, totals_ref, aux_ref, relaxed_ref, sums_ref, block_ref,
):
    cells, lanes = rows_in_ref.shape
    coefficients(gathered_ref, aux_in_ref, block_ref)
    relaxed_rows(rows_in_ref, cells, lanes, velocities, relax_ref, block_ref, relaxed_ref)

    def write(x, lane, value):
        rows_ref[x * row : (x + 1) * row, lane : lane + LANE] = value

    transported_rows(relaxed_ref, cells // row, row, lanes, courant_ref, write)
    moment_rows(rows_ref, cells - 4 * row, basis_ref, sums_ref, block_ref, totals_ref, aux_ref)


def last_kernel(
    velocities, row, gathered_ref, aux_in_ref, rows_in_ref, relax_ref, courant_ref,
    out_ref, relaxed_ref, block_ref,
):
    cells, lanes = rows_in_ref.shape
    ny = out_ref.shape[1]
    coefficients(gathered_ref, aux_in_ref, block_ref)
    relaxed_rows(rows_in_ref, cells, lanes, velocities, relax_ref, block_ref, relaxed_ref)

    def write(x, lane, value):
        width = min(LANE, velocities - lane)
        out_ref[x, :, lane : lane + width] = value[:ny, :width]

    transported_rows(relaxed_ref, cells // row, row, lanes, courant_ref, write)


BLOCK = pltpu.VMEM((COEFFICIENTS * CHUNKS, LANE), F32)
SUMS = pltpu.VMEM((CHUNKS * LANE, LANE), F32)
TOTALS = jax.ShapeDtypeStruct((MOMENTS * CHUNKS, LANE), F32)
AUX = jax.ShapeDtypeStruct((2 * CHUNKS, LANE), F32)


def rows_of(*shape):
    return jax.ShapeDtypeStruct(shape, F32)


def call(kernel, name, out_shape, scratch=(), **options):
    return pl.pallas_call(
        kernel,
        out_shape=out_shape,
        scratch_shapes=scratch,
        compiler_params=pltpu.CompilerParams(vmem_limit_bytes=40 * 1024 * 1024),
        name=name,
        **options,
    )


def gather(totals):
    devices = lax.axis_size("vel")
    copies = jnp.broadcast_to(totals[None], (devices, *totals.shape))
    return lax.all_to_all(copies, "vel", 0, 0)


def ring(axis):
    devices = lax.axis_size(axis)
    up = [(i, (i + 1) % devices) for i in range(devices)]
    return up, [(j, i) for i, j in up]


def body(distribution, cell_kind, local_knudsen):
    nx, ny, velocities = distribution.shape
    lanes = -(-(velocities + 2) // LANE) * LANE
    row = ny + 2 * REACH
    side = rows_of(REACH * ny, lanes)
    whole = pl.BlockSpec((nx, ny), lambda i: (0, 0))
    to_upper, to_lower = call(
        functools.partial(sides_kernel, velocities),
        "x_sides",
        (side, side),
        grid=(1,),
        in_specs=[
            whole,
            whole,
            pl.BlockSpec((REACH, ny, velocities), lambda i: (0, 0, 0)),
            pl.BlockSpec((REACH, ny, velocities), lambda i: (nx // REACH - 1, 0, 0)),
        ],
    )(cell_kind, local_knudsen, distribution, distribution)
    up, down = ring("sx")
    low_x = lax.ppermute(to_upper, "sx", up)
    high_x = lax.ppermute(to_lower, "sx", down)

    own = call(
        functools.partial(own_kernel, velocities), "own_rows", rows_of(nx * ny, lanes)
    )(cell_kind, local_knudsen, distribution)
    first = jnp.full((1,), lax.axis_index("vel") * velocities, jnp.int32)
    moment_basis, relax_basis, courant = call(
        functools.partial(tables_kernel, velocities),
        "tables",
        (
            jax.ShapeDtypeStruct((lanes, LANE), BF16),
            jax.ShapeDtypeStruct((COEFFICIENTS, 2 * lanes + 2 * LANE), BF16),
            rows_of(8, lanes),
        ),
        [pltpu.VMEM((LANE, lanes), F32)],
        in_specs=[pl.BlockSpec(memory_space=pltpu.SMEM)],
    )(first)

    edge = rows_of((nx + 2 * REACH) * REACH, lanes)
    to_upper, to_lower = call(edges_kernel, "y_sides", (edge, edge))(own, low_x, high_x)
    up, down = ring("sy")
    low_y = lax.ppermute(to_upper, "sy", up)
    high_y = lax.ppermute(to_lower, "sy", down)

    cells = (nx + 2 * REACH) * row
    rows, totals, aux = call(
        first_kernel,
        "first_moments",
        (rows_of(cells, lanes), TOTALS, AUX),
        [SUMS, BLOCK],
    )(own, low_x, high_x, low_y, high_y, moment_basis)
    for _ in range(STEPS - 1):
        cells -= 4 * row
        rows, totals, aux = call(
            functools.partial(middle_kernel, velocities, row),
            "step_and_moments",
            (rows_of(cells, lanes), TOTALS, AUX),
            [pltpu.VMEM((cells + 4 * row, lanes), F32), SUMS, BLOCK],
        )(gather(totals), aux, rows, relax_basis, courant, moment_basis)
    return call(
        functools.partial(last_kernel, velocities, row),
        "last_step",
        rows_of(nx, ny, velocities),
        [pltpu.VMEM((cells, lanes), F32), BLOCK],
    )(gather(totals), aux, rows, relax_basis, courant)


def solution(mesh):
    return jax.shard_map(
        body,
        mesh=mesh,
        in_specs=(P("sx", "sy", "vel"), P("sx", "sy"), P("sx", "sy")),
        out_specs=P("sx", "sy", "vel"),
        check_vma=False,
    )
```

time: 307 us -> 99.5 us (0.32)
  the two profiles are of different devices: /device:TPU:8 before, /device:TPU:152 now
where the time goes in v1:
time: 99.5 us; the launch traced here: 99.1 us
  blocking collectives  38.5 us (39%)
  waiting for transfers between devices  28.2 us (28%)
  starting transfers between devices  15.8 us (16%)
  Pallas kernels  13.5 us (14%)
  local copies, waits for them, and re-layouts  3.02 us (3%)
    all_to_all x2, blocking collectives, gather(): return lax.all_to_all(copies, 'vel', 0, 0)  38.5 us
    ppermute x1, waiting for transfers between devices, body(): low_y = lax.ppermute(to_upper, 'sy', up)  11.5 us
    ppermute x1, waiting for transfers between devices, body(): low_x = lax.ppermute(to_upper, 'sx', up)  7.47 us
    ppermute x1, starting transfers between devices, body(): low_y = lax.ppermute(to_upper, 'sy', up)  7.29 us
    pallas_call x1, Pallas kernels, body(): call(functools.partial(middle_kernel, velocities, row), 'step_and_moments...  5.56 us
    ppermute x1, waiting for transfers between devices, body(): high_x = lax.ppermute(to_lower, 'sx', down)  5.33 us
    pallas_call x1, Pallas kernels, body(): call(functools.partial(last_kernel, velocities, row), 'last_step', rows_o...  4.91 us
    ppermute x1, starting transfers between devices, body(): low_x = lax.ppermute(to_upper, 'sx', up)  4.7 us
  transfers between devices with their start and end apart: 4, of which 4 were waited for; matrix products, arithmetic and copies ran while one was open for 0% of the time, Pallas kernels for 1%

profile of v1, /device:TPU:152, one launch (start us, length us, event | category | flops | bytes accessed | tf_op | source)
XLA Modules:
  0.0 99.1 jit_solution(11571506516178783897)
XLA Ops:
  0.0 0.0 copy-start
  0.0 1.5 %copy-done = f32[16,32,864]{2,1,0:T(8,128)S(1)} copy-done((f32[16,32,864]{2,1,0:T(8,128)S(1)}, f32[16,32,864]{2,1,0:T(8,128)}, u32[]{:S(2)}) %copy-start) | copy-done | bytes 1769496
  1.5 0.0 copy-start.1
  1.5 0.7 copy-done.1
  2.2 0.0 copy-start.2
  2.2 0.7 copy-done.2
  2.9 0.2 x_sides.1
  3.1 4.7 %collective-permute-start = (f32[128,896]{1,0:T(8,128)S(1)}, f32[128,896]{1,0:T(8,128)S(1)}, u32[]{:S(2)}, u32[]{:S(2)}) collective-permute-start(f32[128,896]{1,0:T(8,128)S(1)} %get-tuple-element.18), channel_id=1, source_target_pairs={{0,64},{64,128},{128,192},{192,256},{256,320},{320,384},{384,448},... | collective-permute-start | bytes 1376264 | tf_op jit(solution)/shard_map/ppermute | solution.py:399
  7.8 1.9 %collective-permute-start.1 = (f32[128,896]{1,0:T(8,128)S(1)}, f32[128,896]{1,0:T(8,128)S(1)}, u32[]{:S(2)}, u32[]{:S(2)}) collective-permute-start(f32[128,896]{1,0:T(8,128)S(1)} %get-tuple-element.19), channel_id=1, source_target_pairs={{64,0},{128,64},{192,128},{256,192},{320,256},{384,320},{448,384},... | collective-permute-start | bytes 1376264 | tf_op jit(solution)/shard_map/ppermute | solution.py:400
  9.8 0.3 own_rows.1.own_ref
  10.1 7.5 %collective-permute-done.low_x_ref = f32[128,896]{1,0:T(8,128)S(1)} collective-permute-done((f32[128,896]{1,0:T(8,128)S(1)}, f32[128,896]{1,0:T(8,128)S(1)}, u32[]{:S(2)}, u32[]{:S(2)}) %collective-permute-start) | collective-permute-done | bytes 458784 | tf_op jit(solution)/shard_map/ppermute | solution.py:399
  17.6 5.3 %collective-permute-done.1.high_x_ref = f32[128,896]{1,0:T(8,128)S(1)} collective-permute-done((f32[128,896]{1,0:T(8,128)S(1)}, f32[128,896]{1,0:T(8,128)S(1)}, u32[]{:S(2)}, u32[]{:S(2)}) %collective-permute-start.1) | collective-permute-done | bytes 458784 | tf_op jit(solution)/shard_map/ppermute | solution.py:400
  22.9 1.0 y_sides.1
  23.9 7.3 %collective-permute-start.2 = (f32[96,896]{1,0:T(8,128)}, f32[96,896]{1,0:T(8,128)S(1)}, u32[]{:S(2)}, u32[]{:S(2)}) collective-permute-start(f32[96,896]{1,0:T(8,128)} %get-tuple-element.20), channel_id=1, source_target_pairs={{0,16},{16,32},{32,48},{48,0},{1,17},{17,33},{33,49},{49,1},{2,18}... | collective-permute-start | bytes 1032200 | tf_op jit(solution)/shard_map/ppermute | solution.py:421
  31.2 1.9 %collective-permute-start.3 = (f32[96,896]{1,0:T(8,128)}, f32[96,896]{1,0:T(8,128)S(1)}, u32[]{:S(2)}, u32[]{:S(2)}) collective-permute-start(f32[96,896]{1,0:T(8,128)} %get-tuple-element.21), channel_id=1, source_target_pairs={{16,0},{32,16},{48,32},{0,48},{17,1},{33,17},{49,33},{1,49},{18,2}... | collective-permute-start | bytes 1032200 | tf_op jit(solution)/shard_map/ppermute | solution.py:422
  33.1 0.3 tables.1
  33.4 11.5 %collective-permute-done.2.low_y_ref = f32[96,896]{1,0:T(8,128)S(1)} collective-permute-done((f32[96,896]{1,0:T(8,128)}, f32[96,896]{1,0:T(8,128)S(1)}, u32[]{:S(2)}, u32[]{:S(2)}) %collective-permute-start.2) | collective-permute-done | bytes 344096 | tf_op jit(solution)/shard_map/ppermute | solution.py:421
  44.9 3.9 %collective-permute-done.3.high_y_ref = f32[96,896]{1,0:T(8,128)S(1)} collective-permute-done((f32[96,896]{1,0:T(8,128)}, f32[96,896]{1,0:T(8,128)S(1)}, u32[]{:S(2)}, u32[]{:S(2)}) %collective-permute-start.3) | collective-permute-done | bytes 344096 | tf_op jit(solution)/shard_map/ppermute | solution.py:422
  48.9 1.1 %first_moments.1 = (f32[960,896]{1,0:T(8,128)S(1)}, f32[104,128]{1,0:T(8,128)S(1)}, f32[16,128]{1,0:T(8,128)S(1)}) custom-call(f32[512,896]{1,0:T(8,128)S(1)} %own_rows.1.own_ref, f32[128,896]{1,0:T(8,128)S(1)} %collective-permute-done.low_x_ref, f32[128,896]{1,0:T(8,128)S(1)} %collective-permute-done.1.high_x_ref, ...), custom_call_target="tpu_custom_call" | custom-call | tf_op jit(solution)/shard_map/first_moments/pallas_call | solution.py:425
  50.0 0.1 broadcast_in_dim.7
  50.1 21.5 %all_to_all.10.gathered_ref = f32[16,104,128]{2,1,0:T(8,128)S(1)} all-to-all(f32[16,104,128]{2,1,0:T(8,128)S(1)} %broadcast_in_dim.7), channel_id=1, replica_groups=mesh['sx'=8,'sy'=4,'vel'=16] {'vel'}, dimensions={0} | all-to-all | bytes 1703936 | tf_op jit(solution)/shard_map/all_to_all | solution.py:371
  71.6 5.6 %step_and_moments.1 = (f32[800,896]{1,0:T(8,128)S(1)}, f32[104,128]{1,0:T(8,128)S(1)}, f32[16,128]{1,0:T(8,128)S(1)}) custom-call(f32[16,104,128]{2,1,0:T(8,128)S(1)} %all_to_all.10.gathered_ref, f32[16,128]{1,0:T(8,128)S(1)} %get-tuple-element.24.aux_in_ref, f32[960,896]{1,0:T(8,128)S(1)} %get-tuple-element.25.rows_in_ref, ...), custom_call_target="tpu_custom_call" | custom-call | tf_op jit(solution)/shard_map/step_and_moments/pallas_call | solution.py:433
  77.1 0.1 broadcast_in_dim.8
  77.2 17.0 %all_to_all.11.gathered_ref = f32[16,104,128]{2,1,0:T(8,128)S(1)} all-to-all(f32[16,104,128]{2,1,0:T(8,128)S(1)} %broadcast_in_dim.8), channel_id=1, replica_groups=mesh['sx'=8,'sy'=4,'vel'=16] {'vel'}, dimensions={0} | all-to-all | bytes 1703936 | tf_op jit(solution)/shard_map/all_to_all | solution.py:371
  94.2 4.9 %last_step.1 = f32[16,32,864]{2,1,0:T(8,128)} custom-call(f32[16,104,128]{2,1,0:T(8,128)S(1)} %all_to_all.11.gathered_ref, f32[16,128]{1,0:T(8,128)S(1)} %get-tuple-element.29.aux_in_ref, f32[800,896]{1,0:T(8,128)S(1)} %get-tuple-element.30.rows_in_ref, bf16[32,2048]{1,0:T(8,128)(2,1)S(1)} %get-tuple-element.26.relax_ref, ...), custom_call_target="tpu_custom_call" | custom-call | tf_op jit(solution)/shard_map/last_step/pallas_call | solution.py:439
Async XLA Ops:
  0.0 1.5 %copy-start = (f32[16,32,864]{2,1,0:T(8,128)S(1)}, f32[16,32,864]{2,1,0:T(8,128)}, u32[]{:S(2)}) copy-start(f32[16,32,864]{2,1,0:T(8,128)} %last_ref.1) | copy-start | bytes 5308420
  1.5 0.7 copy-start.1
  2.2 0.7 copy-start.2
  3.1 14.5 %collective-permute-start = (f32[128,896]{1,0:T(8,128)S(1)}, f32[128,896]{1,0:T(8,128)S(1)}, u32[]{:S(2)}, u32[]{:S(2)}) collective-permute-start(f32[128,896]{1,0:T(8,128)S(1)} %get-tuple-element.18), channel_id=1, source_target_pairs={{0,64},{64,128},{128,192},{192,256},{256,320},{320,384},{384,448},... | collective-permute-start | bytes 1376264 | tf_op jit(solution)/shard_map/ppermute | solution.py:399
  7.8 15.1 %collective-permute-start.1 = (f32[128,896]{1,0:T(8,128)S(1)}, f32[128,896]{1,0:T(8,128)S(1)}, u32[]{:S(2)}, u32[]{:S(2)}) collective-permute-start(f32[128,896]{1,0:T(8,128)S(1)} %get-tuple-element.19), channel_id=1, source_target_pairs={{64,0},{128,64},{192,128},{256,192},{320,256},{384,320},{448,384},... | collective-permute-start | bytes 1376264 | tf_op jit(solution)/shard_map/ppermute | solution.py:400
  23.9 21.0 %collective-permute-start.2 = (f32[96,896]{1,0:T(8,128)}, f32[96,896]{1,0:T(8,128)S(1)}, u32[]{:S(2)}, u32[]{:S(2)}) collective-permute-start(f32[96,896]{1,0:T(8,128)} %get-tuple-element.20), channel_id=1, source_target_pairs={{0,16},{16,32},{32,48},{48,0},{1,17},{17,33},{33,49},{49,1},{2,18}... | collective-permute-start | bytes 1032200 | tf_op jit(solution)/shard_map/ppermute | solution.py:421
  31.2 17.7 %collective-permute-start.3 = (f32[96,896]{1,0:T(8,128)}, f32[96,896]{1,0:T(8,128)S(1)}, u32[]{:S(2)}, u32[]{:S(2)}) collective-permute-start(f32[96,896]{1,0:T(8,128)} %get-tuple-element.21), channel_id=1, source_target_pairs={{16,0},{32,16},{48,32},{0,48},{17,1},{33,17},{49,33},{1,49},{18,2}... | collective-permute-start | bytes 1032200 | tf_op jit(solution)/shard_map/ppermute | solution.py:422

commit v2 on v1

v2 whole, which is shorter than its diff:
```python
import functools
import math

import jax
import jax.numpy as jnp
from jax import lax
from jax.experimental import pallas as pl
from jax.experimental.pallas import tpu as pltpu
from jax.sharding import PartitionSpec as P

NVX = 24
STEPS = 2

VEL_LIMIT = 4.8
CLOCK_ADVANCE = 0.09
VISCOUS_RATIO = 2.0 / 3.0
WALL_TEMP = 1.0
INFLOW_DENSITY = 12.0
INFLOW_SPEED = 0.5
INFLOW_TEMP = 1.0

SPACING = 2.0 * VEL_LIMIT / NVX
WEIGHT = SPACING**3
LOG2E = 1.0 / math.log(2.0)

LANE = 128
SUBLANE = 8
REACH = 2
MOMENTS = 13
COEFFICIENTS = 32
F32 = jnp.float32
BF16 = jnp.bfloat16


def lattice(first, velocities, lanes):
    lane = lax.broadcasted_iota(jnp.int32, (1, lanes), 1)
    held = lane < velocities
    index = jnp.where(held, first + lane, 0).astype(F32)

    def split(value, by):
        over = jnp.floor((value + 0.5) * (1.0 / by))
        return over, value - by * over

    def line(points):
        half, odd = split(points, 2.0)
        return jnp.where(odd > 0.5, half, -half - 1.0)

    index, a = split(index, float(NVX))
    c, b = split(index, float(NVX))
    return line(a), line(b), line(c), held


def tables_kernel(velocities, first_ref, moment_ref, relax_ref, courant_ref, turn_ref):
    lanes = courant_ref.shape[1]
    a, b, c, held = lattice(first_ref[0], velocities, lanes)
    zero, one = jnp.zeros((1, lanes), F32), jnp.ones((1, lanes), F32)
    square = a * a + b * b + c * c
    cubic = [a * square, b * square, c * square]
    high = [v.astype(BF16).astype(F32) for v in cubic]
    low = [v - h for v, h in zip(cubic, high)]
    rows = [one, a, b, c, a * a, b * b, c * c, a * b, a * c, b * c, *high, *low]
    rows = [jnp.where(held, v, 0.0) for v in rows]
    turn_ref[...] = jnp.zeros_like(turn_ref)
    for i, value in enumerate(rows):
        turn_ref[i : i + 1, :] = value
    for start in range(0, lanes, LANE):
        turned = turn_ref[:, start : start + LANE].T
        moment_ref[start : start + LANE, :] = turned.astype(BF16)

    half = 0.5 * (square + a + b + c)
    turn_ref[...] = jnp.zeros_like(turn_ref)
    for i, value in enumerate((one, a, b, c, half)):
        for j in range(3):
            turn_ref[3 * i + j : 3 * i + j + 1, :] = jnp.where(held, value, 0.0)
    for i, value in enumerate((one, a, b, c)):
        for j in range(2):
            at = COEFFICIENTS + 15 + 2 * i + j
            turn_ref[at : at + 1, :] = jnp.where(held, value, 0.0)
    for start in range(0, lanes, LANE):
        for i in range(2):
            part = turn_ref[i * COEFFICIENTS : (i + 1) * COEFFICIENTS, start : start + LANE]
            at = 2 * start + i * LANE
            relax_ref[:, at : at + LANE] = part.astype(BF16)
    row = lax.broadcasted_iota(jnp.int32, (COEFFICIENTS, LANE), 0)
    for i in range(2):
        at = 2 * lanes + i * LANE
        picked = jnp.where((row >= 23 + 3 * i) & (row < 26 + 3 * i), 1.0, 0.0)
        relax_ref[:, at : at + LANE] = picked.astype(BF16)

    speeds = [jnp.where(held, CLOCK_ADVANCE * SPACING * (v + 0.5), 0.0) for v in (a, b)]
    signs = [jnp.where(v >= 0.0, 0.5, -0.5) for v in (a, b)]
    for i, value in enumerate([*speeds, *signs, zero, zero, zero, zero]):
        courant_ref[i : i + 1, :] = value


def pieces(value, count):
    out = []
    for _ in range(count - 1):
        high = value.astype(BF16).astype(F32)
        out.append(high)
        value = value - high
    return out + [value]


def add_moments(rows, basis, sums_ref, at):
    high = rows.astype(BF16)
    low = (rows - high.astype(F32)).astype(BF16)
    sums_ref[at : at + rows.shape[0], :] = jnp.dot(
        high, basis, preferred_element_type=F32
    ) + jnp.dot(low, basis, preferred_element_type=F32)


def blocks_of(sums_ref, block_ref, totals_ref):
    chunks = sums_ref.shape[0] // LANE
    for chunk in range(chunks):
        turned = sums_ref[chunk * LANE : (chunk + 1) * LANE, :].T
        block_ref[pl.ds(chunk, 16, stride=chunks), :] = turned[:16, :]
    totals_ref[: 10 * chunks, :] = block_ref[: 10 * chunks, :]
    totals_ref[10 * chunks :, :] = (
        block_ref[10 * chunks : 13 * chunks, :] + block_ref[13 * chunks : 16 * chunks, :]
    )


def coefficients(gathered_ref, aux_ref, block_ref):
    chunks = aux_ref.shape[0] // 2
    total = gathered_ref[0]
    for device in range(1, gathered_ref.shape[0]):
        total = total + gathered_ref[device]
    block_ref[: MOMENTS * chunks, :] = total
    n, nx, ny, nz, xx, yy, zz, xy, xz, yz, cx, cy, cz = (
        block_ref[i * chunks : (i + 1) * chunks, :] for i in range(MOMENTS)
    )
    knudsen = aux_ref[:chunks, :]
    kind = aux_ref[chunks:, :]
    inverse = 1.0 / n
    ux, uy, uz = nx * inverse, ny * inverse, nz * inverse
    uu = ux * ux + uy * uy + uz * uz
    trace = xx + yy + zz
    spread = (trace * inverse - uu) / 3.0
    temperature = SPACING * SPACING * spread
    density = WEIGHT * n
    qx = cx - ux * trace - 2.0 * (ux * xx + uy * xy + uz * xz) + 2.0 * ux * uu * n
    qy = cy - uy * trace - 2.0 * (ux * xy + uy * yy + uz * yz) + 2.0 * uy * uu * n
    qz = cz - uz * trace - 2.0 * (ux * xz + uy * yz + uz * zz) + 2.0 * uz * uu * n
    root = jnp.sqrt(temperature)
    keep = jnp.exp(-CLOCK_ADVANCE * density * root / knudsen)
    scale = (1.0 - keep) * density / ((2.0 * math.pi) ** 1.5 * temperature * root)
    heat = (
        scale
        * ((1.0 - VISCOUS_RATIO) * -2.0 * math.log(2.0) / 10.0)
        / (n * spread * spread)
    )

    wall, inflow = kind == 1.0, kind == 2.0
    solid = wall | inflow
    ux = jnp.where(inflow, INFLOW_SPEED / SPACING - 0.5, jnp.where(wall, -0.5, ux))
    uy = jnp.where(solid, -0.5, uy)
    uz = jnp.where(solid, -0.5, uz)
    spread = jnp.where(
        inflow,
        INFLOW_TEMP / SPACING**2,
        jnp.where(wall, WALL_TEMP / SPACING**2, spread),
    )
    scale = jnp.where(
        inflow,
        INFLOW_DENSITY / (2.0 * math.pi * INFLOW_TEMP) ** 1.5,
        jnp.where(wall, density / (2.0 * math.pi * WALL_TEMP) ** 1.5, scale),
    )
    keep = jnp.where(solid, 0.0, keep)
    qx = jnp.where(solid, 0.0, heat * qx)
    qy = jnp.where(solid, 0.0, heat * qy)
    qz = jnp.where(solid, 0.0, heat * qz)
    rate = (0.5 * LOG2E) / spread

    rows = []
    rows += pieces(-rate * (ux * ux + uy * uy + uz * uz), 3)
    for u in (ux, uy, uz):
        rows += pieces(rate * (2.0 * u + 1.0), 3)
    rows += pieces(-2.0 * rate, 3)
    for q in (-(qx * ux + qy * uy + qz * uz), qx, qy, qz):
        rows += pieces(q, 2)
    rows += pieces(keep, 3)
    rows += pieces(scale, 3)
    rows += [jnp.zeros_like(n)] * (COEFFICIENTS - len(rows))
    for i, value in enumerate(rows):
        block_ref[i * chunks : (i + 1) * chunks, :] = value


def relaxed_rows(load, chunks, lanes, basis_ref, block_ref, out_ref):
    tail = 2 * lanes
    for chunk in range(chunks):
        start = chunk * LANE
        left = block_ref[pl.ds(chunk, COEFFICIENTS, stride=chunks), :].T.astype(BF16)
        pair = jnp.dot(left, basis_ref[:, tail : tail + 2 * LANE], preferred_element_type=F32)
        keep, scale = pair[:, :LANE], pair[:, LANE:]
        for lane in range(0, lanes, LANE):
            pair = jnp.dot(
                left, basis_ref[:, 2 * lane : 2 * lane + 2 * LANE], preferred_element_type=F32
            )
            power, linear = pair[:, :LANE], pair[:, LANE:]
            out_ref[start : start + LANE, lane : lane + LANE] = load(start, lane) * keep + (
                jnp.exp2(power) * (scale + linear * (power + 2.5 * LOG2E))
            )


def limited(left, right):
    least, most = jnp.minimum(left, right), jnp.maximum(left, right)
    return jnp.maximum(least, 0.0) + jnp.minimum(most, 0.0)


def transported_rows(load, side, xs, ny, lanes, courant_ref, write):
    row = ny + SUBLANE
    for lane in range(0, lanes, LANE):
        along = slice(lane, lane + LANE)
        speed_x, speed_y = courant_ref[0:1, along], courant_ref[1:2, along]
        half_x, half_y = courant_ref[2:3, along], courant_ref[3:4, along]
        positive_x = jnp.broadcast_to(half_x, (ny, LANE)) > 0.0
        positive_y = jnp.broadcast_to(half_y, (ny, LANE)) > 0.0

        before, centre = load(xs[0] - 2, lane), load(xs[0] - 1, lane)
        slope_before = centre - before
        edge_before = face_before = centre_before = None
        for x in range(xs[0] - 1, xs[-1] + 2):
            after = load(x + 1, lane)
            slope_after = after - centre
            edge = centre + half_x * limited(slope_before, slope_after)
            face = None if edge_before is None else edge - edge_before
            if face_before is not None:
                middle = jnp.concatenate([centre_before, side(x - 1, lane)], axis=0)
                rise = pltpu.roll(middle, row - 1, 0) - middle
                edge_y = middle + half_y * limited(pltpu.roll(rise, 1, 0), rise)
                face_y = pltpu.roll(edge_y, row - 1, 0) - edge_y
                change_x = jnp.where(positive_x, face_before, face)
                change_y = jnp.where(positive_y, pltpu.roll(face_y, 1, 0)[:ny], face_y[:ny])
                write(x - 1, lane, centre_before - speed_x * change_x - speed_y * change_y)
            centre_before, centre = centre, after
            slope_before = slope_after
            edge_before, face_before = edge, face


def side_rows(low_ref, high_ref):
    def side(x, lane):
        at, along = slice(x * REACH, (x + 1) * REACH), slice(lane, lane + LANE)
        gap = jnp.zeros((SUBLANE - 2 * REACH, LANE), F32)
        return jnp.concatenate([high_ref[at, along], gap, low_ref[at, along]], axis=0)

    return side


def first_kernel(state_ref, knudsen_ref, kind_ref, basis_ref, totals_ref, aux_ref, sums_ref, block_ref):
    nx, ny, velocities = state_ref.shape
    step = LANE // ny
    for i, value in enumerate((knudsen_ref[...], kind_ref[...].astype(F32))):
        for x in range(0, nx, step):
            row = [value[x + j : x + j + 1, :] for j in range(step)]
            at = (i * nx + x) // step
            aux_ref[at : at + 1, :] = jnp.concatenate(row, axis=1)
    basis = basis_ref[:velocities, :]
    for x in range(0, nx, step):
        rows = state_ref[x : x + step].reshape(step * ny, velocities)
        add_moments(rows, basis, sums_ref, x * ny)
    blocks_of(sums_ref, block_ref, totals_ref)


def relax_kernel(ny, gathered_ref, aux_ref, *refs):
    *state_refs, basis_ref, out_ref, low_x_ref, high_x_ref, low_y_ref, high_y_ref, block_ref = refs
    cells, lanes = out_ref.shape
    nx = cells // ny
    coefficients(gathered_ref, aux_ref, block_ref)

    def load(start, lane):
        if len(state_refs) == 1:
            (state_ref,) = state_refs
            velocities = state_ref.shape[2]
            width = min(LANE, velocities - lane)
            rows = state_ref[start // ny : (start + LANE) // ny, :, lane : lane + width]
            rows = rows.reshape(LANE, width)
            if width == LANE:
                return rows
            return jnp.concatenate([rows, jnp.zeros((LANE, LANE - width), F32)], axis=1)
        inner_ref, outer_ref = state_refs
        along, edge = slice(lane, lane + LANE), REACH * ny
        if start == 0:
            parts = [outer_ref[:edge, along], inner_ref[: LANE - edge, along]]
        elif start + LANE == cells:
            parts = [inner_ref[start - edge :, along], outer_ref[edge:, along]]
        else:
            return inner_ref[start - edge : start - edge + LANE, along]
        return jnp.concatenate(parts, axis=0)

    relaxed_rows(load, cells // LANE, lanes, basis_ref, block_ref, out_ref)
    low_x_ref[...] = out_ref[: REACH * ny, :]
    high_x_ref[...] = out_ref[cells - REACH * ny :, :]
    for x in range(nx):
        at = slice(x * REACH, (x + 1) * REACH)
        low_y_ref[at, :] = out_ref[x * ny : x * ny + REACH, :]
        high_y_ref[at, :] = out_ref[(x + 1) * ny - REACH : (x + 1) * ny, :]


def inner_kernel(ny, velocities, state_ref, low_y_ref, high_y_ref, courant_ref, *refs):
    cells, lanes = state_ref.shape
    nx = cells // ny

    def load(x, lane):
        return state_ref[x * ny : (x + 1) * ny, lane : lane + LANE]

    if velocities is None:
        basis_ref, out_ref, sums_ref = refs

        def write(x, lane, value):
            at = (x - REACH) * ny
            out_ref[at : at + ny, lane : lane + LANE] = value

    else:
        (out_ref,) = refs

        def write(x, lane, value):
            width = min(LANE, velocities - lane)
            out_ref[x - REACH, :, lane : lane + width] = value[:, :width]

    side = side_rows(low_y_ref, high_y_ref)
    transported_rows(load, side, range(REACH, nx - REACH), ny, lanes, courant_ref, write)
    if velocities is None:
        for at in range(0, out_ref.shape[0], LANE):
            add_moments(out_ref[at : at + LANE, :], basis_ref[...], sums_ref, at)


def outer_kernel(ny, final, state_ref, low_x_ref, high_x_ref, low_y_ref, high_y_ref, courant_ref, *refs):
    cells, lanes = state_ref.shape
    nx = cells // ny

    def load(x, lane):
        if x < 0:
            ref, x = low_x_ref, x + REACH
        elif x >= nx:
            ref, x = high_x_ref, x - nx
        else:
            ref = state_ref
        return ref[x * ny : (x + 1) * ny, lane : lane + LANE]

    if final:
        inner_ref, out_ref = refs
        out_ref[REACH : nx - REACH] = inner_ref[...]

        def write(x, lane, value):
            width = min(LANE, out_ref.shape[2] - lane)
            out_ref[x, :, lane : lane + width] = value[:, :width]

    else:
        basis_ref, inner_sums_ref, out_ref, totals_ref, sums_ref, block_ref = refs

        def write(x, lane, value):
            at = (x if x < REACH else x - nx + 2 * REACH) * ny
            out_ref[at : at + ny, lane : lane + LANE] = value

    side = side_rows(low_y_ref, high_y_ref)
    for xs in (range(REACH), range(nx - REACH, nx)):
        transported_rows(load, side, xs, ny, lanes, courant_ref, write)
    if not final:
        edge = REACH * ny
        sums_ref[edge : cells - edge, :] = inner_sums_ref[...]
        for at, to in ((0, 0), (edge, cells - edge)):
            add_moments(out_ref[at : at + edge, :], basis_ref[...], sums_ref, to)
        blocks_of(sums_ref, block_ref, totals_ref)


def rows_of(*shape):
    return jax.ShapeDtypeStruct(shape, F32)


def call(kernel, name, out_shape, scratch=(), **options):
    return pl.pallas_call(
        kernel,
        out_shape=out_shape,
        scratch_shapes=scratch,
        compiler_params=pltpu.CompilerParams(vmem_limit_bytes=40 * 1024 * 1024),
        name=name,
        **options,
    )


def gather(totals):
    devices = lax.axis_size("vel")
    copies = jnp.broadcast_to(totals[None], (devices, *totals.shape))
    return lax.all_to_all(copies, "vel", 0, 0)


def ring(axis):
    devices = lax.axis_size(axis)
    up = [(i, (i + 1) % devices) for i in range(devices)]
    return up, [(j, i) for i, j in up]


def body(distribution, cell_kind, local_knudsen):
    nx, ny, velocities = distribution.shape
    lanes = -(-velocities // LANE) * LANE
    cells = nx * ny
    chunks = cells // LANE
    first = jnp.full((1,), lax.axis_index("vel") * velocities, jnp.int32)
    moment_basis, relax_basis, courant = call(
        functools.partial(tables_kernel, velocities),
        "tables",
        (
            jax.ShapeDtypeStruct((lanes, LANE), BF16),
            jax.ShapeDtypeStruct((COEFFICIENTS, 2 * lanes + 2 * LANE), BF16),
            rows_of(SUBLANE, lanes),
        ),
        [pltpu.VMEM((LANE, lanes), F32)],
        in_specs=[pl.BlockSpec(memory_space=pltpu.SMEM)],
    )(first)
    sums = pltpu.VMEM((cells, LANE), F32)
    block = pltpu.VMEM((COEFFICIENTS * chunks, LANE), F32)
    totals_shape = rows_of(MOMENTS * chunks, LANE)
    side_x, side_y = rows_of(REACH * ny, lanes), rows_of(REACH * nx, lanes)

    totals, aux = call(
        first_kernel, "first_moments", (totals_shape, rows_of(2 * chunks, LANE)), [sums, block]
    )(distribution, local_knudsen, cell_kind, moment_basis)
    state = (distribution,)
    for step in range(STEPS):
        final = step == STEPS - 1
        relaxed, low_x, high_x, low_y, high_y = call(
            functools.partial(relax_kernel, ny),
            "relax",
            (rows_of(cells, lanes), side_x, side_x, side_y, side_y),
            [block],
        )(gather(totals), aux, *state, relax_basis)
        up, down = ring("sy")
        from_low_y = lax.ppermute(high_y, "sy", up)
        from_high_y = lax.ppermute(low_y, "sy", down)
        up, down = ring("sx")
        from_low_x = lax.ppermute(high_x, "sx", up)
        from_high_x = lax.ppermute(low_x, "sx", down)
        sides_y = (from_low_y, from_high_y, courant)
        sides = (relaxed, from_low_x, from_high_x, *sides_y)
        inner_cells = cells - 2 * REACH * ny
        if final:
            inner = call(
                functools.partial(inner_kernel, ny, velocities),
                "last_inner",
                rows_of(nx - 2 * REACH, ny, velocities),
            )(relaxed, *sides_y)
            return call(
                functools.partial(outer_kernel, ny, True),
                "last_outer",
                rows_of(nx, ny, velocities),
            )(*sides, inner)
        inner, inner_sums = call(
            functools.partial(inner_kernel, ny, None),
            "inner",
            (rows_of(inner_cells, lanes), rows_of(inner_cells, LANE)),
        )(relaxed, *sides_y, moment_basis)
        outer, totals = call(
            functools.partial(outer_kernel, ny, False),
            "outer",
            (rows_of(2 * REACH * ny, lanes), totals_shape),
            [sums, block],
        )(*sides, moment_basis, inner_sums)
        state = (inner, outer)


def solution(mesh):
    return jax.shard_map(
        body,
        mesh=mesh,
        in_specs=(P("sx", "sy", "vel"), P("sx", "sy"), P("sx", "sy")),
        out_specs=P("sx", "sy", "vel"),
        check_vma=False,
    )
```

time: 99.5 us -> 88.9 us (0.89)
  the two profiles are of different devices: /device:TPU:152 before, /device:TPU:32 now
where the time goes in v2:
time: 88.9 us; the launch traced here: 88.4 us
  starting transfers between devices  34.3 us (39%)
  blocking collectives  29.3 us (33%)
  waiting for transfers between devices  11.7 us (13%)
  Pallas kernels  9.97 us (11%)
  local copies, waits for them, and re-layouts  2.97 us (3%)
    all_to_all x2, blocking collectives, gather(): return lax.all_to_all(copies, 'vel', 0, 0)  29.3 us
    ppermute x2, starting transfers between devices, body(): from_low_y = lax.ppermute(high_y, 'sy', up)  12.4 us
    ppermute x2, starting transfers between devices, body(): from_high_x = lax.ppermute(low_x, 'sx', down)  9.6 us
    ppermute x2, waiting for transfers between devices, body(): from_high_y = lax.ppermute(low_y, 'sy', down)  9 us
    ppermute x2, starting transfers between devices, body(): from_high_y = lax.ppermute(low_y, 'sy', down)  7.8 us
    ppermute x2, starting transfers between devices, body(): from_low_x = lax.ppermute(high_x, 'sx', up)  4.51 us
    unnamed x8, local copies, waits for them, and re-layouts  2.89 us
    ppermute x2, waiting for transfers between devices, body(): from_low_y = lax.ppermute(high_y, 'sy', up)  2.73 us
  transfers between devices with their start and end apart: 8, of which 4 were waited for; matrix products, arithmetic and copies ran while one was open for 0% of the time, Pallas kernels for 5%

profile of v2, /device:TPU:32, one launch (start us, length us, event | category | flops | bytes accessed | tf_op | source)
XLA Modules:
  0.0 88.4 jit_solution(5431736387039255892)
XLA Ops:
  0.0 0.3 tables.1
  0.3 0.0 copy-start
  0.3 1.5 %copy-done = f32[16,32,864]{2,1,0:T(8,128)S(1)} copy-done((f32[16,32,864]{2,1,0:T(8,128)S(1)}, f32[16,32,864]{2,1,0:T(8,128)}, u32[]{:S(2)}) %copy-start) | copy-done | bytes 1769496
  1.8 0.0 copy-start.2
  1.8 0.7 copy-done.2
  2.5 0.0 copy-start.3
  2.5 0.7 copy-done.3
  3.2 0.0 copy-start.1
  3.2 0.7 first_moments.1
  3.9 16.2 %all_to_all.10.gathered_ref = f32[16,52,128]{2,1,0:T(8,128)S(1)} all-to-all(f32[16,52,128]{2,1,0:T(8,128)S(1)} %broadcast_in_dim.7), channel_id=1, replica_groups=mesh['sx'=8,'sy'=4,'vel'=16] {'vel'}, dimensions={0} | all-to-all | bytes 851968 | tf_op jit(solution)/shard_map/all_to_all | solution.py:385
  20.1 0.0 copy-done.1
  20.1 1.0 %relax.2 = (f32[512,896]{1,0:T(8,128)S(1)}, f32[64,896]{1,0:T(8,128)S(1)}, f32[64,896]{1,0:T(8,128)S(1)}, f32[32,896]{1,0:T(8,128)S(1)}, f32[32,896]{1,0:T(8,128)S(1)}) custom-call(f32[16,52,128]{2,1,0:T(8,128)S(1)} %all_to_all.10.gathered_ref, f32[8,128]{1,0:T(8,128)S(1)} %get-tuple-element.26.aux_ref, f32[16,32,864]{2,1,0:T(8,128)S(1)} %copy-done.1, ...), custom_call_target="tpu_custom_call" | custom-call | tf_op jit(solution)/shard_map/relax/pallas_call | solution.py:422
  21.1 2.6 %collective-permute-start = (f32[64,896]{1,0:T(8,128)S(1)}, f32[64,896]{1,0:T(8,128)S(1)}, u32[]{:S(2)}, u32[]{:S(2)}) collective-permute-start(f32[64,896]{1,0:T(8,128)S(1)} %get-tuple-element.29), channel_id=1, source_target_pairs={{0,64},{64,128},{128,192},{192,256},{256,320},{320,384},{384,448},... | collective-permute-start | bytes 688136 | tf_op jit(solution)/shard_map/ppermute | solution.py:432
  23.7 4.5 %collective-permute-start.1 = (f32[64,896]{1,0:T(8,128)S(1)}, f32[64,896]{1,0:T(8,128)S(1)}, u32[]{:S(2)}, u32[]{:S(2)}) collective-permute-start(f32[64,896]{1,0:T(8,128)S(1)} %get-tuple-element.30), channel_id=1, source_target_pairs={{64,0},{128,64},{192,128},{256,192},{320,256},{384,320},{448,384},... | collective-permute-start | bytes 688136 | tf_op jit(solution)/shard_map/ppermute | solution.py:433
  28.2 6.1 %collective-permute-start.2 = (f32[32,896]{1,0:T(8,128)S(1)}, f32[32,896]{1,0:T(8,128)S(1)}, u32[]{:S(2)}, u32[]{:S(2)}) collective-permute-start(f32[32,896]{1,0:T(8,128)S(1)} %get-tuple-element.31), channel_id=1, source_target_pairs={{0,16},{16,32},{32,48},{48,0},{1,17},{17,33},{33,49},{49,1},{2,18}... | collective-permute-start | bytes 344072 | tf_op jit(solution)/shard_map/ppermute | solution.py:429
  34.3 5.9 %collective-permute-start.3 = (f32[32,896]{1,0:T(8,128)S(1)}, f32[32,896]{1,0:T(8,128)S(1)}, u32[]{:S(2)}, u32[]{:S(2)}) collective-permute-start(f32[32,896]{1,0:T(8,128)S(1)} %get-tuple-element.32), channel_id=1, source_target_pairs={{16,0},{32,16},{48,32},{0,48},{17,1},{33,17},{49,33},{1,49},{18,2}... | collective-permute-start | bytes 344072 | tf_op jit(solution)/shard_map/ppermute | solution.py:430
  40.1 0.9 %collective-permute-done.2.low_y_ref = f32[32,896]{1,0:T(8,128)S(1)} collective-permute-done((f32[32,896]{1,0:T(8,128)S(1)}, f32[32,896]{1,0:T(8,128)S(1)}, u32[]{:S(2)}, u32[]{:S(2)}) %collective-permute-start.2) | collective-permute-done | bytes 114720 | tf_op jit(solution)/shard_map/ppermute | solution.py:429
  41.1 3.6 %collective-permute-done.3.high_y_ref = f32[32,896]{1,0:T(8,128)S(1)} collective-permute-done((f32[32,896]{1,0:T(8,128)S(1)}, f32[32,896]{1,0:T(8,128)S(1)}, u32[]{:S(2)}, u32[]{:S(2)}) %collective-permute-start.3) | collective-permute-done | bytes 114720 | tf_op jit(solution)/shard_map/ppermute | solution.py:430
  44.7 2.3 %inner.1 = (f32[384,896]{1,0:T(8,128)S(1)}, f32[384,128]{1,0:T(8,128)S(1)}) custom-call(f32[512,896]{1,0:T(8,128)S(1)} %get-tuple-element.28.state_ref, f32[32,896]{1,0:T(8,128)S(1)} %collective-permute-done.2.low_y_ref, f32[32,896]{1,0:T(8,128)S(1)} %collective-permute-done.3.high_y_ref, f32[8,896]{1,0:T(8,128)S(1)} %get-tuple-element.33.courant_ref, ...), custom_call_target="tpu_custom_call" | custom-call | tf_op jit(solution)/shard_map/inner/pallas_call | solution.py:448
  46.9 0.0 collective-permute-done.low_x_ref
  46.9 0.0 collective-permute-done.1.high_x_ref
  47.0 1.0 %outer.1 = (f32[128,896]{1,0:T(8,128)S(1)}, f32[52,128]{1,0:T(8,128)S(1)}) custom-call(f32[512,896]{1,0:T(8,128)S(1)} %get-tuple-element.28.state_ref, f32[64,896]{1,0:T(8,128)S(1)} %collective-permute-done.low_x_ref, f32[64,896]{1,0:T(8,128)S(1)} %collective-permute-done.1.high_x_ref, f32[32,896]{1,0:T(8,128)S(1)} %collective-permute-done.2.low_y_ref, ...), custom_call_target="tpu_custom_call" | custom-call | tf_op jit(solution)/shard_map/outer/pallas_call | solution.py:453
  48.0 13.1 %all_to_all.11.gathered_ref = f32[16,52,128]{2,1,0:T(8,128)S(1)} all-to-all(f32[16,52,128]{2,1,0:T(8,128)S(1)} %broadcast_in_dim.8), channel_id=1, replica_groups=mesh['sx'=8,'sy'=4,'vel'=16] {'vel'}, dimensions={0} | all-to-all | bytes 851968 | tf_op jit(solution)/shard_map/all_to_all | solution.py:385
  61.2 1.0 %relax.3 = (f32[512,896]{1,0:T(8,128)S(1)}, f32[64,896]{1,0:T(8,128)S(1)}, f32[64,896]{1,0:T(8,128)S(1)}, f32[32,896]{1,0:T(8,128)S(1)}, f32[32,896]{1,0:T(8,128)S(1)}) custom-call(f32[16,52,128]{2,1,0:T(8,128)S(1)} %all_to_all.11.gathered_ref, f32[8,128]{1,0:T(8,128)S(1)} %get-tuple-element.26.aux_ref, f32[384,896]{1,0:T(8,128)S(1)} %get-tuple-element.36.refs_0_, ...), custom_call_target="tpu_custom_call" | custom-call | tf_op jit(solution)/shard_map/relax/pallas_call | solution.py:422
  62.2 1.9 %collective-permute-start.4 = (f32[64,896]{1,0:T(8,128)S(1)}, f32[64,896]{1,0:T(8,128)S(1)}, u32[]{:S(2)}, u32[]{:S(2)}) collective-permute-start(f32[64,896]{1,0:T(8,128)S(1)} %get-tuple-element.39), channel_id=1, source_target_pairs={{0,64},{64,128},{128,192},{192,256},{256,320},{320,384},{384,448},... | collective-permute-start | bytes 688136 | tf_op jit(solution)/shard_map/ppermute | solution.py:432
  64.1 5.1 %collective-permute-start.5 = (f32[64,896]{1,0:T(8,128)S(1)}, f32[64,896]{1,0:T(8,128)S(1)}, u32[]{:S(2)}, u32[]{:S(2)}) collective-permute-start(f32[64,896]{1,0:T(8,128)S(1)} %get-tuple-element.40), channel_id=1, source_target_pairs={{64,0},{128,64},{192,128},{256,192},{320,256},{384,320},{448,384},... | collective-permute-start | bytes 688136 | tf_op jit(solution)/shard_map/ppermute | solution.py:433
  69.2 6.3 %collective-permute-start.6 = (f32[32,896]{1,0:T(8,128)S(1)}, f32[32,896]{1,0:T(8,128)S(1)}, u32[]{:S(2)}, u32[]{:S(2)}) collective-permute-start(f32[32,896]{1,0:T(8,128)S(1)} %get-tuple-element.41), channel_id=1, source_target_pairs={{0,16},{16,32},{32,48},{48,0},{1,17},{17,33},{33,49},{49,1},{2,18}... | collective-permute-start | bytes 344072 | tf_op jit(solution)/shard_map/ppermute | solution.py:429
  75.5 1.9 %collective-permute-start.7 = (f32[32,896]{1,0:T(8,128)S(1)}, f32[32,896]{1,0:T(8,128)S(1)}, u32[]{:S(2)}, u32[]{:S(2)}) collective-permute-start(f32[32,896]{1,0:T(8,128)S(1)} %get-tuple-element.42), channel_id=1, source_target_pairs={{16,0},{32,16},{48,32},{0,48},{17,1},{33,17},{49,33},{1,49},{18,2}... | collective-permute-start | bytes 344072 | tf_op jit(solution)/shard_map/ppermute | solution.py:430
  77.4 1.8 %collective-permute-done.6.low_y_ref = f32[32,896]{1,0:T(8,128)S(1)} collective-permute-done((f32[32,896]{1,0:T(8,128)S(1)}, f32[32,896]{1,0:T(8,128)S(1)}, u32[]{:S(2)}, u32[]{:S(2)}) %collective-permute-start.6) | collective-permute-done | bytes 114720 | tf_op jit(solution)/shard_map/ppermute | solution.py:429
  79.2 5.4 %collective-permute-done.7.high_y_ref = f32[32,896]{1,0:T(8,128)S(1)} collective-permute-done((f32[32,896]{1,0:T(8,128)S(1)}, f32[32,896]{1,0:T(8,128)S(1)}, u32[]{:S(2)}, u32[]{:S(2)}) %collective-permute-start.7) | collective-permute-done | bytes 114720 | tf_op jit(solution)/shard_map/ppermute | solution.py:430
  84.7 1.7 %last_inner.1.refs_0_ = f32[12,32,864]{2,1,0:T(8,128)S(1)} custom-call(f32[512,896]{1,0:T(8,128)S(1)} %get-tuple-element.38.state_ref, f32[32,896]{1,0:T(8,128)S(1)} %collective-permute-done.6.low_y_ref, f32[32,896]{1,0:T(8,128)S(1)} %collective-permute-done.7.high_y_ref, f32[8,896]{1,0:T(8,128)S(1)} %get-tuple-element.33.courant_ref), custom_call_target="tpu_custom_call" | custom-call | tf_op jit(solution)/shard_map/last_inner/pallas_call | solution.py:438
  86.4 0.0 collective-permute-done.4.low_x_ref
  86.4 0.0 collective-permute-done.5.high_x_ref
  86.4 2.0 %last_outer.1 = f32[16,32,864]{2,1,0:T(8,128)} custom-call(f32[512,896]{1,0:T(8,128)S(1)} %get-tuple-element.38.state_ref, f32[64,896]{1,0:T(8,128)S(1)} %collective-permute-done.4.low_x_ref, f32[64,896]{1,0:T(8,128)S(1)} %collective-permute-done.5.high_x_ref, f32[32,896]{1,0:T(8,128)S(1)} %collective-permute-done.6.low_y_ref, ...), custom_call_target="tpu_custom_call" | custom-call | tf_op jit(solution)/shard_map/last_outer/pallas_call | solution.py:443
  (2 shorter events, 0.1 us)
Async XLA Ops:
  0.3 1.5 %copy-start = (f32[16,32,864]{2,1,0:T(8,128)S(1)}, f32[16,32,864]{2,1,0:T(8,128)}, u32[]{:S(2)}) copy-start(f32[16,32,864]{2,1,0:T(8,128)} %refs_0_.1) | copy-start | bytes 5308420
  1.8 0.7 copy-start.2
  2.5 0.7 copy-start.3
  3.2 16.9 %copy-start.1 = (f32[16,32,864]{2,1,0:T(8,128)S(1)}, f32[16,32,864]{2,1,0:T(8,128)}, u32[]{:S(2)}) copy-start(f32[16,32,864]{2,1,0:T(8,128)} %refs_0_.1) | copy-start | bytes 5308420
  21.1 25.8 %collective-permute-start = (f32[64,896]{1,0:T(8,128)S(1)}, f32[64,896]{1,0:T(8,128)S(1)}, u32[]{:S(2)}, u32[]{:S(2)}) collective-permute-start(f32[64,896]{1,0:T(8,128)S(1)} %get-tuple-element.29), channel_id=1, source_target_pairs={{0,64},{64,128},{128,192},{192,256},{256,320},{320,384},{384,448},... | collective-permute-start | bytes 688136 | tf_op jit(solution)/shard_map/ppermute | solution.py:432
  23.7 23.3 %collective-permute-start.1 = (f32[64,896]{1,0:T(8,128)S(1)}, f32[64,896]{1,0:T(8,128)S(1)}, u32[]{:S(2)}, u32[]{:S(2)}) collective-permute-start(f32[64,896]{1,0:T(8,128)S(1)} %get-tuple-element.30), channel_id=1, source_target_pairs={{64,0},{128,64},{192,128},{256,192},{320,256},{384,320},{448,384},... | collective-permute-start | bytes 688136 | tf_op jit(solution)/shard_map/ppermute | solution.py:433
  28.2 12.9 %collective-permute-start.2 = (f32[32,896]{1,0:T(8,128)S(1)}, f32[32,896]{1,0:T(8,128)S(1)}, u32[]{:S(2)}, u32[]{:S(2)}) collective-permute-start(f32[32,896]{1,0:T(8,128)S(1)} %get-tuple-element.31), channel_id=1, source_target_pairs={{0,16},{16,32},{32,48},{48,0},{1,17},{17,33},{33,49},{49,1},{2,18}... | collective-permute-start | bytes 344072 | tf_op jit(solution)/shard_map/ppermute | solution.py:429
  34.3 10.4 %collective-permute-start.3 = (f32[32,896]{1,0:T(8,128)S(1)}, f32[32,896]{1,0:T(8,128)S(1)}, u32[]{:S(2)}, u32[]{:S(2)}) collective-permute-start(f32[32,896]{1,0:T(8,128)S(1)} %get-tuple-element.32), channel_id=1, source_target_pairs={{16,0},{32,16},{48,32},{0,48},{17,1},{33,17},{49,33},{1,49},{18,2}... | collective-permute-start | bytes 344072 | tf_op jit(solution)/shard_map/ppermute | solution.py:430
  62.2 24.2 %collective-permute-start.4 = (f32[64,896]{1,0:T(8,128)S(1)}, f32[64,896]{1,0:T(8,128)S(1)}, u32[]{:S(2)}, u32[]{:S(2)}) collective-permute-start(f32[64,896]{1,0:T(8,128)S(1)} %get-tuple-element.39), channel_id=1, source_target_pairs={{0,64},{64,128},{128,192},{192,256},{256,320},{320,384},{384,448},... | collective-permute-start | bytes 688136 | tf_op jit(solution)/shard_map/ppermute | solution.py:432
  64.1 22.3 %collective-permute-start.5 = (f32[64,896]{1,0:T(8,128)S(1)}, f32[64,896]{1,0:T(8,128)S(1)}, u32[]{:S(2)}, u32[]{:S(2)}) collective-permute-start(f32[64,896]{1,0:T(8,128)S(1)} %get-tuple-element.40), channel_id=1, source_target_pairs={{64,0},{128,64},{192,128},{256,192},{320,256},{384,320},{448,384},... | collective-permute-start | bytes 688136 | tf_op jit(solution)/shard_map/ppermute | solution.py:433
  69.2 10.0 %collective-permute-start.6 = (f32[32,896]{1,0:T(8,128)S(1)}, f32[32,896]{1,0:T(8,128)S(1)}, u32[]{:S(2)}, u32[]{:S(2)}) collective-permute-start(f32[32,896]{1,0:T(8,128)S(1)} %get-tuple-element.41), channel_id=1, source_target_pairs={{0,16},{16,32},{32,48},{48,0},{1,17},{17,33},{33,49},{49,1},{2,18}... | collective-permute-start | bytes 344072 | tf_op jit(solution)/shard_map/ppermute | solution.py:429
  75.5 9.1 %collective-permute-start.7 = (f32[32,896]{1,0:T(8,128)S(1)}, f32[32,896]{1,0:T(8,128)S(1)}, u32[]{:S(2)}, u32[]{:S(2)}) collective-permute-start(f32[32,896]{1,0:T(8,128)S(1)} %get-tuple-element.42), channel_id=1, source_target_pairs={{16,0},{32,16},{48,32},{0,48},{17,1},{33,17},{49,33},{1,49},{18,2}... | collective-permute-start | bytes 344072 | tf_op jit(solution)/shard_map/ppermute | solution.py:430

commit v3 on v2

--- a/solution.py
+++ b/solution.py
@@ -121,17 +121,22 @@
     )
 
 
-def coefficients(gathered_ref, aux_ref, block_ref):
-    chunks = aux_ref.shape[0] // 2
+def coefficients(gathered_ref, knudsen_ref, kind_ref, block_ref):
+    nx, ny = kind_ref.shape
+    step = LANE // ny
+    chunks = nx // step
+    for i, value in enumerate((knudsen_ref[...], kind_ref[...].astype(F32))):
+        for x in range(0, nx, step):
+            row = [value[x + j : x + j + 1, :] for j in range(step)]
+            at = (MOMENTS + i) * chunks + x // step
+            block_ref[at : at + 1, :] = jnp.concatenate(row, axis=1)
     total = gathered_ref[0]
     for device in range(1, gathered_ref.shape[0]):
         total = total + gathered_ref[device]
     block_ref[: MOMENTS * chunks, :] = total
-    n, nx, ny, nz, xx, yy, zz, xy, xz, yz, cx, cy, cz = (
-        block_ref[i * chunks : (i + 1) * chunks, :] for i in range(MOMENTS)
-    )
-    knudsen = aux_ref[:chunks, :]
-    kind = aux_ref[chunks:, :]
+    n, nx, ny, nz, xx, yy, zz, xy, xz, yz, cx, cy, cz, knudsen, kind = (
+        block_ref[i * chunks : (i + 1) * chunks, :] for i in range(MOMENTS + 2)
+    )
     inverse = 1.0 / n
     ux, uy, uz = nx * inverse, ny * inverse, nz * inverse
     uu = ux * ux + uy * uy + uz * uz
@@ -247,14 +252,9 @@
     return side
 
 
-def first_kernel(state_ref, knudsen_ref, kind_ref, basis_ref, totals_ref, aux_ref, sums_ref, block_ref):
+def first_kernel(state_ref, basis_ref, totals_ref, sums_ref, block_ref):
     nx, ny, velocities = state_ref.shape
     step = LANE // ny
-    for i, value in enumerate((knudsen_ref[...], kind_ref[...].astype(F32))):
-        for x in range(0, nx, step):
-            row = [value[x + j : x + j + 1, :] for j in range(step)]
-            at = (i * nx + x) // step
-            aux_ref[at : at + 1, :] = jnp.concatenate(row, axis=1)
     basis = basis_ref[:velocities, :]
     for x in range(0, nx, step):
         rows = state_ref[x : x + step].reshape(step * ny, velocities)
@@ -262,11 +262,11 @@
     blocks_of(sums_ref, block_ref, totals_ref)
 
 
-def relax_kernel(ny, gathered_ref, aux_ref, *refs):
+def relax_kernel(ny, gathered_ref, knudsen_ref, kind_ref, *refs):
     *state_refs, basis_ref, out_ref, low_x_ref, high_x_ref, low_y_ref, high_y_ref, block_ref = refs
     cells, lanes = out_ref.shape
     nx = cells // ny
-    coefficients(gathered_ref, aux_ref, block_ref)
+    coefficients(gathered_ref, knudsen_ref, kind_ref, block_ref)
 
     def load(start, lane):
         if len(state_refs) == 1:
@@ -316,7 +316,7 @@
 
         def write(x, lane, value):
             width = min(LANE, velocities - lane)
-            out_ref[x - REACH, :, lane : lane + width] = value[:, :width]
+            out_ref[x, :, lane : lane + width] = value[:, :width]
 
     side = side_rows(low_y_ref, high_y_ref)
     transported_rows(load, side, range(REACH, nx - REACH), ny, lanes, courant_ref, write)
@@ -339,12 +339,12 @@
         return ref[x * ny : (x + 1) * ny, lane : lane + LANE]
 
     if final:
-        inner_ref, out_ref = refs
-        out_ref[REACH : nx - REACH] = inner_ref[...]
+        _, out_ref, edge_ref, sent = refs
 
         def write(x, lane, value):
             width = min(LANE, out_ref.shape[2] - lane)
-            out_ref[x, :, lane : lane + width] = value[:, :width]
+            at = x if x < REACH else x - nx + 2 * REACH
+            edge_ref[at, :, lane : lane + width] = value[:, :width]
 
     else:
         basis_ref, inner_sums_ref, out_ref, totals_ref, sums_ref, block_ref = refs
@@ -354,14 +354,26 @@
             out_ref[at : at + ny, lane : lane + LANE] = value
 
     side = side_rows(low_y_ref, high_y_ref)
-    for xs in (range(REACH), range(nx - REACH, nx)):
+    copies = []
+    for i, xs in enumerate((range(REACH), range(nx - REACH, nx))):
         transported_rows(load, side, xs, ny, lanes, courant_ref, write)
+        if final:
+            part = edge_ref.at[i * REACH : (i + 1) * REACH]
+            copies.append(
+                pltpu.make_async_copy(part, out_ref.at[xs[0] : xs[0] + REACH], sent.at[i])
+            )
+            copies[-1].start()
+    for copy in copies:
+        copy.wait()
     if not final:
         edge = REACH * ny
         sums_ref[edge : cells - edge, :] = inner_sums_ref[...]
         for at, to in ((0, 0), (edge, cells - edge)):
             add_moments(out_ref[at : at + edge, :], basis_ref[...], sums_ref, to)
         blocks_of(sums_ref, block_ref, totals_ref)
+
+
+INNER_COST = pl.CostEstimate(flops=30_000_000_000, bytes_accessed=4_000_000, transcendentals=0)
 
 
 def rows_of(*shape):
@@ -396,7 +408,11 @@
     lanes = -(-velocities // LANE) * LANE
     cells = nx * ny
     chunks = cells // LANE
-    first = jnp.full((1,), lax.axis_index("vel") * velocities, jnp.int32)
+    sums = pltpu.VMEM((cells, LANE), F32)
+    block = pltpu.VMEM((COEFFICIENTS * chunks, LANE), F32)
+    totals_shape = rows_of(MOMENTS * chunks, LANE)
+    side_x, side_y = rows_of(REACH * ny, lanes), rows_of(REACH * nx, lanes)
+
     moment_basis, relax_basis, courant = call(
         functools.partial(tables_kernel, velocities),
         "tables",
@@ -407,15 +423,10 @@
         ),
         [pltpu.VMEM((LANE, lanes), F32)],
         in_specs=[pl.BlockSpec(memory_space=pltpu.SMEM)],
-    )(first)
-    sums = pltpu.VMEM((cells, LANE), F32)
-    block = pltpu.VMEM((COEFFICIENTS * chunks, LANE), F32)
-    totals_shape = rows_of(MOMENTS * chunks, LANE)
-    side_x, side_y = rows_of(REACH * ny, lanes), rows_of(REACH * nx, lanes)
-
-    totals, aux = call(
-        first_kernel, "first_moments", (totals_shape, rows_of(2 * chunks, LANE)), [sums, block]
-    )(distribution, local_knudsen, cell_kind, moment_basis)
+    )(jnp.full((1,), lax.axis_index("vel") * velocities, jnp.int32))
+    totals = call(first_kernel, "first_moments", totals_shape, [sums, block])(
+        distribution, moment_basis
+    )
     state = (distribution,)
     for step in range(STEPS):
         final = step == STEPS - 1
@@ -424,7 +435,7 @@
             "relax",
             (rows_of(cells, lanes), side_x, side_x, side_y, side_y),
             [block],
-        )(gather(totals), aux, *state, relax_basis)
+        )(gather(totals), local_knudsen, cell_kind, *state, relax_basis)
         up, down = ring("sy")
         from_low_y = lax.ppermute(high_y, "sy", up)
         from_high_y = lax.ppermute(low_y, "sy", down)
@@ -438,17 +449,24 @@
             inner = call(
                 functools.partial(inner_kernel, ny, velocities),
                 "last_inner",
-                rows_of(nx - 2 * REACH, ny, velocities),
+                rows_of(nx, ny, velocities),
+                cost_estimate=INNER_COST,
             )(relaxed, *sides_y)
             return call(
                 functools.partial(outer_kernel, ny, True),
                 "last_outer",
                 rows_of(nx, ny, velocities),
+                [pltpu.VMEM((2 * REACH, ny, velocities), F32), pltpu.SemaphoreType.DMA((2,))],
+                in_specs=[pl.BlockSpec(memory_space=pltpu.VMEM)] * len(sides)
+                + [pl.BlockSpec(memory_space=pltpu.HBM)],
+                out_specs=pl.BlockSpec(memory_space=pltpu.HBM),
+                input_output_aliases={len(sides): 0},
             )(*sides, inner)
         inner, inner_sums = call(
             functools.partial(inner_kernel, ny, None),
             "inner",
             (rows_of(inner_cells, lanes), rows_of(inner_cells, LANE)),
+            cost_estimate=INNER_COST,
         )(relaxed, *sides_y, moment_basis)
         outer, totals = call(
             functools.partial(outer_kernel, ny, False),

time: 88.9 us -> 82.4 us (0.927)
  the two profiles are of different devices: /device:TPU:32 before, /device:TPU:16 now
where the time goes in v3:
time: 82.4 us; the launch traced here: 82 us
  starting transfers between devices  32.5 us (39%)
  blocking collectives  29.5 us (36%)
  Pallas kernels  10.6 us (13%)
  waiting for transfers between devices  7.64 us (9%)
  local copies, waits for them, and re-layouts  1.59 us (2%)
    all_to_all x2, blocking collectives, gather(): return lax.all_to_all(copies, 'vel', 0, 0)  29.5 us
    ppermute x2, starting transfers between devices, body(): from_high_y = lax.ppermute(low_y, 'sy', down)  11.4 us
    ppermute x2, starting transfers between devices, body(): from_low_y = lax.ppermute(high_y, 'sy', up)  8.54 us
    ppermute x2, starting transfers between devices, body(): from_low_x = lax.ppermute(high_x, 'sx', up)  8.35 us
    ppermute x2, waiting for transfers between devices, body(): from_high_x = lax.ppermute(low_x, 'sx', down)  7.28 us
    ppermute x2, starting transfers between devices, body(): from_high_x = lax.ppermute(low_x, 'sx', down)  4.28 us
    pallas_call x1, Pallas kernels, body(): call(functools.partial(inner_kernel, ny, velocities), 'last_inner', rows_...  2.95 us
    pallas_call x1, Pallas kernels, body(): call(functools.partial(inner_kernel, ny, None), 'inner', (rows_of(inner_c...  2.23 us
  transfers between devices with their start and end apart: 8, of which 3 were waited for; matrix products, arithmetic and copies ran while one was open for 0% of the time, Pallas kernels for 6%

profile of v3, /device:TPU:16, one launch (start us, length us, event | category | flops | bytes accessed | tf_op | source)
XLA Modules:
  0.0 82.0 jit_solution(8886879426189126018)
XLA Ops:
  0.0 0.0 copy-start.2
  0.0 0.3 tables.1
  0.3 0.0 copy-start
  0.3 1.5 %copy-done = f32[16,32,864]{2,1,0:T(8,128)S(1)} copy-done((f32[16,32,864]{2,1,0:T(8,128)S(1)}, f32[16,32,864]{2,1,0:T(8,128)}, u32[]{:S(2)}) %copy-start) | copy-done | bytes 1769496
  1.8 0.0 copy-start.1
  1.8 0.0 copy-start.3
  1.8 0.7 first_moments.1
  2.5 16.2 %all_to_all.10.gathered_ref = f32[16,52,128]{2,1,0:T(8,128)S(1)} all-to-all(f32[16,52,128]{2,1,0:T(8,128)S(1)} %broadcast_in_dim.7), channel_id=1, replica_groups=mesh['sx'=8,'sy'=4,'vel'=16] {'vel'}, dimensions={0} | all-to-all | bytes 851968 | tf_op jit(solution)/shard_map/all_to_all | solution.py:397
  18.7 0.0 copy-done.2
  18.7 0.0 copy-done.1
  18.7 0.0 copy-done.3
  18.7 1.0 %relax.2 = (f32[512,896]{1,0:T(8,128)S(1)}, f32[64,896]{1,0:T(8,128)S(1)}, f32[64,896]{1,0:T(8,128)S(1)}, f32[32,896]{1,0:T(8,128)S(1)}, f32[32,896]{1,0:T(8,128)S(1)}) custom-call(f32[16,52,128]{2,1,0:T(8,128)S(1)} %all_to_all.10.gathered_ref, f32[16,32]{1,0:T(8,128)S(1)} %copy-done.2, s32[16,32]{1,0:T(8,128)S(1)} %copy-done.3, ...), custom_call_target="tpu_custom_call" | custom-call | tf_op jit(solution)/shard_map/relax/pallas_call | solution.py:433
  19.7 6.1 %collective-permute-start.2 = (f32[32,896]{1,0:T(8,128)S(1)}, f32[32,896]{1,0:T(8,128)S(1)}, u32[]{:S(2)}, u32[]{:S(2)}) collective-permute-start(f32[32,896]{1,0:T(8,128)S(1)} %get-tuple-element.27), channel_id=1, source_target_pairs={{0,16},{16,32},{32,48},{48,0},{1,17},{17,33},{33,49},{49,1},{2,18}... | collective-permute-start | bytes 344072 | tf_op jit(solution)/shard_map/ppermute | solution.py:440
  25.8 5.9 %collective-permute-start.3 = (f32[32,896]{1,0:T(8,128)S(1)}, f32[32,896]{1,0:T(8,128)S(1)}, u32[]{:S(2)}, u32[]{:S(2)}) collective-permute-start(f32[32,896]{1,0:T(8,128)S(1)} %get-tuple-element.28), channel_id=1, source_target_pairs={{16,0},{32,16},{48,32},{0,48},{17,1},{33,17},{49,33},{1,49},{18,2}... | collective-permute-start | bytes 344072 | tf_op jit(solution)/shard_map/ppermute | solution.py:441
  31.7 3.5 %collective-permute-start = (f32[64,896]{1,0:T(8,128)S(1)}, f32[64,896]{1,0:T(8,128)S(1)}, u32[]{:S(2)}, u32[]{:S(2)}) collective-permute-start(f32[64,896]{1,0:T(8,128)S(1)} %get-tuple-element.25), channel_id=1, source_target_pairs={{0,64},{64,128},{128,192},{192,256},{256,320},{320,384},{384,448},... | collective-permute-start | bytes 688136 | tf_op jit(solution)/shard_map/ppermute | solution.py:443
  35.2 2.4 %collective-permute-start.1 = (f32[64,896]{1,0:T(8,128)S(1)}, f32[64,896]{1,0:T(8,128)S(1)}, u32[]{:S(2)}, u32[]{:S(2)}) collective-permute-start(f32[64,896]{1,0:T(8,128)S(1)} %get-tuple-element.26), channel_id=1, source_target_pairs={{64,0},{128,64},{192,128},{256,192},{320,256},{384,320},{448,384},... | collective-permute-start | bytes 688136 | tf_op jit(solution)/shard_map/ppermute | solution.py:444
  37.6 0.0 collective-permute-done.2.low_y_ref
  37.6 0.0 collective-permute-done.3.high_y_ref
  37.6 2.2 %inner.1 = (f32[384,896]{1,0:T(8,128)S(1)}, f32[384,128]{1,0:T(8,128)S(1)}) custom-call(f32[512,896]{1,0:T(8,128)S(1)} %get-tuple-element.24.state_ref, f32[32,896]{1,0:T(8,128)S(1)} %collective-permute-done.2.low_y_ref, f32[32,896]{1,0:T(8,128)S(1)} %collective-permute-done.3.high_y_ref, f32[8,896]{1,0:T(8,128)S(1)} %get-tuple-element.29.courant_ref, ...), custom_call_target="tpu_custom_call" | custom-call | flops 30000001024 | bytes 4000000 | tf_op jit(solution)/shard_map/inner/pallas_call | solution.py:465
  39.8 0.4 collective-permute-done.low_x_ref
  40.2 4.3 %collective-permute-done.1.high_x_ref = f32[64,896]{1,0:T(8,128)S(1)} collective-permute-done((f32[64,896]{1,0:T(8,128)S(1)}, f32[64,896]{1,0:T(8,128)S(1)}, u32[]{:S(2)}, u32[]{:S(2)}) %collective-permute-start.1) | collective-permute-done | bytes 229408 | tf_op jit(solution)/shard_map/ppermute | solution.py:444
  44.4 1.0 %outer.1 = (f32[128,896]{1,0:T(8,128)S(1)}, f32[52,128]{1,0:T(8,128)S(1)}) custom-call(f32[512,896]{1,0:T(8,128)S(1)} %get-tuple-element.24.state_ref, f32[64,896]{1,0:T(8,128)S(1)} %collective-permute-done.low_x_ref, f32[64,896]{1,0:T(8,128)S(1)} %collective-permute-done.1.high_x_ref, f32[32,896]{1,0:T(8,128)S(1)} %collective-permute-done.2.low_y_ref, ...), custom_call_target="tpu_custom_call" | custom-call | tf_op jit(solution)/shard_map/outer/pallas_call | solution.py:471
  45.5 13.3 %all_to_all.11.gathered_ref = f32[16,52,128]{2,1,0:T(8,128)S(1)} all-to-all(f32[16,52,128]{2,1,0:T(8,128)S(1)} %broadcast_in_dim.8), channel_id=1, replica_groups=mesh['sx'=8,'sy'=4,'vel'=16] {'vel'}, dimensions={0} | all-to-all | bytes 851968 | tf_op jit(solution)/shard_map/all_to_all | solution.py:397
  58.8 1.0 %relax.3 = (f32[512,896]{1,0:T(8,128)S(1)}, f32[64,896]{1,0:T(8,128)S(1)}, f32[64,896]{1,0:T(8,128)S(1)}, f32[32,896]{1,0:T(8,128)S(1)}, f32[32,896]{1,0:T(8,128)S(1)}) custom-call(f32[16,52,128]{2,1,0:T(8,128)S(1)} %all_to_all.11.gathered_ref, f32[16,32]{1,0:T(8,128)S(1)} %copy-done.2, s32[16,32]{1,0:T(8,128)S(1)} %copy-done.3, ...), custom_call_target="tpu_custom_call" | custom-call | tf_op jit(solution)/shard_map/relax/pallas_call | solution.py:433
  59.8 2.4 %collective-permute-start.6 = (f32[32,896]{1,0:T(8,128)S(1)}, f32[32,896]{1,0:T(8,128)S(1)}, u32[]{:S(2)}, u32[]{:S(2)}) collective-permute-start(f32[32,896]{1,0:T(8,128)S(1)} %get-tuple-element.37), channel_id=1, source_target_pairs={{0,16},{16,32},{32,48},{48,0},{1,17},{17,33},{33,49},{49,1},{2,18}... | collective-permute-start | bytes 344072 | tf_op jit(solution)/shard_map/ppermute | solution.py:440
  62.3 5.5 %collective-permute-start.7 = (f32[32,896]{1,0:T(8,128)S(1)}, f32[32,896]{1,0:T(8,128)S(1)}, u32[]{:S(2)}, u32[]{:S(2)}) collective-permute-start(f32[32,896]{1,0:T(8,128)S(1)} %get-tuple-element.38), channel_id=1, source_target_pairs={{16,0},{32,16},{48,32},{0,48},{17,1},{33,17},{49,33},{1,49},{18,2}... | collective-permute-start | bytes 344072 | tf_op jit(solution)/shard_map/ppermute | solution.py:441
  67.8 4.9 %collective-permute-start.4 = (f32[64,896]{1,0:T(8,128)S(1)}, f32[64,896]{1,0:T(8,128)S(1)}, u32[]{:S(2)}, u32[]{:S(2)}) collective-permute-start(f32[64,896]{1,0:T(8,128)S(1)} %get-tuple-element.35), channel_id=1, source_target_pairs={{0,64},{64,128},{128,192},{192,256},{256,320},{320,384},{384,448},... | collective-permute-start | bytes 688136 | tf_op jit(solution)/shard_map/ppermute | solution.py:443
  72.7 1.9 %collective-permute-start.5 = (f32[64,896]{1,0:T(8,128)S(1)}, f32[64,896]{1,0:T(8,128)S(1)}, u32[]{:S(2)}, u32[]{:S(2)}) collective-permute-start(f32[64,896]{1,0:T(8,128)S(1)} %get-tuple-element.36), channel_id=1, source_target_pairs={{64,0},{128,64},{192,128},{256,192},{320,256},{384,320},{448,384},... | collective-permute-start | bytes 688136 | tf_op jit(solution)/shard_map/ppermute | solution.py:444
  74.6 0.0 collective-permute-done.6.low_y_ref
  74.6 0.0 collective-permute-done.7.high_y_ref
  74.6 2.9 %last_inner.1.refs_0_ = f32[16,32,864]{2,1,0:T(8,128)} custom-call(f32[512,896]{1,0:T(8,128)S(1)} %get-tuple-element.34.state_ref, f32[32,896]{1,0:T(8,128)S(1)} %collective-permute-done.6.low_y_ref, f32[32,896]{1,0:T(8,128)S(1)} %collective-permute-done.7.high_y_ref, f32[8,896]{1,0:T(8,128)S(1)} %get-tuple-element.29.courant_ref), custom_call_target="tpu_custom_call" | custom-call | flops 30000001024 | bytes 4000000 | tf_op jit(solution)/shard_map/last_inner/pallas_call | solution.py:449
  77.6 0.0 collective-permute-done.4.low_x_ref
  77.6 3.0 %collective-permute-done.5.high_x_ref = f32[64,896]{1,0:T(8,128)S(1)} collective-permute-done((f32[64,896]{1,0:T(8,128)S(1)}, f32[64,896]{1,0:T(8,128)S(1)}, u32[]{:S(2)}, u32[]{:S(2)}) %collective-permute-start.5) | collective-permute-done | bytes 229408 | tf_op jit(solution)/shard_map/ppermute | solution.py:444
  80.6 1.4 %last_outer.1 = f32[16,32,864]{2,1,0:T(8,128)} custom-call(f32[512,896]{1,0:T(8,128)S(1)} %get-tuple-element.34.state_ref, f32[64,896]{1,0:T(8,128)S(1)} %collective-permute-done.4.low_x_ref, f32[64,896]{1,0:T(8,128)S(1)} %collective-permute-done.5.high_x_ref, f32[32,896]{1,0:T(8,128)S(1)} %collective-permute-done.6.low_y_ref, ...), custom_call_target="tpu_custom_call", output_to_operand_aliasing={{}: (6, {})} | custom-call | tf_op jit(solution)/shard_map/last_outer/pallas_call | solution.py:455
  (2 shorter events, 0.1 us)
Async XLA Ops:
  0.0 18.7 %copy-start.2 = (f32[16,32]{1,0:T(8,128)S(1)}, f32[16,32]{1,0:T(8,128)}, u32[]{:S(2)}) copy-start(f32[16,32]{1,0:T(8,128)} %knudsen_ref.3) | copy-start | bytes 6148
  0.3 1.5 %copy-start = (f32[16,32,864]{2,1,0:T(8,128)S(1)}, f32[16,32,864]{2,1,0:T(8,128)}, u32[]{:S(2)}) copy-start(f32[16,32,864]{2,1,0:T(8,128)} %refs_0_.1) | copy-start | bytes 5308420
  1.8 16.9 %copy-start.1 = (f32[16,32,864]{2,1,0:T(8,128)S(1)}, f32[16,32,864]{2,1,0:T(8,128)}, u32[]{:S(2)}) copy-start(f32[16,32,864]{2,1,0:T(8,128)} %refs_0_.1) | copy-start | bytes 5308420
  1.8 16.9 %copy-start.3 = (s32[16,32]{1,0:T(8,128)S(1)}, s32[16,32]{1,0:T(8,128)}, u32[]{:S(2)}) copy-start(s32[16,32]{1,0:T(8,128)} %kind_ref.3) | copy-start | bytes 6148
  19.7 17.8 %collective-permute-start.2 = (f32[32,896]{1,0:T(8,128)S(1)}, f32[32,896]{1,0:T(8,128)S(1)}, u32[]{:S(2)}, u32[]{:S(2)}) collective-permute-start(f32[32,896]{1,0:T(8,128)S(1)} %get-tuple-element.27), channel_id=1, source_target_pairs={{0,16},{16,32},{32,48},{48,0},{1,17},{17,33},{33,49},{49,1},{2,18}... | collective-permute-start | bytes 344072 | tf_op jit(solution)/shard_map/ppermute | solution.py:440
  25.8 11.7 %collective-permute-start.3 = (f32[32,896]{1,0:T(8,128)S(1)}, f32[32,896]{1,0:T(8,128)S(1)}, u32[]{:S(2)}, u32[]{:S(2)}) collective-permute-start(f32[32,896]{1,0:T(8,128)S(1)} %get-tuple-element.28), channel_id=1, source_target_pairs={{16,0},{32,16},{48,32},{0,48},{17,1},{33,17},{49,33},{1,49},{18,2}... | collective-permute-start | bytes 344072 | tf_op jit(solution)/shard_map/ppermute | solution.py:441
  31.7 8.5 %collective-permute-start = (f32[64,896]{1,0:T(8,128)S(1)}, f32[64,896]{1,0:T(8,128)S(1)}, u32[]{:S(2)}, u32[]{:S(2)}) collective-permute-start(f32[64,896]{1,0:T(8,128)S(1)} %get-tuple-element.25), channel_id=1, source_target_pairs={{0,64},{64,128},{128,192},{192,256},{256,320},{320,384},{384,448},... | collective-permute-start | bytes 688136 | tf_op jit(solution)/shard_map/ppermute | solution.py:443
  35.2 9.2 %collective-permute-start.1 = (f32[64,896]{1,0:T(8,128)S(1)}, f32[64,896]{1,0:T(8,128)S(1)}, u32[]{:S(2)}, u32[]{:S(2)}) collective-permute-start(f32[64,896]{1,0:T(8,128)S(1)} %get-tuple-element.26), channel_id=1, source_target_pairs={{64,0},{128,64},{192,128},{256,192},{320,256},{384,320},{448,384},... | collective-permute-start | bytes 688136 | tf_op jit(solution)/shard_map/ppermute | solution.py:444
  59.8 14.8 %collective-permute-start.6 = (f32[32,896]{1,0:T(8,128)S(1)}, f32[32,896]{1,0:T(8,128)S(1)}, u32[]{:S(2)}, u32[]{:S(2)}) collective-permute-start(f32[32,896]{1,0:T(8,128)S(1)} %get-tuple-element.37), channel_id=1, source_target_pairs={{0,16},{16,32},{32,48},{48,0},{1,17},{17,33},{33,49},{49,1},{2,18}... | collective-permute-start | bytes 344072 | tf_op jit(solution)/shard_map/ppermute | solution.py:440
  62.3 12.3 %collective-permute-start.7 = (f32[32,896]{1,0:T(8,128)S(1)}, f32[32,896]{1,0:T(8,128)S(1)}, u32[]{:S(2)}, u32[]{:S(2)}) collective-permute-start(f32[32,896]{1,0:T(8,128)S(1)} %get-tuple-element.38), channel_id=1, source_target_pairs={{16,0},{32,16},{48,32},{0,48},{17,1},{33,17},{49,33},{1,49},{18,2}... | collective-permute-start | bytes 344072 | tf_op jit(solution)/shard_map/ppermute | solution.py:441
  67.8 9.8 %collective-permute-start.4 = (f32[64,896]{1,0:T(8,128)S(1)}, f32[64,896]{1,0:T(8,128)S(1)}, u32[]{:S(2)}, u32[]{:S(2)}) collective-permute-start(f32[64,896]{1,0:T(8,128)S(1)} %get-tuple-element.35), channel_id=1, source_target_pairs={{0,64},{64,128},{128,192},{192,256},{256,320},{320,384},{384,448},... | collective-permute-start | bytes 688136 | tf_op jit(solution)/shard_map/ppermute | solution.py:443
  72.7 7.9 %collective-permute-start.5 = (f32[64,896]{1,0:T(8,128)S(1)}, f32[64,896]{1,0:T(8,128)S(1)}, u32[]{:S(2)}, u32[]{:S(2)}) collective-permute-start(f32[64,896]{1,0:T(8,128)S(1)} %get-tuple-element.36), channel_id=1, source_target_pairs={{64,0},{128,64},{192,128},{256,192},{320,256},{384,320},{448,384},... | collective-permute-start | bytes 688136 | tf_op jit(solution)/shard_map/ppermute | solution.py:444

commit v4 on v3

--- a/solution.py
+++ b/solution.py
@@ -102,23 +102,30 @@
     return out + [value]
 
 
-def add_moments(rows, basis, sums_ref, at):
+def moment_sums(rows, basis):
     high = rows.astype(BF16)
     low = (rows - high.astype(F32)).astype(BF16)
-    sums_ref[at : at + rows.shape[0], :] = jnp.dot(
-        high, basis, preferred_element_type=F32
-    ) + jnp.dot(low, basis, preferred_element_type=F32)
-
-
-def blocks_of(sums_ref, block_ref, totals_ref):
-    chunks = sums_ref.shape[0] // LANE
-    for chunk in range(chunks):
-        turned = sums_ref[chunk * LANE : (chunk + 1) * LANE, :].T
-        block_ref[pl.ds(chunk, 16, stride=chunks), :] = turned[:16, :]
+    return jnp.dot(high, basis, preferred_element_type=F32) + jnp.dot(
+        low, basis, preferred_element_type=F32
+    )
+
+
+def blocks_of(sums, chunk, chunks, block_ref):
+    block_ref[pl.ds(chunk, 16, stride=chunks), :] = sums.T[:16, :]
+
+
+def write_totals(chunks, block_ref, totals_ref):
     totals_ref[: 10 * chunks, :] = block_ref[: 10 * chunks, :]
     totals_ref[10 * chunks :, :] = (
         block_ref[10 * chunks : 13 * chunks, :] + block_ref[13 * chunks : 16 * chunks, :]
     )
+
+
+def rows_in_chunk(chunk, nx, step):
+    if chunk == 0:
+        return [*range(REACH), *range(nx - REACH, nx)]
+    start = REACH + (chunk - 1) * step
+    return list(range(start, start + step))
 
 
 def coefficients(gathered_ref, knudsen_ref, kind_ref, block_ref):
@@ -126,9 +133,9 @@
     step = LANE // ny
     chunks = nx // step
     for i, value in enumerate((knudsen_ref[...], kind_ref[...].astype(F32))):
-        for x in range(0, nx, step):
-            row = [value[x + j : x + j + 1, :] for j in range(step)]
-            at = (MOMENTS + i) * chunks + x // step
+        for chunk in range(chunks):
+            row = [value[x : x + 1, :] for x in rows_in_chunk(chunk, nx, step)]
+            at = (MOMENTS + i) * chunks + chunk
             block_ref[at : at + 1, :] = jnp.concatenate(row, axis=1)
     total = gathered_ref[0]
     for device in range(1, gathered_ref.shape[0]):
@@ -191,10 +198,11 @@
         block_ref[i * chunks : (i + 1) * chunks, :] = value
 
 
-def relaxed_rows(load, chunks, lanes, basis_ref, block_ref, out_ref):
-    tail = 2 * lanes
+def relaxed_rows(load, nx, ny, lanes, basis_ref, block_ref, out_ref):
+    step = LANE // ny
+    chunks, tail = nx // step, 2 * lanes
     for chunk in range(chunks):
-        start = chunk * LANE
+        xs = rows_in_chunk(chunk, nx, step)
         left = block_ref[pl.ds(chunk, COEFFICIENTS, stride=chunks), :].T.astype(BF16)
         pair = jnp.dot(left, basis_ref[:, tail : tail + 2 * LANE], preferred_element_type=F32)
         keep, scale = pair[:, :LANE], pair[:, LANE:]
@@ -203,9 +211,13 @@
                 left, basis_ref[:, 2 * lane : 2 * lane + 2 * LANE], preferred_element_type=F32
             )
             power, linear = pair[:, :LANE], pair[:, LANE:]
-            out_ref[start : start + LANE, lane : lane + LANE] = load(start, lane) * keep + (
+            value = load(chunk, xs, lane) * keep + (
                 jnp.exp2(power) * (scale + linear * (power + 2.5 * LOG2E))
             )
+            for half in (0, step // 2):
+                rows = value[half * ny : (half + step // 2) * ny, :]
+                at = xs[half] * ny
+                out_ref[at : at + rows.shape[0], lane : lane + LANE] = rows
 
 
 def limited(left, right):
@@ -252,14 +264,16 @@
     return side
 
 
-def first_kernel(state_ref, basis_ref, totals_ref, sums_ref, block_ref):
+def first_kernel(state_ref, basis_ref, totals_ref, block_ref):
     nx, ny, velocities = state_ref.shape
     step = LANE // ny
     basis = basis_ref[:velocities, :]
-    for x in range(0, nx, step):
-        rows = state_ref[x : x + step].reshape(step * ny, velocities)
-        add_moments(rows, basis, sums_ref, x * ny)
-    blocks_of(sums_ref, block_ref, totals_ref)
+    for chunk in range(nx // step):
+        xs = rows_in_chunk(chunk, nx, step)
+        halves = [state_ref[xs[i] : xs[i] + step // 2] for i in (0, step // 2)]
+        rows = jnp.concatenate(halves, axis=0).reshape(LANE, velocities)
+        blocks_of(moment_sums(rows, basis), chunk, nx // step, block_ref)
+    write_totals(nx // step, block_ref, totals_ref)
 
 
 def relax_kernel(ny, gathered_ref, knudsen_ref, kind_ref, *refs):
@@ -268,27 +282,26 @@
     nx = cells // ny
     coefficients(gathered_ref, knudsen_ref, kind_ref, block_ref)
 
-    def load(start, lane):
-        if len(state_refs) == 1:
-            (state_ref,) = state_refs
-            velocities = state_ref.shape[2]
-            width = min(LANE, velocities - lane)
-            rows = state_ref[start // ny : (start + LANE) // ny, :, lane : lane + width]
-            rows = rows.reshape(LANE, width)
-            if width == LANE:
-                return rows
-            return jnp.concatenate([rows, jnp.zeros((LANE, LANE - width), F32)], axis=1)
-        inner_ref, outer_ref = state_refs
-        along, edge = slice(lane, lane + LANE), REACH * ny
-        if start == 0:
-            parts = [outer_ref[:edge, along], inner_ref[: LANE - edge, along]]
-        elif start + LANE == cells:
-            parts = [inner_ref[start - edge :, along], outer_ref[edge:, along]]
-        else:
-            return inner_ref[start - edge : start - edge + LANE, along]
-        return jnp.concatenate(parts, axis=0)
-
-    relaxed_rows(load, cells // LANE, lanes, basis_ref, block_ref, out_ref)
+    def load_given(chunk, xs, lane):
+        (state_ref,) = state_refs
+        velocities = state_ref.shape[2]
+        width = min(LANE, velocities - lane)
+        half = len(xs) // 2
+        parts = [state_ref[xs[i] : xs[i] + half, :, lane : lane + width] for i in (0, half)]
+        rows = jnp.concatenate(parts, axis=0).reshape(LANE, width)
+        if width == LANE:
+            return rows
+        return jnp.concatenate([rows, jnp.zeros((LANE, LANE - width), F32)], axis=1)
+
+    def load(chunk, xs, lane):
+        inner_ref, low_ref, high_ref = state_refs
+        along = slice(lane, lane + LANE)
+        if chunk == 0:
+            return jnp.concatenate([low_ref[:, along], high_ref[:, along]], axis=0)
+        return inner_ref[(chunk - 1) * LANE : chunk * LANE, along]
+
+    load = load_given if len(state_refs) == 1 else load
+    relaxed_rows(load, nx, ny, lanes, basis_ref, block_ref, out_ref)
     low_x_ref[...] = out_ref[: REACH * ny, :]
     high_x_ref[...] = out_ref[cells - REACH * ny :, :]
     for x in range(nx):
@@ -305,7 +318,7 @@
         return state_ref[x * ny : (x + 1) * ny, lane : lane + LANE]
 
     if velocities is None:
-        basis_ref, out_ref, sums_ref = refs
+        basis_ref, out_ref, block_ref = refs
 
         def write(x, lane, value):
             at = (x - REACH) * ny
@@ -321,19 +334,22 @@
     side = side_rows(low_y_ref, high_y_ref)
     transported_rows(load, side, range(REACH, nx - REACH), ny, lanes, courant_ref, write)
     if velocities is None:
-        for at in range(0, out_ref.shape[0], LANE):
-            add_moments(out_ref[at : at + LANE, :], basis_ref[...], sums_ref, at)
-
-
-def outer_kernel(ny, final, state_ref, low_x_ref, high_x_ref, low_y_ref, high_y_ref, courant_ref, *refs):
+        chunks = cells // LANE
+        for chunk in range(1, chunks):
+            rows = out_ref[(chunk - 1) * LANE : chunk * LANE, :]
+            blocks_of(moment_sums(rows, basis_ref[...]), chunk, chunks, block_ref)
+
+
+def outer_kernel(ny, high, final, state_ref, side_x_ref, low_y_ref, high_y_ref, courant_ref, *refs):
     cells, lanes = state_ref.shape
     nx = cells // ny
+    first = nx - REACH if high else 0
 
     def load(x, lane):
         if x < 0:
-            ref, x = low_x_ref, x + REACH
+            ref, x = side_x_ref, x + REACH
         elif x >= nx:
-            ref, x = high_x_ref, x - nx
+            ref, x = side_x_ref, x - nx
         else:
             ref = state_ref
         return ref[x * ny : (x + 1) * ny, lane : lane + LANE]
@@ -343,34 +359,36 @@
 
         def write(x, lane, value):
             width = min(LANE, out_ref.shape[2] - lane)
-            at = x if x < REACH else x - nx + 2 * REACH
-            edge_ref[at, :, lane : lane + width] = value[:, :width]
+            edge_ref[x - first, :, lane : lane + width] = value[:, :width]
 
     else:
-        basis_ref, inner_sums_ref, out_ref, totals_ref, sums_ref, block_ref = refs
+        basis_ref, *refs = refs
+        if high:
+            low_sums_ref, inner_block_ref, out_ref, totals_ref, block_ref = refs
+        else:
+            out_ref, sums_ref = refs
 
         def write(x, lane, value):
-            at = (x if x < REACH else x - nx + 2 * REACH) * ny
+            at = (x - first) * ny
             out_ref[at : at + ny, lane : lane + LANE] = value
 
     side = side_rows(low_y_ref, high_y_ref)
-    copies = []
-    for i, xs in enumerate((range(REACH), range(nx - REACH, nx))):
-        transported_rows(load, side, xs, ny, lanes, courant_ref, write)
-        if final:
-            part = edge_ref.at[i * REACH : (i + 1) * REACH]
-            copies.append(
-                pltpu.make_async_copy(part, out_ref.at[xs[0] : xs[0] + REACH], sent.at[i])
-            )
-            copies[-1].start()
-    for copy in copies:
+    xs = range(first, first + REACH)
+    transported_rows(load, side, xs, ny, lanes, courant_ref, write)
+    if final:
+        copy = pltpu.make_async_copy(edge_ref, out_ref.at[first : first + REACH], sent)
+        copy.start()
         copy.wait()
-    if not final:
-        edge = REACH * ny
-        sums_ref[edge : cells - edge, :] = inner_sums_ref[...]
-        for at, to in ((0, 0), (edge, cells - edge)):
-            add_moments(out_ref[at : at + edge, :], basis_ref[...], sums_ref, to)
-        blocks_of(sums_ref, block_ref, totals_ref)
+        return
+    sums = moment_sums(out_ref[...], basis_ref[...])
+    if not high:
+        sums_ref[...] = sums
+        return
+    chunks = cells // LANE
+    block_ref[...] = inner_block_ref[...]
+    sums = jnp.concatenate([low_sums_ref[...], sums], axis=0)
+    blocks_of(sums, 0, chunks, block_ref)
+    write_totals(chunks, block_ref, totals_ref)
 
 
 INNER_COST = pl.CostEstimate(flops=30_000_000_000, bytes_accessed=4_000_000, transcendentals=0)
@@ -408,7 +426,6 @@
     lanes = -(-velocities // LANE) * LANE
     cells = nx * ny
     chunks = cells // LANE
-    sums = pltpu.VMEM((cells, LANE), F32)
     block = pltpu.VMEM((COEFFICIENTS * chunks, LANE), F32)
     totals_shape = rows_of(MOMENTS * chunks, LANE)
     side_x, side_y = rows_of(REACH * ny, lanes), rows_of(REACH * nx, lanes)
@@ -424,7 +441,7 @@
         [pltpu.VMEM((LANE, lanes), F32)],
         in_specs=[pl.BlockSpec(memory_space=pltpu.SMEM)],
     )(jnp.full((1,), lax.axis_index("vel") * velocities, jnp.int32))
-    totals = call(first_kernel, "first_moments", totals_shape, [sums, block])(
+    totals = call(first_kernel, "first_moments", totals_shape, [block])(
         distribution, moment_basis
     )
     state = (distribution,)
@@ -443,38 +460,43 @@
         from_low_x = lax.ppermute(high_x, "sx", up)
         from_high_x = lax.ppermute(low_x, "sx", down)
         sides_y = (from_low_y, from_high_y, courant)
-        sides = (relaxed, from_low_x, from_high_x, *sides_y)
-        inner_cells = cells - 2 * REACH * ny
         if final:
-            inner = call(
+            out = call(
                 functools.partial(inner_kernel, ny, velocities),
                 "last_inner",
                 rows_of(nx, ny, velocities),
                 cost_estimate=INNER_COST,
             )(relaxed, *sides_y)
-            return call(
-                functools.partial(outer_kernel, ny, True),
-                "last_outer",
-                rows_of(nx, ny, velocities),
-                [pltpu.VMEM((2 * REACH, ny, velocities), F32), pltpu.SemaphoreType.DMA((2,))],
-                in_specs=[pl.BlockSpec(memory_space=pltpu.VMEM)] * len(sides)
-                + [pl.BlockSpec(memory_space=pltpu.HBM)],
-                out_specs=pl.BlockSpec(memory_space=pltpu.HBM),
-                input_output_aliases={len(sides): 0},
-            )(*sides, inner)
-        inner, inner_sums = call(
+            for high, side in enumerate((from_low_x, from_high_x)):
+                out = call(
+                    functools.partial(outer_kernel, ny, high, True),
+                    "last_high" if high else "last_low",
+                    rows_of(nx, ny, velocities),
+                    [pltpu.VMEM((REACH, ny, velocities), F32), pltpu.SemaphoreType.DMA],
+                    in_specs=[pl.BlockSpec(memory_space=pltpu.VMEM)] * 5
+                    + [pl.BlockSpec(memory_space=pltpu.HBM)],
+                    out_specs=pl.BlockSpec(memory_space=pltpu.HBM),
+                    input_output_aliases={5: 0},
+                )(relaxed, side, *sides_y, out)
+            return out
+        inner, inner_block = call(
             functools.partial(inner_kernel, ny, None),
             "inner",
-            (rows_of(inner_cells, lanes), rows_of(inner_cells, LANE)),
+            (rows_of(cells - 2 * REACH * ny, lanes), rows_of(16 * chunks, LANE)),
             cost_estimate=INNER_COST,
         )(relaxed, *sides_y, moment_basis)
-        outer, totals = call(
-            functools.partial(outer_kernel, ny, False),
-            "outer",
-            (rows_of(2 * REACH * ny, lanes), totals_shape),
-            [sums, block],
-        )(*sides, moment_basis, inner_sums)
-        state = (inner, outer)
+        low, low_sums = call(
+            functools.partial(outer_kernel, ny, False, False),
+            "outer_low",
+            (side_x, rows_of(REACH * ny, LANE)),
+        )(relaxed, from_low_x, *sides_y, moment_basis)
+        high, totals = call(
+            functools.partial(outer_kernel, ny, True, False),
+            "outer_high",
+            (side_x, totals_shape),
+            [pltpu.VMEM((16 * chunks, LANE), F32)],
+        )(relaxed, from_high_x, *sides_y, moment_basis, low_sums, inner_block)
+        state = (inner, low, high)
 
 
 def solution(mesh):

time: 82.4 us -> 83.1 us (level)
  the two profiles are of different devices: /device:TPU:16 before, /device:TPU:64 now
where the time goes in v4:
time: 83.1 us; the launch traced here: 82.6 us
  starting transfers between devices  31.1 us (37%)
  blocking collectives  29.1 us (35%)
  Pallas kernels  11.5 us (14%)
  waiting for transfers between devices  9.22 us (11%)
  local copies, waits for them, and re-layouts  1.59 us (2%)
    all_to_all x2, blocking collectives, gather(): return lax.all_to_all(copies, 'vel', 0, 0)  29.1 us
    ppermute x2, starting transfers between devices, body(): from_high_y = lax.ppermute(low_y, 'sy', down)  11.4 us
    ppermute x2, waiting for transfers between devices, body(): from_low_x = lax.ppermute(high_x, 'sx', up)  9.21 us
    ppermute x2, starting transfers between devices, body(): from_high_x = lax.ppermute(low_x, 'sx', down)  7.42 us
    ppermute x2, starting transfers between devices, body(): from_low_y = lax.ppermute(high_y, 'sy', up)  6.6 us
    ppermute x2, starting transfers between devices, body(): from_low_x = lax.ppermute(high_x, 'sx', up)  5.72 us
    pallas_call x1, Pallas kernels, body(): call(functools.partial(inner_kernel, ny, velocities), 'last_inner', rows_...  2.95 us
    pallas_call x1, Pallas kernels, body(): call(functools.partial(inner_kernel, ny, None), 'inner', (rows_of(cells -...  2.27 us
  transfers between devices with their start and end apart: 8, of which 2 were waited for; matrix products, arithmetic and copies ran while one was open for 0% of the time, Pallas kernels for 8%

profile of v4, /device:TPU:64, one launch (start us, length us, event | category | flops | bytes accessed | tf_op | source)
XLA Modules:
  0.0 82.6 jit_solution(14096727907312040830)
XLA Ops:
  0.0 0.0 copy-start.2
  0.0 0.3 tables.1
  0.3 0.0 copy-start
  0.3 1.5 %copy-done = f32[16,32,864]{2,1,0:T(8,128)S(1)} copy-done((f32[16,32,864]{2,1,0:T(8,128)S(1)}, f32[16,32,864]{2,1,0:T(8,128)}, u32[]{:S(2)}) %copy-start) | copy-done | bytes 1769496
  1.8 0.0 copy-start.1
  1.8 0.0 copy-start.3
  1.8 0.7 first_moments.1
  2.5 16.5 %all_to_all.10.gathered_ref = f32[16,52,128]{2,1,0:T(8,128)S(1)} all-to-all(f32[16,52,128]{2,1,0:T(8,128)S(1)} %broadcast_in_dim.7), channel_id=1, replica_groups=mesh['sx'=8,'sy'=4,'vel'=16] {'vel'}, dimensions={0} | all-to-all | bytes 851968 | tf_op jit(solution)/shard_map/all_to_all | solution.py:415
  19.1 0.0 copy-done.2
  19.1 0.0 copy-done.1
  19.1 0.0 copy-done.3
  19.1 1.0 %relax.2 = (f32[512,896]{1,0:T(8,128)S(1)}, f32[64,896]{1,0:T(8,128)S(1)}, f32[64,896]{1,0:T(8,128)S(1)}, f32[32,896]{1,0:T(8,128)S(1)}, f32[32,896]{1,0:T(8,128)S(1)}) custom-call(f32[16,52,128]{2,1,0:T(8,128)S(1)} %all_to_all.10.gathered_ref, f32[16,32]{1,0:T(8,128)S(1)} %copy-done.2, s32[16,32]{1,0:T(8,128)S(1)} %copy-done.3, ...), custom_call_target="tpu_custom_call" | custom-call | tf_op jit(solution)/shard_map/relax/pallas_call | solution.py:450
  20.1 4.2 %collective-permute-start.1 = (f32[32,896]{1,0:T(8,128)S(1)}, f32[32,896]{1,0:T(8,128)S(1)}, u32[]{:S(2)}, u32[]{:S(2)}) collective-permute-start(f32[32,896]{1,0:T(8,128)S(1)} %get-tuple-element.28), channel_id=1, source_target_pairs={{0,16},{16,32},{32,48},{48,0},{1,17},{17,33},{33,49},{49,1},{2,18}... | collective-permute-start | bytes 344072 | tf_op jit(solution)/shard_map/ppermute | solution.py:457
  24.3 5.9 %collective-permute-start.2 = (f32[32,896]{1,0:T(8,128)S(1)}, f32[32,896]{1,0:T(8,128)S(1)}, u32[]{:S(2)}, u32[]{:S(2)}) collective-permute-start(f32[32,896]{1,0:T(8,128)S(1)} %get-tuple-element.29), channel_id=1, source_target_pairs={{16,0},{32,16},{48,32},{0,48},{17,1},{33,17},{49,33},{1,49},{18,2}... | collective-permute-start | bytes 344072 | tf_op jit(solution)/shard_map/ppermute | solution.py:458
  30.1 5.4 %collective-permute-start = (f32[64,896]{1,0:T(8,128)S(1)}, f32[64,896]{1,0:T(8,128)S(1)}, u32[]{:S(2)}, u32[]{:S(2)}) collective-permute-start(f32[64,896]{1,0:T(8,128)S(1)} %get-tuple-element.27), channel_id=1, source_target_pairs={{64,0},{128,64},{192,128},{256,192},{320,256},{384,320},{448,384},... | collective-permute-start | bytes 688136 | tf_op jit(solution)/shard_map/ppermute | solution.py:461
  35.5 1.9 %collective-permute-start.3 = (f32[64,896]{1,0:T(8,128)S(1)}, f32[64,896]{1,0:T(8,128)S(1)}, u32[]{:S(2)}, u32[]{:S(2)}) collective-permute-start(f32[64,896]{1,0:T(8,128)S(1)} %get-tuple-element.31), channel_id=1, source_target_pairs={{0,64},{64,128},{128,192},{192,256},{256,320},{320,384},{384,448},... | collective-permute-start | bytes 688136 | tf_op jit(solution)/shard_map/ppermute | solution.py:460
  37.4 0.0 collective-permute-done.1.low_y_ref
  37.5 0.0 collective-permute-done.2.high_y_ref
  37.5 2.3 %inner.1 = (f32[384,896]{1,0:T(8,128)S(1)}, f32[64,128]{1,0:T(8,128)S(1)}) custom-call(f32[512,896]{1,0:T(8,128)S(1)} %get-tuple-element.26.state_ref, f32[32,896]{1,0:T(8,128)S(1)} %collective-permute-done.1.low_y_ref, f32[32,896]{1,0:T(8,128)S(1)} %collective-permute-done.2.high_y_ref, f32[8,896]{1,0:T(8,128)S(1)} %get-tuple-element.30.courant_ref, ...), custom_call_target="tpu_custom_call" | custom-call | flops 30000001024 | bytes 4000000 | tf_op jit(solution)/shard_map/inner/pallas_call | solution.py:482
  39.7 5.9 %collective-permute-done.3.side_x_ref = f32[64,896]{1,0:T(8,128)S(1)} collective-permute-done((f32[64,896]{1,0:T(8,128)S(1)}, f32[64,896]{1,0:T(8,128)S(1)}, u32[]{:S(2)}, u32[]{:S(2)}) %collective-permute-start.3) | collective-permute-done | bytes 229408 | tf_op jit(solution)/shard_map/ppermute | solution.py:460
  45.7 0.6 outer_low.1
  46.3 0.0 collective-permute-done.side_x_ref
  46.3 0.6 outer_high.1
  46.9 12.5 %all_to_all.11.gathered_ref = f32[16,52,128]{2,1,0:T(8,128)S(1)} all-to-all(f32[16,52,128]{2,1,0:T(8,128)S(1)} %broadcast_in_dim.8), channel_id=1, replica_groups=mesh['sx'=8,'sy'=4,'vel'=16] {'vel'}, dimensions={0} | all-to-all | bytes 851968 | tf_op jit(solution)/shard_map/all_to_all | solution.py:415
  59.4 1.0 %relax.3 = (f32[512,896]{1,0:T(8,128)S(1)}, f32[64,896]{1,0:T(8,128)S(1)}, f32[64,896]{1,0:T(8,128)S(1)}, f32[32,896]{1,0:T(8,128)S(1)}, f32[32,896]{1,0:T(8,128)S(1)}) custom-call(f32[16,52,128]{2,1,0:T(8,128)S(1)} %all_to_all.11.gathered_ref, f32[16,32]{1,0:T(8,128)S(1)} %copy-done.2, s32[16,32]{1,0:T(8,128)S(1)} %copy-done.3, ...), custom_call_target="tpu_custom_call" | custom-call | tf_op jit(solution)/shard_map/relax/pallas_call | solution.py:450
  60.5 2.4 %collective-permute-start.5 = (f32[32,896]{1,0:T(8,128)S(1)}, f32[32,896]{1,0:T(8,128)S(1)}, u32[]{:S(2)}, u32[]{:S(2)}) collective-permute-start(f32[32,896]{1,0:T(8,128)S(1)} %get-tuple-element.40), channel_id=1, source_target_pairs={{0,16},{16,32},{32,48},{48,0},{1,17},{17,33},{33,49},{49,1},{2,18}... | collective-permute-start | bytes 344072 | tf_op jit(solution)/shard_map/ppermute | solution.py:457
  62.9 5.5 %collective-permute-start.6 = (f32[32,896]{1,0:T(8,128)S(1)}, f32[32,896]{1,0:T(8,128)S(1)}, u32[]{:S(2)}, u32[]{:S(2)}) collective-permute-start(f32[32,896]{1,0:T(8,128)S(1)} %get-tuple-element.41), channel_id=1, source_target_pairs={{16,0},{32,16},{48,32},{0,48},{17,1},{33,17},{49,33},{1,49},{18,2}... | collective-permute-start | bytes 344072 | tf_op jit(solution)/shard_map/ppermute | solution.py:458
  68.4 2.0 %collective-permute-start.4 = (f32[64,896]{1,0:T(8,128)S(1)}, f32[64,896]{1,0:T(8,128)S(1)}, u32[]{:S(2)}, u32[]{:S(2)}) collective-permute-start(f32[64,896]{1,0:T(8,128)S(1)} %get-tuple-element.39), channel_id=1, source_target_pairs={{64,0},{128,64},{192,128},{256,192},{320,256},{384,320},{448,384},... | collective-permute-start | bytes 688136 | tf_op jit(solution)/shard_map/ppermute | solution.py:461
  70.5 3.8 %collective-permute-start.7 = (f32[64,896]{1,0:T(8,128)S(1)}, f32[64,896]{1,0:T(8,128)S(1)}, u32[]{:S(2)}, u32[]{:S(2)}) collective-permute-start(f32[64,896]{1,0:T(8,128)S(1)} %get-tuple-element.42), channel_id=1, source_target_pairs={{0,64},{64,128},{128,192},{192,256},{256,320},{320,384},{384,448},... | collective-permute-start | bytes 688136 | tf_op jit(solution)/shard_map/ppermute | solution.py:460
  74.3 0.0 collective-permute-done.5.low_y_ref
  74.3 0.0 collective-permute-done.6.high_y_ref
  74.3 3.0 %last_inner.1.refs_0_ = f32[16,32,864]{2,1,0:T(8,128)} custom-call(f32[512,896]{1,0:T(8,128)S(1)} %get-tuple-element.38.state_ref, f32[32,896]{1,0:T(8,128)S(1)} %collective-permute-done.5.low_y_ref, f32[32,896]{1,0:T(8,128)S(1)} %collective-permute-done.6.high_y_ref, f32[8,896]{1,0:T(8,128)S(1)} %get-tuple-element.30.courant_ref), custom_call_target="tpu_custom_call" | custom-call | flops 30000001024 | bytes 4000000 | tf_op jit(solution)/shard_map/last_inner/pallas_call | solution.py:464
  77.3 3.3 %collective-permute-done.7.side_x_ref = f32[64,896]{1,0:T(8,128)S(1)} collective-permute-done((f32[64,896]{1,0:T(8,128)S(1)}, f32[64,896]{1,0:T(8,128)S(1)}, u32[]{:S(2)}, u32[]{:S(2)}) %collective-permute-start.7) | collective-permute-done | bytes 229408 | tf_op jit(solution)/shard_map/ppermute | solution.py:460
  80.5 1.0 %last_low.1.refs_0_ = f32[16,32,864]{2,1,0:T(8,128)} custom-call(f32[512,896]{1,0:T(8,128)S(1)} %get-tuple-element.38.state_ref, f32[64,896]{1,0:T(8,128)S(1)} %collective-permute-done.7.side_x_ref, f32[32,896]{1,0:T(8,128)S(1)} %collective-permute-done.5.low_y_ref, f32[32,896]{1,0:T(8,128)S(1)} %collective-permute-done.6.high_y_ref, ...), custom_call_target="tpu_custom_call", output_to_operand_aliasing={{}: (5, {})} | custom-call | tf_op jit(solution)/shard_map/last_low/pallas_call | solution.py:471
  81.6 0.0 collective-permute-done.4.side_x_ref
  81.6 1.0 %last_high.1 = f32[16,32,864]{2,1,0:T(8,128)} custom-call(f32[512,896]{1,0:T(8,128)S(1)} %get-tuple-element.38.state_ref, f32[64,896]{1,0:T(8,128)S(1)} %collective-permute-done.4.side_x_ref, f32[32,896]{1,0:T(8,128)S(1)} %collective-permute-done.5.low_y_ref, f32[32,896]{1,0:T(8,128)S(1)} %collective-permute-done.6.high_y_ref, ...), custom_call_target="tpu_custom_call", output_to_operand_aliasing={{}: (5, {})} | custom-call | tf_op jit(solution)/shard_map/last_high/pallas_call | solution.py:471
  (2 shorter events, 0.1 us)
Async XLA Ops:
  0.0 19.1 %copy-start.2 = (f32[16,32]{1,0:T(8,128)S(1)}, f32[16,32]{1,0:T(8,128)}, u32[]{:S(2)}) copy-start(f32[16,32]{1,0:T(8,128)} %knudsen_ref.3) | copy-start | bytes 6148
  0.3 1.5 %copy-start = (f32[16,32,864]{2,1,0:T(8,128)S(1)}, f32[16,32,864]{2,1,0:T(8,128)}, u32[]{:S(2)}) copy-start(f32[16,32,864]{2,1,0:T(8,128)} %refs_0_.1) | copy-start | bytes 5308420
  1.8 17.3 %copy-start.1 = (f32[16,32,864]{2,1,0:T(8,128)S(1)}, f32[16,32,864]{2,1,0:T(8,128)}, u32[]{:S(2)}) copy-start(f32[16,32,864]{2,1,0:T(8,128)} %refs_0_.1) | copy-start | bytes 5308420
  1.8 17.3 %copy-start.3 = (s32[16,32]{1,0:T(8,128)S(1)}, s32[16,32]{1,0:T(8,128)}, u32[]{:S(2)}) copy-start(s32[16,32]{1,0:T(8,128)} %kind_ref.3) | copy-start | bytes 6148
  20.1 17.4 %collective-permute-start.1 = (f32[32,896]{1,0:T(8,128)S(1)}, f32[32,896]{1,0:T(8,128)S(1)}, u32[]{:S(2)}, u32[]{:S(2)}) collective-permute-start(f32[32,896]{1,0:T(8,128)S(1)} %get-tuple-element.28), channel_id=1, source_target_pairs={{0,16},{16,32},{32,48},{48,0},{1,17},{17,33},{33,49},{49,1},{2,18}... | collective-permute-start | bytes 344072 | tf_op jit(solution)/shard_map/ppermute | solution.py:457
  24.3 13.2 %collective-permute-start.2 = (f32[32,896]{1,0:T(8,128)S(1)}, f32[32,896]{1,0:T(8,128)S(1)}, u32[]{:S(2)}, u32[]{:S(2)}) collective-permute-start(f32[32,896]{1,0:T(8,128)S(1)} %get-tuple-element.29), channel_id=1, source_target_pairs={{16,0},{32,16},{48,32},{0,48},{17,1},{33,17},{49,33},{1,49},{18,2}... | collective-permute-start | bytes 344072 | tf_op jit(solution)/shard_map/ppermute | solution.py:458
  30.1 16.1 %collective-permute-start = (f32[64,896]{1,0:T(8,128)S(1)}, f32[64,896]{1,0:T(8,128)S(1)}, u32[]{:S(2)}, u32[]{:S(2)}) collective-permute-start(f32[64,896]{1,0:T(8,128)S(1)} %get-tuple-element.27), channel_id=1, source_target_pairs={{64,0},{128,64},{192,128},{256,192},{320,256},{384,320},{448,384},... | collective-permute-start | bytes 688136 | tf_op jit(solution)/shard_map/ppermute | solution.py:461
  35.5 10.2 %collective-permute-start.3 = (f32[64,896]{1,0:T(8,128)S(1)}, f32[64,896]{1,0:T(8,128)S(1)}, u32[]{:S(2)}, u32[]{:S(2)}) collective-permute-start(f32[64,896]{1,0:T(8,128)S(1)} %get-tuple-element.31), channel_id=1, source_target_pairs={{0,64},{64,128},{128,192},{192,256},{256,320},{320,384},{384,448},... | collective-permute-start | bytes 688136 | tf_op jit(solution)/shard_map/ppermute | solution.py:460
  60.5 13.8 %collective-permute-start.5 = (f32[32,896]{1,0:T(8,128)S(1)}, f32[32,896]{1,0:T(8,128)S(1)}, u32[]{:S(2)}, u32[]{:S(2)}) collective-permute-start(f32[32,896]{1,0:T(8,128)S(1)} %get-tuple-element.40), channel_id=1, source_target_pairs={{0,16},{16,32},{32,48},{48,0},{1,17},{17,33},{33,49},{49,1},{2,18}... | collective-permute-start | bytes 344072 | tf_op jit(solution)/shard_map/ppermute | solution.py:457
  62.9 11.4 %collective-permute-start.6 = (f32[32,896]{1,0:T(8,128)S(1)}, f32[32,896]{1,0:T(8,128)S(1)}, u32[]{:S(2)}, u32[]{:S(2)}) collective-permute-start(f32[32,896]{1,0:T(8,128)S(1)} %get-tuple-element.41), channel_id=1, source_target_pairs={{16,0},{32,16},{48,32},{0,48},{17,1},{33,17},{49,33},{1,49},{18,2}... | collective-permute-start | bytes 344072 | tf_op jit(solution)/shard_map/ppermute | solution.py:458
  68.4 13.1 %collective-permute-start.4 = (f32[64,896]{1,0:T(8,128)S(1)}, f32[64,896]{1,0:T(8,128)S(1)}, u32[]{:S(2)}, u32[]{:S(2)}) collective-permute-start(f32[64,896]{1,0:T(8,128)S(1)} %get-tuple-element.39), channel_id=1, source_target_pairs={{64,0},{128,64},{192,128},{256,192},{320,256},{384,320},{448,384},... | collective-permute-start | bytes 688136 | tf_op jit(solution)/shard_map/ppermute | solution.py:461
  70.5 10.0 %collective-permute-start.7 = (f32[64,896]{1,0:T(8,128)S(1)}, f32[64,896]{1,0:T(8,128)S(1)}, u32[]{:S(2)}, u32[]{:S(2)}) collective-permute-start(f32[64,896]{1,0:T(8,128)S(1)} %get-tuple-element.42), channel_id=1, source_target_pairs={{0,64},{64,128},{128,192},{192,256},{256,320},{320,384},{384,448},... | collective-permute-start | bytes 688136 | tf_op jit(solution)/shard_map/ppermute | solution.py:460

commit v5 on v4

--- a/solution.py
+++ b/solution.py
@@ -391,7 +391,8 @@
     write_totals(chunks, block_ref, totals_ref)
 
 
-INNER_COST = pl.CostEstimate(flops=30_000_000_000, bytes_accessed=4_000_000, transcendentals=0)
+INNER_COST = pl.CostEstimate(flops=2_000_000_000, bytes_accessed=1000, transcendentals=0)
+LOW_COST = pl.CostEstimate(flops=1_000_000_000, bytes_accessed=1000, transcendentals=0)
 
 
 def rows_of(*shape):
@@ -477,6 +478,7 @@
                     + [pl.BlockSpec(memory_space=pltpu.HBM)],
                     out_specs=pl.BlockSpec(memory_space=pltpu.HBM),
                     input_output_aliases={5: 0},
+                    cost_estimate=None if high else LOW_COST,
                 )(relaxed, side, *sides_y, out)
             return out
         inner, inner_block = call(
@@ -489,6 +491,7 @@
             functools.partial(outer_kernel, ny, False, False),
             "outer_low",
             (side_x, rows_of(REACH * ny, LANE)),
+            cost_estimate=LOW_COST,
         )(relaxed, from_low_x, *sides_y, moment_basis)
         high, totals = call(
             functools.partial(outer_kernel, ny, True, False),

time: 83.1 us -> 81.6 us (0.982)
  the two profiles are of different devices: /device:TPU:64 before, /device:TPU:16 now
where the time goes in v5:
time: 81.6 us; the launch traced here: 81.2 us
  starting transfers between devices  32.5 us (40%)
  blocking collectives  29.5 us (36%)
  Pallas kernels  11.5 us (14%)
  waiting for transfers between devices  6 us (7%)
  local copies, waits for them, and re-layouts  1.59 us (2%)
    all_to_all x2, blocking collectives, gather(): return lax.all_to_all(copies, 'vel', 0, 0)  29.5 us
    ppermute x2, starting transfers between devices, body(): from_high_y = lax.ppermute(low_y, 'sy', down)  11.4 us
    ppermute x2, starting transfers between devices, body(): from_low_y = lax.ppermute(high_y, 'sy', up)  8.55 us
    ppermute x2, starting transfers between devices, body(): from_low_x = lax.ppermute(high_x, 'sx', up)  8.34 us
    ppermute x2, waiting for transfers between devices, body(): from_high_x = lax.ppermute(low_x, 'sx', down)  5.65 us
    ppermute x2, starting transfers between devices, body(): from_high_x = lax.ppermute(low_x, 'sx', down)  4.27 us
    pallas_call x1, Pallas kernels, body(): call(functools.partial(inner_kernel, ny, velocities), 'last_inner', rows_...  2.95 us
    pallas_call x1, Pallas kernels, body(): call(functools.partial(inner_kernel, ny, None), 'inner', (rows_of(cells -...  2.25 us
  transfers between devices with their start and end apart: 8, of which 3 were waited for; matrix products, arithmetic and copies ran while one was open for 0% of the time, Pallas kernels for 8%

profile of v5, /device:TPU:16, one launch (start us, length us, event | category | flops | bytes accessed | tf_op | source)
XLA Modules:
  0.0 81.2 jit_solution(7411957541484376941)
XLA Ops:
  0.0 0.0 copy-start.2
  0.0 0.3 tables.1
  0.3 0.0 copy-start
  0.3 1.5 %copy-done = f32[16,32,864]{2,1,0:T(8,128)S(1)} copy-done((f32[16,32,864]{2,1,0:T(8,128)S(1)}, f32[16,32,864]{2,1,0:T(8,128)}, u32[]{:S(2)}) %copy-start) | copy-done | bytes 1769496
  1.8 0.0 copy-start.1
  1.8 0.0 copy-start.3
  1.8 0.7 first_moments.1
  2.5 16.2 %all_to_all.10.gathered_ref = f32[16,52,128]{2,1,0:T(8,128)S(1)} all-to-all(f32[16,52,128]{2,1,0:T(8,128)S(1)} %broadcast_in_dim.7), channel_id=1, replica_groups=mesh['sx'=8,'sy'=4,'vel'=16] {'vel'}, dimensions={0} | all-to-all | bytes 851968 | tf_op jit(solution)/shard_map/all_to_all | solution.py:416
  18.7 0.0 copy-done.2
  18.7 0.0 copy-done.1
  18.7 0.0 copy-done.3
  18.7 1.0 %relax.2 = (f32[512,896]{1,0:T(8,128)S(1)}, f32[64,896]{1,0:T(8,128)S(1)}, f32[64,896]{1,0:T(8,128)S(1)}, f32[32,896]{1,0:T(8,128)S(1)}, f32[32,896]{1,0:T(8,128)S(1)}) custom-call(f32[16,52,128]{2,1,0:T(8,128)S(1)} %all_to_all.10.gathered_ref, f32[16,32]{1,0:T(8,128)S(1)} %copy-done.2, s32[16,32]{1,0:T(8,128)S(1)} %copy-done.3, ...), custom_call_target="tpu_custom_call" | custom-call | tf_op jit(solution)/shard_map/relax/pallas_call | solution.py:451
  19.7 6.1 %collective-permute-start.1 = (f32[32,896]{1,0:T(8,128)S(1)}, f32[32,896]{1,0:T(8,128)S(1)}, u32[]{:S(2)}, u32[]{:S(2)}) collective-permute-start(f32[32,896]{1,0:T(8,128)S(1)} %get-tuple-element.28), channel_id=1, source_target_pairs={{0,16},{16,32},{32,48},{48,0},{1,17},{17,33},{33,49},{49,1},{2,18}... | collective-permute-start | bytes 344072 | tf_op jit(solution)/shard_map/ppermute | solution.py:458
  25.9 5.9 %collective-permute-start.2 = (f32[32,896]{1,0:T(8,128)S(1)}, f32[32,896]{1,0:T(8,128)S(1)}, u32[]{:S(2)}, u32[]{:S(2)}) collective-permute-start(f32[32,896]{1,0:T(8,128)S(1)} %get-tuple-element.29), channel_id=1, source_target_pairs={{16,0},{32,16},{48,32},{0,48},{17,1},{33,17},{49,33},{1,49},{18,2}... | collective-permute-start | bytes 344072 | tf_op jit(solution)/shard_map/ppermute | solution.py:459
  31.7 3.5 %collective-permute-start.3 = (f32[64,896]{1,0:T(8,128)S(1)}, f32[64,896]{1,0:T(8,128)S(1)}, u32[]{:S(2)}, u32[]{:S(2)}) collective-permute-start(f32[64,896]{1,0:T(8,128)S(1)} %get-tuple-element.31), channel_id=1, source_target_pairs={{0,64},{64,128},{128,192},{192,256},{256,320},{320,384},{384,448},... | collective-permute-start | bytes 688136 | tf_op jit(solution)/shard_map/ppermute | solution.py:461
  35.2 2.3 %collective-permute-start = (f32[64,896]{1,0:T(8,128)S(1)}, f32[64,896]{1,0:T(8,128)S(1)}, u32[]{:S(2)}, u32[]{:S(2)}) collective-permute-start(f32[64,896]{1,0:T(8,128)S(1)} %get-tuple-element.27), channel_id=1, source_target_pairs={{64,0},{128,64},{192,128},{256,192},{320,256},{384,320},{448,384},... | collective-permute-start | bytes 688136 | tf_op jit(solution)/shard_map/ppermute | solution.py:462
  37.6 0.0 collective-permute-done.1.low_y_ref
  37.6 0.0 collective-permute-done.2.high_y_ref
  37.6 2.2 %inner.1 = (f32[384,896]{1,0:T(8,128)S(1)}, f32[64,128]{1,0:T(8,128)S(1)}) custom-call(f32[512,896]{1,0:T(8,128)S(1)} %get-tuple-element.26.state_ref, f32[32,896]{1,0:T(8,128)S(1)} %collective-permute-done.1.low_y_ref, f32[32,896]{1,0:T(8,128)S(1)} %collective-permute-done.2.high_y_ref, f32[8,896]{1,0:T(8,128)S(1)} %get-tuple-element.30.courant_ref, ...), custom_call_target="tpu_custom_call" | custom-call | flops 2000000000 | bytes 1000 | tf_op jit(solution)/shard_map/inner/pallas_call | solution.py:484
  39.9 0.3 collective-permute-done.3.side_x_ref
  40.2 0.6 outer_low.1
  40.8 3.7 %collective-permute-done.side_x_ref = f32[64,896]{1,0:T(8,128)S(1)} collective-permute-done((f32[64,896]{1,0:T(8,128)S(1)}, f32[64,896]{1,0:T(8,128)S(1)}, u32[]{:S(2)}, u32[]{:S(2)}) %collective-permute-start) | collective-permute-done | bytes 229408 | tf_op jit(solution)/shard_map/ppermute | solution.py:462
  44.5 0.6 outer_high.1
  45.1 13.3 %all_to_all.11.gathered_ref = f32[16,52,128]{2,1,0:T(8,128)S(1)} all-to-all(f32[16,52,128]{2,1,0:T(8,128)S(1)} %broadcast_in_dim.8), channel_id=1, replica_groups=mesh['sx'=8,'sy'=4,'vel'=16] {'vel'}, dimensions={0} | all-to-all | bytes 851968 | tf_op jit(solution)/shard_map/all_to_all | solution.py:416
  58.4 1.0 %relax.3 = (f32[512,896]{1,0:T(8,128)S(1)}, f32[64,896]{1,0:T(8,128)S(1)}, f32[64,896]{1,0:T(8,128)S(1)}, f32[32,896]{1,0:T(8,128)S(1)}, f32[32,896]{1,0:T(8,128)S(1)}) custom-call(f32[16,52,128]{2,1,0:T(8,128)S(1)} %all_to_all.11.gathered_ref, f32[16,32]{1,0:T(8,128)S(1)} %copy-done.2, s32[16,32]{1,0:T(8,128)S(1)} %copy-done.3, ...), custom_call_target="tpu_custom_call" | custom-call | tf_op jit(solution)/shard_map/relax/pallas_call | solution.py:451
  59.4 2.5 %collective-permute-start.5 = (f32[32,896]{1,0:T(8,128)S(1)}, f32[32,896]{1,0:T(8,128)S(1)}, u32[]{:S(2)}, u32[]{:S(2)}) collective-permute-start(f32[32,896]{1,0:T(8,128)S(1)} %get-tuple-element.40), channel_id=1, source_target_pairs={{0,16},{16,32},{32,48},{48,0},{1,17},{17,33},{33,49},{49,1},{2,18}... | collective-permute-start | bytes 344072 | tf_op jit(solution)/shard_map/ppermute | solution.py:458
  61.9 5.5 %collective-permute-start.6 = (f32[32,896]{1,0:T(8,128)S(1)}, f32[32,896]{1,0:T(8,128)S(1)}, u32[]{:S(2)}, u32[]{:S(2)}) collective-permute-start(f32[32,896]{1,0:T(8,128)S(1)} %get-tuple-element.41), channel_id=1, source_target_pairs={{16,0},{32,16},{48,32},{0,48},{17,1},{33,17},{49,33},{1,49},{18,2}... | collective-permute-start | bytes 344072 | tf_op jit(solution)/shard_map/ppermute | solution.py:459
  67.4 4.8 %collective-permute-start.7 = (f32[64,896]{1,0:T(8,128)S(1)}, f32[64,896]{1,0:T(8,128)S(1)}, u32[]{:S(2)}, u32[]{:S(2)}) collective-permute-start(f32[64,896]{1,0:T(8,128)S(1)} %get-tuple-element.42), channel_id=1, source_target_pairs={{0,64},{64,128},{128,192},{192,256},{256,320},{320,384},{384,448},... | collective-permute-start | bytes 688136 | tf_op jit(solution)/shard_map/ppermute | solution.py:461
  72.2 1.9 %collective-permute-start.4 = (f32[64,896]{1,0:T(8,128)S(1)}, f32[64,896]{1,0:T(8,128)S(1)}, u32[]{:S(2)}, u32[]{:S(2)}) collective-permute-start(f32[64,896]{1,0:T(8,128)S(1)} %get-tuple-element.39), channel_id=1, source_target_pairs={{64,0},{128,64},{192,128},{256,192},{320,256},{384,320},{448,384},... | collective-permute-start | bytes 688136 | tf_op jit(solution)/shard_map/ppermute | solution.py:462
  74.2 0.0 collective-permute-done.5.low_y_ref
  74.2 0.0 collective-permute-done.6.high_y_ref
  74.2 2.9 %last_inner.1.refs_0_ = f32[16,32,864]{2,1,0:T(8,128)} custom-call(f32[512,896]{1,0:T(8,128)S(1)} %get-tuple-element.38.state_ref, f32[32,896]{1,0:T(8,128)S(1)} %collective-permute-done.5.low_y_ref, f32[32,896]{1,0:T(8,128)S(1)} %collective-permute-done.6.high_y_ref, f32[8,896]{1,0:T(8,128)S(1)} %get-tuple-element.30.courant_ref), custom_call_target="tpu_custom_call" | custom-call | flops 2000000000 | bytes 1000 | tf_op jit(solution)/shard_map/last_inner/pallas_call | solution.py:465
  77.1 0.0 collective-permute-done.7.side_x_ref
  77.2 1.0 %last_low.1.refs_0_ = f32[16,32,864]{2,1,0:T(8,128)} custom-call(f32[512,896]{1,0:T(8,128)S(1)} %get-tuple-element.38.state_ref, f32[64,896]{1,0:T(8,128)S(1)} %collective-permute-done.7.side_x_ref, f32[32,896]{1,0:T(8,128)S(1)} %collective-permute-done.5.low_y_ref, f32[32,896]{1,0:T(8,128)S(1)} %collective-permute-done.6.high_y_ref, ...), custom_call_target="tpu_custom_call", output_to_operand_aliasing={{}: (5, {})} | custom-call | flops 1000000000 | bytes 1000 | tf_op jit(solution)/shard_map/last_low/pallas_call | solution.py:472
  78.2 2.0 %collective-permute-done.4.side_x_ref = f32[64,896]{1,0:T(8,128)S(1)} collective-permute-done((f32[64,896]{1,0:T(8,128)S(1)}, f32[64,896]{1,0:T(8,128)S(1)}, u32[]{:S(2)}, u32[]{:S(2)}) %collective-permute-start.4) | collective-permute-done | bytes 229408 | tf_op jit(solution)/shard_map/ppermute | solution.py:462
  80.2 1.0 %last_high.1 = f32[16,32,864]{2,1,0:T(8,128)} custom-call(f32[512,896]{1,0:T(8,128)S(1)} %get-tuple-element.38.state_ref, f32[64,896]{1,0:T(8,128)S(1)} %collective-permute-done.4.side_x_ref, f32[32,896]{1,0:T(8,128)S(1)} %collective-permute-done.5.low_y_ref, f32[32,896]{1,0:T(8,128)S(1)} %collective-permute-done.6.high_y_ref, ...), custom_call_target="tpu_custom_call", output_to_operand_aliasing={{}: (5, {})} | custom-call | tf_op jit(solution)/shard_map/last_high/pallas_call | solution.py:472
  (2 shorter events, 0.1 us)
Async XLA Ops:
  0.0 18.7 %copy-start.2 = (f32[16,32]{1,0:T(8,128)S(1)}, f32[16,32]{1,0:T(8,128)}, u32[]{:S(2)}) copy-start(f32[16,32]{1,0:T(8,128)} %knudsen_ref.3) | copy-start | bytes 6148
  0.3 1.5 %copy-start = (f32[16,32,864]{2,1,0:T(8,128)S(1)}, f32[16,32,864]{2,1,0:T(8,128)}, u32[]{:S(2)}) copy-start(f32[16,32,864]{2,1,0:T(8,128)} %refs_0_.1) | copy-start | bytes 5308420
  1.8 16.9 %copy-start.1 = (f32[16,32,864]{2,1,0:T(8,128)S(1)}, f32[16,32,864]{2,1,0:T(8,128)}, u32[]{:S(2)}) copy-start(f32[16,32,864]{2,1,0:T(8,128)} %refs_0_.1) | copy-start | bytes 5308420
  1.8 16.9 %copy-start.3 = (s32[16,32]{1,0:T(8,128)S(1)}, s32[16,32]{1,0:T(8,128)}, u32[]{:S(2)}) copy-start(s32[16,32]{1,0:T(8,128)} %kind_ref.3) | copy-start | bytes 6148
  19.7 17.8 %collective-permute-start.1 = (f32[32,896]{1,0:T(8,128)S(1)}, f32[32,896]{1,0:T(8,128)S(1)}, u32[]{:S(2)}, u32[]{:S(2)}) collective-permute-start(f32[32,896]{1,0:T(8,128)S(1)} %get-tuple-element.28), channel_id=1, source_target_pairs={{0,16},{16,32},{32,48},{48,0},{1,17},{17,33},{33,49},{49,1},{2,18}... | collective-permute-start | bytes 344072 | tf_op jit(solution)/shard_map/ppermute | solution.py:458
  25.9 11.7 %collective-permute-start.2 = (f32[32,896]{1,0:T(8,128)S(1)}, f32[32,896]{1,0:T(8,128)S(1)}, u32[]{:S(2)}, u32[]{:S(2)}) collective-permute-start(f32[32,896]{1,0:T(8,128)S(1)} %get-tuple-element.29), channel_id=1, source_target_pairs={{16,0},{32,16},{48,32},{0,48},{17,1},{33,17},{49,33},{1,49},{18,2}... | collective-permute-start | bytes 344072 | tf_op jit(solution)/shard_map/ppermute | solution.py:459
  31.7 8.5 %collective-permute-start.3 = (f32[64,896]{1,0:T(8,128)S(1)}, f32[64,896]{1,0:T(8,128)S(1)}, u32[]{:S(2)}, u32[]{:S(2)}) collective-permute-start(f32[64,896]{1,0:T(8,128)S(1)} %get-tuple-element.31), channel_id=1, source_target_pairs={{0,64},{64,128},{128,192},{192,256},{256,320},{320,384},{384,448},... | collective-permute-start | bytes 688136 | tf_op jit(solution)/shard_map/ppermute | solution.py:461
  35.2 9.2 %collective-permute-start = (f32[64,896]{1,0:T(8,128)S(1)}, f32[64,896]{1,0:T(8,128)S(1)}, u32[]{:S(2)}, u32[]{:S(2)}) collective-permute-start(f32[64,896]{1,0:T(8,128)S(1)} %get-tuple-element.27), channel_id=1, source_target_pairs={{64,0},{128,64},{192,128},{256,192},{320,256},{384,320},{448,384},... | collective-permute-start | bytes 688136 | tf_op jit(solution)/shard_map/ppermute | solution.py:462
  59.4 14.8 %collective-permute-start.5 = (f32[32,896]{1,0:T(8,128)S(1)}, f32[32,896]{1,0:T(8,128)S(1)}, u32[]{:S(2)}, u32[]{:S(2)}) collective-permute-start(f32[32,896]{1,0:T(8,128)S(1)} %get-tuple-element.40), channel_id=1, source_target_pairs={{0,16},{16,32},{32,48},{48,0},{1,17},{17,33},{33,49},{49,1},{2,18}... | collective-permute-start | bytes 344072 | tf_op jit(solution)/shard_map/ppermute | solution.py:458
  61.9 12.3 %collective-permute-start.6 = (f32[32,896]{1,0:T(8,128)S(1)}, f32[32,896]{1,0:T(8,128)S(1)}, u32[]{:S(2)}, u32[]{:S(2)}) collective-permute-start(f32[32,896]{1,0:T(8,128)S(1)} %get-tuple-element.41), channel_id=1, source_target_pairs={{16,0},{32,16},{48,32},{0,48},{17,1},{33,17},{49,33},{1,49},{18,2}... | collective-permute-start | bytes 344072 | tf_op jit(solution)/shard_map/ppermute | solution.py:459
  67.4 9.8 %collective-permute-start.7 = (f32[64,896]{1,0:T(8,128)S(1)}, f32[64,896]{1,0:T(8,128)S(1)}, u32[]{:S(2)}, u32[]{:S(2)}) collective-permute-start(f32[64,896]{1,0:T(8,128)S(1)} %get-tuple-element.42), channel_id=1, source_target_pairs={{0,64},{64,128},{128,192},{192,256},{256,320},{320,384},{384,448},... | collective-permute-start | bytes 688136 | tf_op jit(solution)/shard_map/ppermute | solution.py:461
  72.2 7.9 %collective-permute-start.4 = (f32[64,896]{1,0:T(8,128)S(1)}, f32[64,896]{1,0:T(8,128)S(1)}, u32[]{:S(2)}, u32[]{:S(2)}) collective-permute-start(f32[64,896]{1,0:T(8,128)S(1)} %get-tuple-element.39), channel_id=1, source_target_pairs={{64,0},{128,64},{192,128},{256,192},{320,256},{384,320},{448,384},... | collective-permute-start | bytes 688136 | tf_op jit(solution)/shard_map/ppermute | solution.py:462

commit v6 on v5

--- a/solution.py
+++ b/solution.py
@@ -121,20 +121,24 @@
     )
 
 
-def rows_in_chunk(chunk, nx, step):
-    if chunk == 0:
-        return [*range(REACH), *range(nx - REACH, nx)]
-    start = REACH + (chunk - 1) * step
-    return list(range(start, start + step))
+def pieces_in_chunk(chunk, nx, ny):
+    inner = range(2 * REACH, nx - 2 * REACH)
+    if chunk < 2:
+        start = REACH * chunk
+        xs = [*range(start, start + REACH), *range(nx - start - REACH, nx - start)]
+        return [(x, 0, ny) for x in xs]
+    end = ny // 4
+    if chunk == 2:
+        return [(x, y, end) for x in inner for y in (0, ny - end)]
+    return [(x, end, ny - 2 * end) for x in inner]
 
 
 def coefficients(gathered_ref, knudsen_ref, kind_ref, block_ref):
     nx, ny = kind_ref.shape
-    step = LANE // ny
-    chunks = nx // step
+    chunks = nx * ny // LANE
     for i, value in enumerate((knudsen_ref[...], kind_ref[...].astype(F32))):
         for chunk in range(chunks):
-            row = [value[x : x + 1, :] for x in rows_in_chunk(chunk, nx, step)]
+            row = [value[x : x + 1, y : y + n] for x, y, n in pieces_in_chunk(chunk, nx, ny)]
             at = (MOMENTS + i) * chunks + chunk
             block_ref[at : at + 1, :] = jnp.concatenate(row, axis=1)
     total = gathered_ref[0]
@@ -198,11 +202,9 @@
         block_ref[i * chunks : (i + 1) * chunks, :] = value
 
 
-def relaxed_rows(load, nx, ny, lanes, basis_ref, block_ref, out_ref):
-    step = LANE // ny
-    chunks, tail = nx // step, 2 * lanes
-    for chunk in range(chunks):
-        xs = rows_in_chunk(chunk, nx, step)
+def relaxed_rows(load, store, which, chunks, lanes, basis_ref, block_ref):
+    tail = 2 * lanes
+    for chunk in which:
         left = block_ref[pl.ds(chunk, COEFFICIENTS, stride=chunks), :].T.astype(BF16)
         pair = jnp.dot(left, basis_ref[:, tail : tail + 2 * LANE], preferred_element_type=F32)
         keep, scale = pair[:, :LANE], pair[:, LANE:]
@@ -211,13 +213,30 @@
                 left, basis_ref[:, 2 * lane : 2 * lane + 2 * LANE], preferred_element_type=F32
             )
             power, linear = pair[:, :LANE], pair[:, LANE:]
-            value = load(chunk, xs, lane) * keep + (
+            value = load(chunk, lane) * keep + (
                 jnp.exp2(power) * (scale + linear * (power + 2.5 * LOG2E))
             )
-            for half in (0, step // 2):
-                rows = value[half * ny : (half + step // 2) * ny, :]
-                at = xs[half] * ny
-                out_ref[at : at + rows.shape[0], lane : lane + LANE] = rows
+            store(chunk, lane, value)
+
+
+def chunk_rows(state_refs, chunk, nx, ny, lane):
+    def piece(x, y, n):
+        if len(state_refs) == 1:
+            width = min(LANE, state_refs[0].shape[2] - lane)
+            rows = state_refs[0][x, y : y + n, lane : lane + width]
+            if width == LANE:
+                return rows
+            return jnp.concatenate([rows, jnp.zeros((n, LANE - width), F32)], axis=1)
+        inner_ref, low_ref, high_ref = state_refs
+        if x < REACH:
+            ref, at = low_ref, x * ny
+        elif x >= nx - REACH:
+            ref, at = high_ref, (x - nx + REACH) * ny
+        else:
+            ref, at = inner_ref, (x - REACH) * ny
+        return ref[at + y : at + y + n, lane : lane + LANE]
+
+    return jnp.concatenate([piece(*p) for p in pieces_in_chunk(chunk, nx, ny)], axis=0)
 
 
 def limited(left, right):
@@ -255,6 +274,31 @@
             edge_before, face_before = edge, face
 
 
+def alternate(shape, positive):
+    odd = lax.broadcasted_iota(jnp.int32, shape, 1) % 2 == 1
+    return odd if positive else ~odd
+
+
+def pack_layers(near, far, positive, lanes, out_ref):
+    for lane in range(0, lanes, LANE):
+        along = slice(lane, lane + LANE)
+        nearest, second = near(lane), far(lane)
+        ny = nearest.shape[0]
+        first, rest = second[: ny // 2], second[ny // 2 :]
+        out_ref[:ny, along] = nearest
+        out_ref[ny:, along] = jnp.where(
+            alternate(first.shape, positive), first, pltpu.roll(rest, 1, 1)
+        )
+
+
+def unpack_layer(ref, distance, ny, lane):
+    along = slice(lane, lane + LANE)
+    if distance == 0:
+        return ref[:ny, along]
+    packed = ref[ny:, along]
+    return jnp.concatenate([packed, pltpu.roll(packed, LANE - 1, 1)], axis=0)
+
+
 def side_rows(low_ref, high_ref):
     def side(x, lane):
         at, along = slice(x * REACH, (x + 1) * REACH), slice(lane, lane + LANE)
@@ -266,56 +310,67 @@
 
 def first_kernel(state_ref, basis_ref, totals_ref, block_ref):
     nx, ny, velocities = state_ref.shape
-    step = LANE // ny
+    chunks = nx * ny // LANE
     basis = basis_ref[:velocities, :]
-    for chunk in range(nx // step):
-        xs = rows_in_chunk(chunk, nx, step)
-        halves = [state_ref[xs[i] : xs[i] + step // 2] for i in (0, step // 2)]
-        rows = jnp.concatenate(halves, axis=0).reshape(LANE, velocities)
-        blocks_of(moment_sums(rows, basis), chunk, nx // step, block_ref)
-    write_totals(nx // step, block_ref, totals_ref)
+    for chunk in range(chunks):
+        parts = [state_ref[x, y : y + n, :] for x, y, n in pieces_in_chunk(chunk, nx, ny)]
+        blocks_of(moment_sums(jnp.concatenate(parts, axis=0), basis), chunk, chunks, block_ref)
+    write_totals(chunks, block_ref, totals_ref)
 
 
 def relax_kernel(ny, gathered_ref, knudsen_ref, kind_ref, *refs):
     *state_refs, basis_ref, out_ref, low_x_ref, high_x_ref, low_y_ref, high_y_ref, block_ref = refs
     cells, lanes = out_ref.shape
-    nx = cells // ny
+    nx, chunks = cells // ny, cells // LANE
     coefficients(gathered_ref, knudsen_ref, kind_ref, block_ref)
 
-    def load_given(chunk, xs, lane):
-        (state_ref,) = state_refs
-        velocities = state_ref.shape[2]
-        width = min(LANE, velocities - lane)
-        half = len(xs) // 2
-        parts = [state_ref[xs[i] : xs[i] + half, :, lane : lane + width] for i in (0, half)]
-        rows = jnp.concatenate(parts, axis=0).reshape(LANE, width)
-        if width == LANE:
-            return rows
-        return jnp.concatenate([rows, jnp.zeros((LANE, LANE - width), F32)], axis=1)
-
-    def load(chunk, xs, lane):
-        inner_ref, low_ref, high_ref = state_refs
-        along = slice(lane, lane + LANE)
-        if chunk == 0:
-            return jnp.concatenate([low_ref[:, along], high_ref[:, along]], axis=0)
-        return inner_ref[(chunk - 1) * LANE : chunk * LANE, along]
-
-    load = load_given if len(state_refs) == 1 else load
-    relaxed_rows(load, nx, ny, lanes, basis_ref, block_ref, out_ref)
-    low_x_ref[...] = out_ref[: REACH * ny, :]
-    high_x_ref[...] = out_ref[cells - REACH * ny :, :]
+    def load(chunk, lane):
+        return chunk_rows(state_refs, chunk, nx, ny, lane)
+
+    def store(chunk, lane, value):
+        done = 0
+        for x, y, n in pieces_in_chunk(chunk, nx, ny):
+            at = x * ny + y
+            out_ref[at : at + n, lane : lane + LANE] = value[done : done + n, :]
+            done += n
+
+    relaxed_rows(load, store, range(chunks - 1), chunks, lanes, basis_ref, block_ref)
+
+    def row_of(x):
+        return lambda lane: out_ref[x * ny : (x + 1) * ny, lane : lane + LANE]
+
+    pack_layers(row_of(0), row_of(1), False, lanes, low_x_ref)
+    pack_layers(row_of(nx - 1), row_of(nx - 2), True, lanes, high_x_ref)
     for x in range(nx):
         at = slice(x * REACH, (x + 1) * REACH)
         low_y_ref[at, :] = out_ref[x * ny : x * ny + REACH, :]
         high_y_ref[at, :] = out_ref[(x + 1) * ny - REACH : (x + 1) * ny, :]
 
 
-def inner_kernel(ny, velocities, state_ref, low_y_ref, high_y_ref, courant_ref, *refs):
+def inner_kernel(ny, velocities, state_ref, low_y_ref, high_y_ref, courant_ref, coefficient_ref, relax_ref, *refs):
     cells, lanes = state_ref.shape
-    nx = cells // ny
+    nx, chunks = cells // ny, cells // LANE
+    *refs, rest_ref = refs
+    outputs = 3 if velocities is None else 1
+    before_refs, refs = refs[: len(refs) - outputs], refs[len(refs) - outputs :]
+
+    def load_rest(chunk, lane):
+        return chunk_rows(before_refs, chunk, nx, ny, lane)
+
+    def store_rest(chunk, lane, value):
+        rest_ref[:, lane : lane + LANE] = value
+
+    relaxed_rows(load_rest, store_rest, [chunks - 1], chunks, lanes, relax_ref, coefficient_ref)
+    rest = {p[0]: p for p in pieces_in_chunk(chunks - 1, nx, ny)}
+    first = min(rest)
 
     def load(x, lane):
-        return state_ref[x * ny : (x + 1) * ny, lane : lane + LANE]
+        along, at = slice(lane, lane + LANE), x * ny
+        if x not in rest:
+            return state_ref[at : at + ny, along]
+        _, y, n = rest[x]
+        parts = [state_ref[at : at + y, along], rest_ref[(x - first) * n : (x - first + 1) * n, along]]
+        return jnp.concatenate([*parts, state_ref[at + y + n : at + ny, along]], axis=0)
 
     if velocities is None:
         basis_ref, out_ref, block_ref = refs
@@ -334,10 +389,13 @@
     side = side_rows(low_y_ref, high_y_ref)
     transported_rows(load, side, range(REACH, nx - REACH), ny, lanes, courant_ref, write)
     if velocities is None:
-        chunks = cells // LANE
         for chunk in range(1, chunks):
-            rows = out_ref[(chunk - 1) * LANE : chunk * LANE, :]
-            blocks_of(moment_sums(rows, basis_ref[...]), chunk, chunks, block_ref)
+            parts = []
+            for x, y, n in pieces_in_chunk(chunk, nx, ny):
+                at = (x - REACH) * ny + y
+                parts.append(out_ref[at : at + n, :])
+            sums = moment_sums(jnp.concatenate(parts, axis=0), basis_ref[...])
+            blocks_of(sums, chunk, chunks, block_ref)
 
 
 def outer_kernel(ny, high, final, state_ref, side_x_ref, low_y_ref, high_y_ref, courant_ref, *refs):
@@ -347,12 +405,10 @@
 
     def load(x, lane):
         if x < 0:
-            ref, x = side_x_ref, x + REACH
-        elif x >= nx:
-            ref, x = side_x_ref, x - nx
-        else:
-            ref = state_ref
-        return ref[x * ny : (x + 1) * ny, lane : lane + LANE]
+            return unpack_layer(side_x_ref, -1 - x, ny, lane)
+        if x >= nx:
+            return unpack_layer(side_x_ref, x - nx, ny, lane)
+        return state_ref[x * ny : (x + 1) * ny, lane : lane + LANE]
 
     if final:
         _, out_ref, edge_ref, sent = refs
@@ -391,7 +447,7 @@
     write_totals(chunks, block_ref, totals_ref)
 
 
-INNER_COST = pl.CostEstimate(flops=2_000_000_000, bytes_accessed=1000, transcendentals=0)
+INNER_COST = pl.CostEstimate(flops=1_100_000_000, bytes_accessed=1000, transcendentals=0)
 LOW_COST = pl.CostEstimate(flops=1_000_000_000, bytes_accessed=1000, transcendentals=0)
 
 
@@ -429,7 +485,7 @@
     chunks = cells // LANE
     block = pltpu.VMEM((COEFFICIENTS * chunks, LANE), F32)
     totals_shape = rows_of(MOMENTS * chunks, LANE)
-    side_x, side_y = rows_of(REACH * ny, lanes), rows_of(REACH * nx, lanes)
+    edge, side_x, side_y = (rows_of(n, lanes) for n in (REACH * ny, ny + ny // 2, REACH * nx))
 
     moment_basis, relax_basis, courant = call(
         functools.partial(tables_kernel, velocities),
@@ -448,11 +504,13 @@
     state = (distribution,)
     for step in range(STEPS):
         final = step == STEPS - 1
-        relaxed, low_x, high_x, low_y, high_y = call(
+        relaxed, low_x, high_x, low_y, high_y, coefficient = call(
             functools.partial(relax_kernel, ny),
             "relax",
-            (rows_of(cells, lanes), side_x, side_x, side_y, side_y),
-            [block],
+            (
+                rows_of(cells, lanes), side_x, side_x, side_y, side_y,
+                rows_of(COEFFICIENTS * chunks, LANE),
+            ),
         )(gather(totals), local_knudsen, cell_kind, *state, relax_basis)
         up, down = ring("sy")
         from_low_y = lax.ppermute(high_y, "sy", up)
@@ -466,8 +524,9 @@
                 functools.partial(inner_kernel, ny, velocities),
                 "last_inner",
                 rows_of(nx, ny, velocities),
+                [pltpu.VMEM((LANE, lanes), F32)],
                 cost_estimate=INNER_COST,
-            )(relaxed, *sides_y)
+            )(relaxed, *sides_y, coefficient, relax_basis, *state)
             for high, side in enumerate((from_low_x, from_high_x)):
                 out = call(
                     functools.partial(outer_kernel, ny, high, True),
@@ -485,18 +544,19 @@
             functools.partial(inner_kernel, ny, None),
             "inner",
             (rows_of(cells - 2 * REACH * ny, lanes), rows_of(16 * chunks, LANE)),
+            [pltpu.VMEM((LANE, lanes), F32)],
             cost_estimate=INNER_COST,
-        )(relaxed, *sides_y, moment_basis)
+        )(relaxed, *sides_y, coefficient, relax_basis, *state, moment_basis)
         low, low_sums = call(
             functools.partial(outer_kernel, ny, False, False),
             "outer_low",
-            (side_x, rows_of(REACH * ny, LANE)),
+            (edge, rows_of(REACH * ny, LANE)),
             cost_estimate=LOW_COST,
         )(relaxed, from_low_x, *sides_y, moment_basis)
         high, totals = call(
             functools.partial(outer_kernel, ny, True, False),
             "outer_high",
-            (side_x, totals_shape),
+            (edge, totals_shape),
             [pltpu.VMEM((16 * chunks, LANE), F32)],
         )(relaxed, from_high_x, *sides_y, moment_basis, low_sums, inner_block)
         state = (inner, low, high)

time: 81.6 us -> 79.5 us (0.974)
  waiting for transfers between devices: 6 us -> 3.46 us
    ppermute x2, waiting for transfers between devices: 5.65 us -> 3.44 us  [body(): from_high_x = lax.ppermute(low_x, 'sx', down)]
  transfers between devices with their start and end apart: 8 -> 8, of which waited for: 3 -> 2; matrix products, arithmetic and copies ran while one was open for 0% -> 0% of each run, Pallas kernels for 8% -> 10%
where the time goes in v6:
time: 79.5 us; the launch traced here: 79.1 us
  starting transfers between devices  32.5 us (41%)
  blocking collectives  29.4 us (37%)
  Pallas kernels  12 us (15%)
  waiting for transfers between devices  3.46 us (4%)
  local copies, waits for them, and re-layouts  1.59 us (2%)
    all_to_all x2, blocking collectives, gather(): return lax.all_to_all(copies, 'vel', 0, 0)  29.4 us
    ppermute x2, starting transfers between devices, body(): from_high_y = lax.ppermute(low_y, 'sy', down)  10.9 us
    ppermute x2, starting transfers between devices, body(): from_low_y = lax.ppermute(high_y, 'sy', up)  9 us
    ppermute x2, starting transfers between devices, body(): from_low_x = lax.ppermute(high_x, 'sx', up)  8.34 us
    ppermute x2, starting transfers between devices, body(): from_high_x = lax.ppermute(low_x, 'sx', down)  4.28 us
    ppermute x2, waiting for transfers between devices, body(): from_high_x = lax.ppermute(low_x, 'sx', down)  3.44 us
    pallas_call x1, Pallas kernels, body(): call(functools.partial(inner_kernel, ny, velocities), 'last_inner', rows_...  3.31 us
    pallas_call x1, Pallas kernels, body(): call(functools.partial(inner_kernel, ny, None), 'inner', (rows_of(cells -...  2.63 us
  transfers between devices with their start and end apart: 8, of which 2 were waited for; matrix products, arithmetic and copies ran while one was open for 0% of the time, Pallas kernels for 10%

profile of v6, /device:TPU:16, one launch (start us, length us, event | category | flops | bytes accessed | tf_op | source)
XLA Modules:
  0.0 79.1 jit_solution(11116662101031759281)
XLA Ops:
  0.0 0.0 copy-start.2
  0.0 0.3 tables.1
  0.3 0.0 copy-start
  0.3 1.5 %copy-done = f32[16,32,864]{2,1,0:T(8,128)S(1)} copy-done((f32[16,32,864]{2,1,0:T(8,128)S(1)}, f32[16,32,864]{2,1,0:T(8,128)}, u32[]{:S(2)}) %copy-start) | copy-done | bytes 1769496
  1.8 0.0 copy-start.1
  1.8 0.0 copy-start.3
  1.8 0.7 first_moments.1
  2.5 16.2 %all_to_all.10.gathered_ref = f32[16,52,128]{2,1,0:T(8,128)S(1)} all-to-all(f32[16,52,128]{2,1,0:T(8,128)S(1)} %broadcast_in_dim.7), channel_id=1, replica_groups=mesh['sx'=8,'sy'=4,'vel'=16] {'vel'}, dimensions={0} | all-to-all | bytes 851968 | tf_op jit(solution)/shard_map/all_to_all | solution.py:472
  18.7 0.0 copy-done.2
  18.7 0.0 copy-done.1
  18.7 0.0 copy-done.3
  18.7 0.9 %relax.2 = (f32[512,896]{1,0:T(8,128)S(1)}, f32[48,896]{1,0:T(8,128)S(1)}, f32[48,896]{1,0:T(8,128)S(1)}, f32[32,896]{1,0:T(8,128)S(1)}, f32[32,896]{1,0:T(8,128)S(1)}, /*index=5*/f32[128,128]{1,0:T(8,128)S(1)}) custom-call(f32[16,52,128]{2,1,0:T(8,128)S(1)} %all_to_all.10.gathered_ref, f32[16,32]{1,0:T(8,128)S(1)} %copy-done.2, s32[16,32]{1,0:T(8,128)S(1)} %copy-done.3, ...), custom_call_target="tpu_custom_call" | custom-call | tf_op jit(solution)/shard_map/relax/pallas_call | solution.py:507
  19.6 6.1 %collective-permute-start.1 = (f32[32,896]{1,0:T(8,128)S(1)}, f32[32,896]{1,0:T(8,128)S(1)}, u32[]{:S(2)}, u32[]{:S(2)}) collective-permute-start(f32[32,896]{1,0:T(8,128)S(1)} %get-tuple-element.30), channel_id=1, source_target_pairs={{0,16},{16,32},{32,48},{48,0},{1,17},{17,33},{33,49},{49,1},{2,18}... | collective-permute-start | bytes 344072 | tf_op jit(solution)/shard_map/ppermute | solution.py:516
  25.7 5.9 %collective-permute-start.2 = (f32[32,896]{1,0:T(8,128)S(1)}, f32[32,896]{1,0:T(8,128)S(1)}, u32[]{:S(2)}, u32[]{:S(2)}) collective-permute-start(f32[32,896]{1,0:T(8,128)S(1)} %get-tuple-element.31), channel_id=1, source_target_pairs={{16,0},{32,16},{48,32},{0,48},{17,1},{33,17},{49,33},{1,49},{18,2}... | collective-permute-start | bytes 344072 | tf_op jit(solution)/shard_map/ppermute | solution.py:517
  31.6 3.5 %collective-permute-start.3 = (f32[48,896]{1,0:T(8,128)S(1)}, f32[48,896]{1,0:T(8,128)S(1)}, u32[]{:S(2)}, u32[]{:S(2)}) collective-permute-start(f32[48,896]{1,0:T(8,128)S(1)} %get-tuple-element.33), channel_id=1, source_target_pairs={{0,64},{64,128},{128,192},{192,256},{256,320},{320,384},{384,448},... | collective-permute-start | bytes 516104 | tf_op jit(solution)/shard_map/ppermute | solution.py:519
  35.1 2.4 %collective-permute-start = (f32[48,896]{1,0:T(8,128)S(1)}, f32[48,896]{1,0:T(8,128)S(1)}, u32[]{:S(2)}, u32[]{:S(2)}) collective-permute-start(f32[48,896]{1,0:T(8,128)S(1)} %get-tuple-element.29), channel_id=1, source_target_pairs={{64,0},{128,64},{192,128},{256,192},{320,256},{384,320},{448,384},... | collective-permute-start | bytes 516104 | tf_op jit(solution)/shard_map/ppermute | solution.py:520
  37.5 0.0 collective-permute-done.1.low_y_ref
  37.5 0.0 collective-permute-done.2.high_y_ref
  37.5 2.6 %inner.1 = (f32[384,896]{1,0:T(8,128)S(1)}, f32[64,128]{1,0:T(8,128)S(1)}) custom-call(f32[512,896]{1,0:T(8,128)S(1)} %get-tuple-element.28.state_ref, f32[32,896]{1,0:T(8,128)S(1)} %collective-permute-done.1.low_y_ref, f32[32,896]{1,0:T(8,128)S(1)} %collective-permute-done.2.high_y_ref, f32[8,896]{1,0:T(8,128)S(1)} %get-tuple-element.32.courant_ref, ...), custom_call_target="tpu_custom_call" | custom-call | flops 1100000000 | bytes 1000 | tf_op jit(solution)/shard_map/inner/pallas_call | solution.py:543
  40.1 0.0 collective-permute-done.3.side_x_ref
  40.1 0.6 outer_low.1
  40.7 2.5 %collective-permute-done.side_x_ref = f32[48,896]{1,0:T(8,128)S(1)} collective-permute-done((f32[48,896]{1,0:T(8,128)S(1)}, f32[48,896]{1,0:T(8,128)S(1)}, u32[]{:S(2)}, u32[]{:S(2)}) %collective-permute-start) | collective-permute-done | bytes 172064 | tf_op jit(solution)/shard_map/ppermute | solution.py:520
  43.2 0.6 outer_high.1
  43.8 13.2 %all_to_all.11.gathered_ref = f32[16,52,128]{2,1,0:T(8,128)S(1)} all-to-all(f32[16,52,128]{2,1,0:T(8,128)S(1)} %broadcast_in_dim.8), channel_id=1, replica_groups=mesh['sx'=8,'sy'=4,'vel'=16] {'vel'}, dimensions={0} | all-to-all | bytes 851968 | tf_op jit(solution)/shard_map/all_to_all | solution.py:472
  57.0 0.9 %relax.3 = (f32[512,896]{1,0:T(8,128)S(1)}, f32[48,896]{1,0:T(8,128)S(1)}, f32[48,896]{1,0:T(8,128)S(1)}, f32[32,896]{1,0:T(8,128)S(1)}, f32[32,896]{1,0:T(8,128)S(1)}, /*index=5*/f32[128,128]{1,0:T(8,128)S(1)}) custom-call(f32[16,52,128]{2,1,0:T(8,128)S(1)} %all_to_all.11.gathered_ref, f32[16,32]{1,0:T(8,128)S(1)} %copy-done.2, s32[16,32]{1,0:T(8,128)S(1)} %copy-done.3, ...), custom_call_target="tpu_custom_call" | custom-call | tf_op jit(solution)/shard_map/relax/pallas_call | solution.py:507
  57.9 2.9 %collective-permute-start.5 = (f32[32,896]{1,0:T(8,128)S(1)}, f32[32,896]{1,0:T(8,128)S(1)}, u32[]{:S(2)}, u32[]{:S(2)}) collective-permute-start(f32[32,896]{1,0:T(8,128)S(1)} %get-tuple-element.43), channel_id=1, source_target_pairs={{0,16},{16,32},{32,48},{48,0},{1,17},{17,33},{33,49},{49,1},{2,18}... | collective-permute-start | bytes 344072 | tf_op jit(solution)/shard_map/ppermute | solution.py:516
  60.9 5.0 %collective-permute-start.6 = (f32[32,896]{1,0:T(8,128)S(1)}, f32[32,896]{1,0:T(8,128)S(1)}, u32[]{:S(2)}, u32[]{:S(2)}) collective-permute-start(f32[32,896]{1,0:T(8,128)S(1)} %get-tuple-element.44), channel_id=1, source_target_pairs={{16,0},{32,16},{48,32},{0,48},{17,1},{33,17},{49,33},{1,49},{18,2}... | collective-permute-start | bytes 344072 | tf_op jit(solution)/shard_map/ppermute | solution.py:517
  65.9 4.9 %collective-permute-start.7 = (f32[48,896]{1,0:T(8,128)S(1)}, f32[48,896]{1,0:T(8,128)S(1)}, u32[]{:S(2)}, u32[]{:S(2)}) collective-permute-start(f32[48,896]{1,0:T(8,128)S(1)} %get-tuple-element.45), channel_id=1, source_target_pairs={{0,64},{64,128},{128,192},{192,256},{256,320},{320,384},{384,448},... | collective-permute-start | bytes 516104 | tf_op jit(solution)/shard_map/ppermute | solution.py:519
  70.8 1.9 %collective-permute-start.4 = (f32[48,896]{1,0:T(8,128)S(1)}, f32[48,896]{1,0:T(8,128)S(1)}, u32[]{:S(2)}, u32[]{:S(2)}) collective-permute-start(f32[48,896]{1,0:T(8,128)S(1)} %get-tuple-element.42), channel_id=1, source_target_pairs={{64,0},{128,64},{192,128},{256,192},{320,256},{384,320},{448,384},... | collective-permute-start | bytes 516104 | tf_op jit(solution)/shard_map/ppermute | solution.py:520
  72.7 0.0 collective-permute-done.5.low_y_ref
  72.7 0.0 collective-permute-done.6.high_y_ref
  72.7 3.3 %last_inner.1.refs_0_ = f32[16,32,864]{2,1,0:T(8,128)} custom-call(f32[512,896]{1,0:T(8,128)S(1)} %get-tuple-element.41.state_ref, f32[32,896]{1,0:T(8,128)S(1)} %collective-permute-done.5.low_y_ref, f32[32,896]{1,0:T(8,128)S(1)} %collective-permute-done.6.high_y_ref, f32[8,896]{1,0:T(8,128)S(1)} %get-tuple-element.32.courant_ref, ...), custom_call_target="tpu_custom_call" | custom-call | flops 1100000000 | bytes 1000 | tf_op jit(solution)/shard_map/last_inner/pallas_call | solution.py:523
  76.0 0.0 collective-permute-done.7.side_x_ref
  76.0 1.0 %last_low.1.refs_0_ = f32[16,32,864]{2,1,0:T(8,128)} custom-call(f32[512,896]{1,0:T(8,128)S(1)} %get-tuple-element.41.state_ref, f32[48,896]{1,0:T(8,128)S(1)} %collective-permute-done.7.side_x_ref, f32[32,896]{1,0:T(8,128)S(1)} %collective-permute-done.5.low_y_ref, f32[32,896]{1,0:T(8,128)S(1)} %collective-permute-done.6.high_y_ref, ...), custom_call_target="tpu_custom_call", output_to_operand_aliasing={{}: (5, {})} | custom-call | flops 1000000000 | bytes 1000 | tf_op jit(solution)/shard_map/last_low/pallas_call | solution.py:531
  77.1 1.0 %collective-permute-done.4.side_x_ref = f32[48,896]{1,0:T(8,128)S(1)} collective-permute-done((f32[48,896]{1,0:T(8,128)S(1)}, f32[48,896]{1,0:T(8,128)S(1)}, u32[]{:S(2)}, u32[]{:S(2)}) %collective-permute-start.4) | collective-permute-done | bytes 172064 | tf_op jit(solution)/shard_map/ppermute | solution.py:520
  78.1 1.0 %last_high.1 = f32[16,32,864]{2,1,0:T(8,128)} custom-call(f32[512,896]{1,0:T(8,128)S(1)} %get-tuple-element.41.state_ref, f32[48,896]{1,0:T(8,128)S(1)} %collective-permute-done.4.side_x_ref, f32[32,896]{1,0:T(8,128)S(1)} %collective-permute-done.5.low_y_ref, f32[32,896]{1,0:T(8,128)S(1)} %collective-permute-done.6.high_y_ref, ...), custom_call_target="tpu_custom_call", output_to_operand_aliasing={{}: (5, {})} | custom-call | tf_op jit(solution)/shard_map/last_high/pallas_call | solution.py:531
  (2 shorter events, 0.1 us)
Async XLA Ops:
  0.0 18.7 %copy-start.2 = (f32[16,32]{1,0:T(8,128)S(1)}, f32[16,32]{1,0:T(8,128)}, u32[]{:S(2)}) copy-start(f32[16,32]{1,0:T(8,128)} %knudsen_ref.3) | copy-start | bytes 6148
  0.3 1.5 %copy-start = (f32[16,32,864]{2,1,0:T(8,128)S(1)}, f32[16,32,864]{2,1,0:T(8,128)}, u32[]{:S(2)}) copy-start(f32[16,32,864]{2,1,0:T(8,128)} %refs_0_.3) | copy-start | bytes 5308420
  1.8 16.9 %copy-start.1 = (f32[16,32,864]{2,1,0:T(8,128)S(1)}, f32[16,32,864]{2,1,0:T(8,128)}, u32[]{:S(2)}) copy-start(f32[16,32,864]{2,1,0:T(8,128)} %refs_0_.3) | copy-start | bytes 5308420
  1.8 16.9 %copy-start.3 = (s32[16,32]{1,0:T(8,128)S(1)}, s32[16,32]{1,0:T(8,128)}, u32[]{:S(2)}) copy-start(s32[16,32]{1,0:T(8,128)} %kind_ref.3) | copy-start | bytes 6148
  19.6 17.8 %collective-permute-start.1 = (f32[32,896]{1,0:T(8,128)S(1)}, f32[32,896]{1,0:T(8,128)S(1)}, u32[]{:S(2)}, u32[]{:S(2)}) collective-permute-start(f32[32,896]{1,0:T(8,128)S(1)} %get-tuple-element.30), channel_id=1, source_target_pairs={{0,16},{16,32},{32,48},{48,0},{1,17},{17,33},{33,49},{49,1},{2,18}... | collective-permute-start | bytes 344072 | tf_op jit(solution)/shard_map/ppermute | solution.py:516
  25.7 11.8 %collective-permute-start.2 = (f32[32,896]{1,0:T(8,128)S(1)}, f32[32,896]{1,0:T(8,128)S(1)}, u32[]{:S(2)}, u32[]{:S(2)}) collective-permute-start(f32[32,896]{1,0:T(8,128)S(1)} %get-tuple-element.31), channel_id=1, source_target_pairs={{16,0},{32,16},{48,32},{0,48},{17,1},{33,17},{49,33},{1,49},{18,2}... | collective-permute-start | bytes 344072 | tf_op jit(solution)/shard_map/ppermute | solution.py:517
  31.6 8.5 %collective-permute-start.3 = (f32[48,896]{1,0:T(8,128)S(1)}, f32[48,896]{1,0:T(8,128)S(1)}, u32[]{:S(2)}, u32[]{:S(2)}) collective-permute-start(f32[48,896]{1,0:T(8,128)S(1)} %get-tuple-element.33), channel_id=1, source_target_pairs={{0,64},{64,128},{128,192},{192,256},{256,320},{320,384},{384,448},... | collective-permute-start | bytes 516104 | tf_op jit(solution)/shard_map/ppermute | solution.py:519
  35.1 8.1 %collective-permute-start = (f32[48,896]{1,0:T(8,128)S(1)}, f32[48,896]{1,0:T(8,128)S(1)}, u32[]{:S(2)}, u32[]{:S(2)}) collective-permute-start(f32[48,896]{1,0:T(8,128)S(1)} %get-tuple-element.29), channel_id=1, source_target_pairs={{64,0},{128,64},{192,128},{256,192},{320,256},{384,320},{448,384},... | collective-permute-start | bytes 516104 | tf_op jit(solution)/shard_map/ppermute | solution.py:520
  57.9 14.8 %collective-permute-start.5 = (f32[32,896]{1,0:T(8,128)S(1)}, f32[32,896]{1,0:T(8,128)S(1)}, u32[]{:S(2)}, u32[]{:S(2)}) collective-permute-start(f32[32,896]{1,0:T(8,128)S(1)} %get-tuple-element.43), channel_id=1, source_target_pairs={{0,16},{16,32},{32,48},{48,0},{1,17},{17,33},{33,49},{49,1},{2,18}... | collective-permute-start | bytes 344072 | tf_op jit(solution)/shard_map/ppermute | solution.py:516
  60.9 11.8 %collective-permute-start.6 = (f32[32,896]{1,0:T(8,128)S(1)}, f32[32,896]{1,0:T(8,128)S(1)}, u32[]{:S(2)}, u32[]{:S(2)}) collective-permute-start(f32[32,896]{1,0:T(8,128)S(1)} %get-tuple-element.44), channel_id=1, source_target_pairs={{16,0},{32,16},{48,32},{0,48},{17,1},{33,17},{49,33},{1,49},{18,2}... | collective-permute-start | bytes 344072 | tf_op jit(solution)/shard_map/ppermute | solution.py:517
  65.9 10.1 %collective-permute-start.7 = (f32[48,896]{1,0:T(8,128)S(1)}, f32[48,896]{1,0:T(8,128)S(1)}, u32[]{:S(2)}, u32[]{:S(2)}) collective-permute-start(f32[48,896]{1,0:T(8,128)S(1)} %get-tuple-element.45), channel_id=1, source_target_pairs={{0,64},{64,128},{128,192},{192,256},{256,320},{320,384},{384,448},... | collective-permute-start | bytes 516104 | tf_op jit(solution)/shard_map/ppermute | solution.py:519
  70.8 7.3 %collective-permute-start.4 = (f32[48,896]{1,0:T(8,128)S(1)}, f32[48,896]{1,0:T(8,128)S(1)}, u32[]{:S(2)}, u32[]{:S(2)}) collective-permute-start(f32[48,896]{1,0:T(8,128)S(1)} %get-tuple-element.42), channel_id=1, source_target_pairs={{64,0},{128,64},{192,128},{256,192},{320,256},{384,320},{448,384},... | collective-permute-start | bytes 516104 | tf_op jit(solution)/shard_map/ppermute | solution.py:520

commit v7 on v6

--- a/solution.py
+++ b/solution.py
@@ -227,11 +227,11 @@
             if width == LANE:
                 return rows
             return jnp.concatenate([rows, jnp.zeros((n, LANE - width), F32)], axis=1)
-        inner_ref, low_ref, high_ref = state_refs
+        inner_ref, edges_ref = state_refs
         if x < REACH:
-            ref, at = low_ref, x * ny
+            ref, at = edges_ref, x * ny
         elif x >= nx - REACH:
-            ref, at = high_ref, (x - nx + REACH) * ny
+            ref, at = edges_ref, (x - nx + 2 * REACH) * ny
         else:
             ref, at = inner_ref, (x - REACH) * ny
         return ref[at + y : at + y + n, lane : lane + LANE]
@@ -273,7 +273,6 @@
             slope_before = slope_after
             edge_before, face_before = edge, face
 
-
 def alternate(shape, positive):
     odd = lax.broadcasted_iota(jnp.int32, shape, 1) % 2 == 1
     return odd if positive else ~odd
@@ -299,11 +298,53 @@
     return jnp.concatenate([packed, pltpu.roll(packed, LANE - 1, 1)], axis=0)
 
 
-def side_rows(low_ref, high_ref):
+def run_alternate(shape, lane, positive):
+    odd = (lax.broadcasted_iota(jnp.int32, shape, 1) + lane) // NVX % 2 == 1
+    return odd if positive else ~odd
+
+
+def pack_ends(state_ref, near, far, ny, positive, out_ref, far_ref):
+    nx, lanes = far_ref.shape
+    for x in range(nx):
+        out_ref[x : x + 1, :] = state_ref[x * ny + near : x * ny + near + 1, :]
+        far_ref[x : x + 1, :] = state_ref[x * ny + far : x * ny + far + 1, :]
+    before = None
+    for lane in range(0, lanes, LANE):
+        along = slice(lane, lane + LANE)
+        second = far_ref[:, along]
+        half = nx // 2
+        turned = pltpu.roll(second[half:], NVX, 1)
+        moved = turned
+        if before is not None:
+            crossed = lax.broadcasted_iota(jnp.int32, turned.shape, 1) < NVX
+            moved = jnp.where(crossed, before, turned)
+        before = turned
+        own = run_alternate(turned.shape, lane, positive)
+        out_ref[nx:, along] = jnp.where(own, second[:half], moved)
+
+
+def unpack_ends(ref, near_at, far_at, side_ref):
+    rows, lanes = ref.shape
+    half = rows // 3
+    after = None
+    for lane in range(lanes - LANE, -1, -LANE):
+        along = slice(lane, lane + LANE)
+        block = lane // LANE
+        side_ref[block, pl.ds(near_at, 2 * half, stride=SUBLANE), :] = ref[: 2 * half, along]
+        packed = ref[2 * half :, along]
+        turned = pltpu.roll(packed, LANE - NVX, 1)
+        moved = turned
+        if after is not None:
+            crossed = lax.broadcasted_iota(jnp.int32, turned.shape, 1) >= LANE - NVX
+            moved = jnp.where(crossed, after, turned)
+        after = turned
+        both = jnp.concatenate([packed, moved], axis=0)
+        side_ref[block, pl.ds(far_at, 2 * half, stride=SUBLANE), :] = both
+
+
+def side_rows(side_ref):
     def side(x, lane):
-        at, along = slice(x * REACH, (x + 1) * REACH), slice(lane, lane + LANE)
-        gap = jnp.zeros((SUBLANE - 2 * REACH, LANE), F32)
-        return jnp.concatenate([high_ref[at, along], gap, low_ref[at, along]], axis=0)
+        return side_ref[lane // LANE, x * SUBLANE : (x + 1) * SUBLANE, :]
 
     return side
 
@@ -318,8 +359,19 @@
     write_totals(chunks, block_ref, totals_ref)
 
 
-def relax_kernel(ny, gathered_ref, knudsen_ref, kind_ref, *refs):
-    *state_refs, basis_ref, out_ref, low_x_ref, high_x_ref, low_y_ref, high_y_ref, block_ref = refs
+def by_parity(odd_ref, do, first_ref, second_ref):
+    @pl.when(odd_ref[0] == 0)
+    def _():
+        do(second_ref, first_ref)
+
+    @pl.when(odd_ref[0] != 0)
+    def _():
+        do(first_ref, second_ref)
+
+
+def relax_kernel(ny, odd_x_ref, odd_y_ref, gathered_ref, knudsen_ref, kind_ref, *refs):
+    *state_refs, basis_ref, out_ref, first_x_ref, second_x_ref, first_y_ref, second_y_ref = refs[:-2]
+    block_ref, far_ref = refs[-2:]
     cells, lanes = out_ref.shape
     nx, chunks = cells // ny, cells // LANE
     coefficients(gathered_ref, knudsen_ref, kind_ref, block_ref)
@@ -336,22 +388,31 @@
 
     relaxed_rows(load, store, range(chunks - 1), chunks, lanes, basis_ref, block_ref)
 
+
     def row_of(x):
         return lambda lane: out_ref[x * ny : (x + 1) * ny, lane : lane + LANE]
 
-    pack_layers(row_of(0), row_of(1), False, lanes, low_x_ref)
-    pack_layers(row_of(nx - 1), row_of(nx - 2), True, lanes, high_x_ref)
-    for x in range(nx):
-        at = slice(x * REACH, (x + 1) * REACH)
-        low_y_ref[at, :] = out_ref[x * ny : x * ny + REACH, :]
-        high_y_ref[at, :] = out_ref[(x + 1) * ny - REACH : (x + 1) * ny, :]
-
-
-def inner_kernel(ny, velocities, state_ref, low_y_ref, high_y_ref, courant_ref, coefficient_ref, relax_ref, *refs):
+    def pack_x(low_ref, high_ref):
+        pack_layers(row_of(0), row_of(1), False, lanes, low_ref)
+        pack_layers(row_of(nx - 1), row_of(nx - 2), True, lanes, high_ref)
+
+    def pack_y(low_ref, high_ref):
+        pack_ends(out_ref, 0, 1, ny, False, low_ref, far_ref)
+        pack_ends(out_ref, ny - 1, ny - 2, ny, True, high_ref, far_ref)
+
+    by_parity(odd_x_ref, pack_x, first_x_ref, second_x_ref)
+    by_parity(odd_y_ref, pack_y, first_y_ref, second_y_ref)
+
+
+def inner_kernel(ny, velocities, odd_y_ref, state_ref, first_y_ref, second_y_ref, courant_ref, coefficient_ref, relax_ref, *refs):
     cells, lanes = state_ref.shape
     nx, chunks = cells // ny, cells // LANE
-    *refs, rest_ref = refs
-    outputs = 3 if velocities is None else 1
+    if velocities is None:
+        *refs, side_ref, rest_ref = refs
+        outputs = 3
+    else:
+        *refs, side_ref, rest_ref, stage_ref, sent = refs
+        outputs = 1
     before_refs, refs = refs[: len(refs) - outputs], refs[len(refs) - outputs :]
 
     def load_rest(chunk, lane):
@@ -372,6 +433,14 @@
         parts = [state_ref[at : at + y, along], rest_ref[(x - first) * n : (x - first + 1) * n, along]]
         return jnp.concatenate([*parts, state_ref[at + y + n : at + ny, along]], axis=0)
 
+    side_ref[...] = jnp.zeros_like(side_ref)
+
+    def unpack_y(low_ref, high_ref):
+        unpack_ends(high_ref, 0, 1, side_ref)
+        unpack_ends(low_ref, SUBLANE - 1, SUBLANE - 2, side_ref)
+
+    by_parity(odd_y_ref, unpack_y, first_y_ref, second_y_ref)
+    copies = []
     if velocities is None:
         basis_ref, out_ref, block_ref = refs
 
@@ -379,15 +448,28 @@
             at = (x - REACH) * ny
             out_ref[at : at + ny, lane : lane + LANE] = value
 
+        groups = 1
     else:
         (out_ref,) = refs
+        groups = sent.shape[0]
 
         def write(x, lane, value):
             width = min(LANE, velocities - lane)
-            out_ref[x, :, lane : lane + width] = value[:, :width]
-
-    side = side_rows(low_y_ref, high_y_ref)
-    transported_rows(load, side, range(REACH, nx - REACH), ny, lanes, courant_ref, write)
+            stage_ref[x - REACH, :, lane : lane + width] = value[:, :width]
+
+    count = (nx - 2 * REACH) // groups
+    for group in range(groups):
+        start = REACH + group * count
+        xs = range(start, start + count)
+        transported_rows(load, side_rows(side_ref), xs, ny, lanes, courant_ref, write)
+        if velocities is not None:
+            part = stage_ref.at[start - REACH : start - REACH + count]
+            copies.append(
+                pltpu.make_async_copy(part, out_ref.at[start : start + count], sent.at[group])
+            )
+            copies[-1].start()
+    for copy in copies:
+        copy.wait()
     if velocities is None:
         for chunk in range(1, chunks):
             parts = []
@@ -398,10 +480,11 @@
             blocks_of(sums, chunk, chunks, block_ref)
 
 
-def outer_kernel(ny, high, final, state_ref, side_x_ref, low_y_ref, high_y_ref, courant_ref, *refs):
+def outer_kernel(ny, second, final, odd_x_ref, state_ref, side_x_ref, side_ref, courant_ref, *refs):
     cells, lanes = state_ref.shape
-    nx = cells // ny
-    first = nx - REACH if high else 0
+    nx, edge = cells // ny, REACH * ny
+    odd = odd_x_ref[0] != 0
+    high = odd if second else ~odd
 
     def load(x, lane):
         if x < 0:
@@ -410,40 +493,66 @@
             return unpack_layer(side_x_ref, x - nx, ny, lane)
         return state_ref[x * ny : (x + 1) * ny, lane : lane + LANE]
 
+    def transport(write):
+        for start, chosen in ((0, ~high), (nx - REACH, high)):
+
+            @pl.when(chosen)
+            def _(start=start):
+                def write_row(x, lane, value):
+                    write(x - start, lane, value)
+
+                xs = range(start, start + REACH)
+                transported_rows(load, side_rows(side_ref), xs, ny, lanes, courant_ref, write_row)
+
     if final:
-        _, out_ref, edge_ref, sent = refs
+        if second:
+            other_ref, _, out_ref, edge_ref, sent = refs
+            own_at = jnp.where(high, nx - REACH, 0)
+            other_at = jnp.where(high, 0, nx - REACH)
+            other_copy = pltpu.make_async_copy(
+                other_ref, out_ref.at[pl.ds(other_at, REACH)], sent.at[0]
+            )
+            other_copy.start()
+        else:
+            (edge_ref,) = refs
 
         def write(x, lane, value):
-            width = min(LANE, out_ref.shape[2] - lane)
-            edge_ref[x - first, :, lane : lane + width] = value[:, :width]
-
+            width = min(LANE, edge_ref.shape[2] - lane)
+            edge_ref[x, :, lane : lane + width] = value[:, :width]
+
+        transport(write)
+        if second:
+            copy = pltpu.make_async_copy(
+                edge_ref, out_ref.at[pl.ds(own_at, REACH)], sent.at[1]
+            )
+            copy.start()
+            other_copy.wait()
+            copy.wait()
+        return
+
+    basis_ref, *refs = refs
+    if second:
+        other_ref, other_sums_ref, inner_block_ref, edges_ref, totals_ref, own_ref, sums_ref, block_ref = refs
     else:
-        basis_ref, *refs = refs
-        if high:
-            low_sums_ref, inner_block_ref, out_ref, totals_ref, block_ref = refs
-        else:
-            out_ref, sums_ref = refs
-
-        def write(x, lane, value):
-            at = (x - first) * ny
-            out_ref[at : at + ny, lane : lane + LANE] = value
-
-    side = side_rows(low_y_ref, high_y_ref)
-    xs = range(first, first + REACH)
-    transported_rows(load, side, xs, ny, lanes, courant_ref, write)
-    if final:
-        copy = pltpu.make_async_copy(edge_ref, out_ref.at[first : first + REACH], sent)
-        copy.start()
-        copy.wait()
+        own_ref, own_sums_ref = refs
+
+    def write(x, lane, value):
+        own_ref[x * ny : (x + 1) * ny, lane : lane + LANE] = value
+
+    transport(write)
+    own_sums = moment_sums(own_ref[...], basis_ref[...])
+    if not second:
+        own_sums_ref[...] = own_sums
         return
-    sums = moment_sums(out_ref[...], basis_ref[...])
-    if not high:
-        sums_ref[...] = sums
-        return
+    own_at = pl.multiple_of(jnp.where(high, edge, 0), edge)
+    other_at = pl.multiple_of(jnp.where(high, 0, edge), edge)
+    edges_ref[pl.ds(own_at, edge), :] = own_ref[...]
+    edges_ref[pl.ds(other_at, edge), :] = other_ref[...]
+    sums_ref[pl.ds(own_at, edge), :] = own_sums
+    sums_ref[pl.ds(other_at, edge), :] = other_sums_ref[...]
     chunks = cells // LANE
     block_ref[...] = inner_block_ref[...]
-    sums = jnp.concatenate([low_sums_ref[...], sums], axis=0)
-    blocks_of(sums, 0, chunks, block_ref)
+    blocks_of(sums_ref[...], 0, chunks, block_ref)
     write_totals(chunks, block_ref, totals_ref)
 
 
@@ -472,10 +581,13 @@
     return lax.all_to_all(copies, "vel", 0, 0)
 
 
-def ring(axis):
+def partners(axis):
     devices = lax.axis_size(axis)
-    up = [(i, (i + 1) % devices) for i in range(devices)]
-    return up, [(j, i) for i, j in up]
+    pairs = []
+    for first in (0, 1):
+        couples = [((i + first) % devices, (i + first + 1) % devices) for i in range(0, devices, 2)]
+        pairs.append(couples + [(b, a) for a, b in couples])
+    return pairs
 
 
 def body(distribution, cell_kind, local_knudsen):
@@ -485,8 +597,18 @@
     chunks = cells // LANE
     block = pltpu.VMEM((COEFFICIENTS * chunks, LANE), F32)
     totals_shape = rows_of(MOMENTS * chunks, LANE)
-    edge, side_x, side_y = (rows_of(n, lanes) for n in (REACH * ny, ny + ny // 2, REACH * nx))
-
+    edge, side_x, side_y = (rows_of(n, lanes) for n in (REACH * ny, ny + ny // 2, nx + nx // 2))
+
+    first, odd_x, odd_y = lax.optimization_barrier(
+        tuple(
+            jnp.full((1,), value, jnp.int32)
+            for value in (
+                lax.axis_index("vel") * velocities,
+                lax.axis_index("sx") % 2,
+                lax.axis_index("sy") % 2,
+            )
+        )
+    )
     moment_basis, relax_basis, courant = call(
         functools.partial(tables_kernel, velocities),
         "tables",
@@ -497,69 +619,93 @@
         ),
         [pltpu.VMEM((LANE, lanes), F32)],
         in_specs=[pl.BlockSpec(memory_space=pltpu.SMEM)],
-    )(jnp.full((1,), lax.axis_index("vel") * velocities, jnp.int32))
+    )(first)
     totals = call(first_kernel, "first_moments", totals_shape, [block])(
         distribution, moment_basis
     )
     state = (distribution,)
     for step in range(STEPS):
         final = step == STEPS - 1
-        relaxed, low_x, high_x, low_y, high_y, coefficient = call(
+        smem, vmem, hbm = (
+            pl.BlockSpec(memory_space=m) for m in (pltpu.SMEM, pltpu.VMEM, pltpu.HBM)
+        )
+        operands = (gather(totals), local_knudsen, cell_kind, *state, relax_basis)
+        relaxed, first_x, second_x, first_y, second_y, coefficient = call(
             functools.partial(relax_kernel, ny),
             "relax",
             (
                 rows_of(cells, lanes), side_x, side_x, side_y, side_y,
                 rows_of(COEFFICIENTS * chunks, LANE),
             ),
-        )(gather(totals), local_knudsen, cell_kind, *state, relax_basis)
-        up, down = ring("sy")
-        from_low_y = lax.ppermute(high_y, "sy", up)
-        from_high_y = lax.ppermute(low_y, "sy", down)
-        up, down = ring("sx")
-        from_low_x = lax.ppermute(high_x, "sx", up)
-        from_high_x = lax.ppermute(low_x, "sx", down)
-        sides_y = (from_low_y, from_high_y, courant)
+            [pltpu.VMEM((nx, lanes), F32)],
+            in_specs=[smem, smem] + [vmem] * len(operands),
+        )(odd_x, odd_y, *operands)
+        to_first, to_second = partners("sy")
+        sides_y = (lax.ppermute(first_y, "sy", to_first), lax.ppermute(second_y, "sy", to_second))
+        to_first, to_second = partners("sx")
+        first_x = lax.ppermute(first_x, "sx", to_first)
+        second_x = lax.ppermute(second_x, "sx", to_second)
+        side_shape = rows_of(lanes // LANE, nx * SUBLANE, LANE)
+        rest = pltpu.VMEM((LANE, lanes), F32)
+        operands = (relaxed, *sides_y, courant, coefficient, relax_basis, *state)
         if final:
-            out = call(
+            inner, side = call(
                 functools.partial(inner_kernel, ny, velocities),
                 "last_inner",
+                (rows_of(nx, ny, velocities), side_shape),
+                [
+                    rest,
+                    pltpu.VMEM((nx - 2 * REACH, ny, velocities), F32),
+                    pltpu.SemaphoreType.DMA((3,)),
+                ],
+                in_specs=[smem] + [vmem] * len(operands),
+                out_specs=(hbm, vmem),
+                cost_estimate=INNER_COST,
+            )(odd_y, *operands)
+            ends = rows_of(REACH, ny, velocities)
+            other = call(
+                functools.partial(outer_kernel, ny, False, True),
+                "last_first",
+                ends,
+                in_specs=[smem] + [vmem] * 4,
+                cost_estimate=LOW_COST,
+            )(odd_x, relaxed, first_x, side, courant)
+            return call(
+                functools.partial(outer_kernel, ny, True, True),
+                "last_second",
                 rows_of(nx, ny, velocities),
-                [pltpu.VMEM((LANE, lanes), F32)],
-                cost_estimate=INNER_COST,
-            )(relaxed, *sides_y, coefficient, relax_basis, *state)
-            for high, side in enumerate((from_low_x, from_high_x)):
-                out = call(
-                    functools.partial(outer_kernel, ny, high, True),
-                    "last_high" if high else "last_low",
-                    rows_of(nx, ny, velocities),
-                    [pltpu.VMEM((REACH, ny, velocities), F32), pltpu.SemaphoreType.DMA],
-                    in_specs=[pl.BlockSpec(memory_space=pltpu.VMEM)] * 5
-                    + [pl.BlockSpec(memory_space=pltpu.HBM)],
-                    out_specs=pl.BlockSpec(memory_space=pltpu.HBM),
-                    input_output_aliases={5: 0},
-                    cost_estimate=None if high else LOW_COST,
-                )(relaxed, side, *sides_y, out)
-            return out
-        inner, inner_block = call(
+                [pltpu.VMEM(ends.shape, F32), pltpu.SemaphoreType.DMA((2,))],
+                in_specs=[smem] + [vmem] * 5 + [hbm],
+                out_specs=hbm,
+                input_output_aliases={6: 0},
+            )(odd_x, relaxed, second_x, side, courant, other, inner)
+        inner, inner_block, side = call(
             functools.partial(inner_kernel, ny, None),
             "inner",
-            (rows_of(cells - 2 * REACH * ny, lanes), rows_of(16 * chunks, LANE)),
-            [pltpu.VMEM((LANE, lanes), F32)],
+            (rows_of(cells - 2 * REACH * ny, lanes), rows_of(16 * chunks, LANE), side_shape),
+            [rest],
+            in_specs=[smem] + [vmem] * (len(operands) + 1),
             cost_estimate=INNER_COST,
-        )(relaxed, *sides_y, coefficient, relax_basis, *state, moment_basis)
-        low, low_sums = call(
+        )(odd_y, *operands, moment_basis)
+        other, other_sums = call(
             functools.partial(outer_kernel, ny, False, False),
-            "outer_low",
+            "outer_first",
             (edge, rows_of(REACH * ny, LANE)),
+            in_specs=[smem] + [vmem] * 5,
             cost_estimate=LOW_COST,
-        )(relaxed, from_low_x, *sides_y, moment_basis)
-        high, totals = call(
+        )(odd_x, relaxed, first_x, side, courant, moment_basis)
+        edges, totals = call(
             functools.partial(outer_kernel, ny, True, False),
-            "outer_high",
-            (edge, totals_shape),
-            [pltpu.VMEM((16 * chunks, LANE), F32)],
-        )(relaxed, from_high_x, *sides_y, moment_basis, low_sums, inner_block)
-        state = (inner, low, high)
+            "outer_second",
+            (rows_of(2 * REACH * ny, lanes), totals_shape),
+            [
+                pltpu.VMEM((REACH * ny, lanes), F32),
+                pltpu.VMEM((2 * REACH * ny, LANE), F32),
+                pltpu.VMEM((16 * chunks, LANE), F32),
+            ],
+            in_specs=[smem] + [vmem] * 8,
+        )(odd_x, relaxed, second_x, side, courant, moment_basis, other, other_sums, inner_block)
+        state = (inner, edges)
 
 
 def solution(mesh):

time: 79.5 us -> 77.3 us (0.972)
  the two profiles are of different devices: /device:TPU:16 before, /device:TPU:56 now
where the time goes in v7:
time: 77.3 us; the launch traced here: 76.9 us
  blocking collectives  28.9 us (37%)
  starting transfers between devices  28.5 us (37%)
  Pallas kernels  11.2 us (14%)
  waiting for transfers between devices  6.46 us (8%)
  local copies, waits for them, and re-layouts  1.6 us (2%)
    all_to_all x2, blocking collectives, gather(): return lax.all_to_all(copies, 'vel', 0, 0)  28.9 us
    ppermute x2, starting transfers between devices, body(): lax.ppermute(first_y, 'sy', to_first)  10.4 us
    ppermute x2, starting transfers between devices, body(): lax.ppermute(second_y, 'sy', to_second)  8.49 us
    ppermute x2, starting transfers between devices, body(): first_x = lax.ppermute(first_x, 'sx', to_first)  5.78 us
    ppermute x2, waiting for transfers between devices, body(): second_x = lax.ppermute(second_x, 'sx', to_second)  4.53 us
    ppermute x2, starting transfers between devices, body(): second_x = lax.ppermute(second_x, 'sx', to_second)  3.84 us
    pallas_call x1, Pallas kernels, body(): call(functools.partial(inner_kernel, ny, velocities), 'last_inner', (rows...  3.03 us
    pallas_call x1, Pallas kernels, body(): call(functools.partial(inner_kernel, ny, None), 'inner', (rows_of(cells -...  2.68 us
  transfers between devices with their start and end apart: 8, of which 3 were waited for; matrix products, arithmetic and copies ran while one was open for 0% of the time, Pallas kernels for 9%

profile of v7, /device:TPU:56, one launch (start us, length us, event | category | flops | bytes accessed | tf_op | source)
XLA Modules:
  0.0 76.9 jit_solution(17919649267240166878)
XLA Ops:
  0.0 0.0 copy-start.2
  0.0 0.0 copy-start.3
  0.0 0.3 tables.1
  0.3 0.0 copy-start
  0.3 1.5 %copy-done = f32[16,32,864]{2,1,0:T(8,128)S(1)} copy-done((f32[16,32,864]{2,1,0:T(8,128)S(1)}, f32[16,32,864]{2,1,0:T(8,128)}, u32[]{:S(2)}) %copy-start) | copy-done | bytes 1769496
  1.8 0.0 copy-start.1
  1.8 0.7 first_moments.1
  2.5 16.2 %all_to_all.10.gathered_ref = f32[16,52,128]{2,1,0:T(8,128)S(1)} all-to-all(f32[16,52,128]{2,1,0:T(8,128)S(1)} %broadcast_in_dim.24), channel_id=1, replica_groups=mesh['sx'=8,'sy'=4,'vel'=16] {'vel'}, dimensions={0} | all-to-all | bytes 851968 | tf_op jit(solution)/shard_map/all_to_all | solution.py:581
  18.7 0.0 copy-done.2
  18.7 0.0 copy-done.3
  18.7 0.0 copy-done.1
  18.7 1.0 %relax.2 = (f32[512,896]{1,0:T(8,128)S(1)}, f32[48,896]{1,0:T(8,128)S(1)}, f32[48,896]{1,0:T(8,128)S(1)}, f32[24,896]{1,0:T(8,128)S(1)}, f32[24,896]{1,0:T(8,128)S(1)}, /*index=5*/f32[128,128]{1,0:T(8,128)S(1)}) custom-call(s32[1]{0:T(128)} %bitcast.1.odd_x_ref, s32[1]{0:T(128)} %bitcast.2.odd_y_ref, f32[16,52,128]{2,1,0:T(8,128)S(1)} %all_to_all.10.gathered_ref, ...), custom_call_target="tpu_custom_call" | custom-call | tf_op jit(solution)/shard_map/relax/pallas_call | solution.py:633
  19.7 6.1 %collective-permute-start.1 = (f32[24,896]{1,0:T(8,128)S(1)}, f32[24,896]{1,0:T(8,128)S(1)}, u32[]{:S(2)}, u32[]{:S(2)}) collective-permute-start(f32[24,896]{1,0:T(8,128)S(1)} %get-tuple-element.39), channel_id=1, source_target_pairs={{0,16},{32,48},{16,0},{48,32},{1,17},{33,49},{17,1},{49,33},{2,18}... | collective-permute-start | bytes 258056 | tf_op jit(solution)/shard_map/ppermute | solution.py:644
  25.8 6.4 %collective-permute-start.2 = (f32[24,896]{1,0:T(8,128)S(1)}, f32[24,896]{1,0:T(8,128)S(1)}, u32[]{:S(2)}, u32[]{:S(2)}) collective-permute-start(f32[24,896]{1,0:T(8,128)S(1)} %get-tuple-element.40), channel_id=1, source_target_pairs={{16,32},{48,0},{32,16},{0,48},{17,33},{49,1},{33,17},{1,49},{18,34... | collective-permute-start | bytes 258056 | tf_op jit(solution)/shard_map/ppermute | solution.py:644
  32.2 3.3 %collective-permute-start.3 = (f32[48,896]{1,0:T(8,128)S(1)}, f32[48,896]{1,0:T(8,128)S(1)}, u32[]{:S(2)}, u32[]{:S(2)}) collective-permute-start(f32[48,896]{1,0:T(8,128)S(1)} %get-tuple-element.44), channel_id=1, source_target_pairs={{0,64},{128,192},{256,320},{384,448},{64,0},{192,128},{320,256},{4... | collective-permute-start | bytes 516104 | tf_op jit(solution)/shard_map/ppermute | solution.py:646
  35.5 1.9 %collective-permute-start = (f32[48,896]{1,0:T(8,128)S(1)}, f32[48,896]{1,0:T(8,128)S(1)}, u32[]{:S(2)}, u32[]{:S(2)}) collective-permute-start(f32[48,896]{1,0:T(8,128)S(1)} %get-tuple-element.38), channel_id=1, source_target_pairs={{64,128},{192,256},{320,384},{448,0},{128,64},{256,192},{384,320},... | collective-permute-start | bytes 516104 | tf_op jit(solution)/shard_map/ppermute | solution.py:647
  37.4 0.0 collective-permute-done.1.first_y_ref
  37.4 0.0 collective-permute-done.2.second_y_ref
  37.4 2.7 %inner.1 = (f32[384,896]{1,0:T(8,128)S(1)}, f32[64,128]{1,0:T(8,128)S(1)}, f32[7,128,128]{2,1,0:T(8,128)S(1)}) custom-call(s32[1]{0:T(128)} %bitcast.2.odd_y_ref, f32[512,896]{1,0:T(8,128)S(1)} %get-tuple-element.37.state_ref, f32[24,896]{1,0:T(8,128)S(1)} %collective-permute-done.1.first_y_ref, f32[24,896]{1,0:T(8,128)S(1)} %collective-permute-done.2.second_y_ref, ...), custom_call_target="tpu_custom_call" | custom-call | flops 1100000000 | bytes 1000 | tf_op jit(solution)/shard_map/inner/pallas_call | solution.py:682
  40.1 0.0 collective-permute-done.3.side_x_ref
  40.1 0.6 outer_first.1
  40.7 3.3 %collective-permute-done.side_x_ref = f32[48,896]{1,0:T(8,128)S(1)} collective-permute-done((f32[48,896]{1,0:T(8,128)S(1)}, f32[48,896]{1,0:T(8,128)S(1)}, u32[]{:S(2)}, u32[]{:S(2)}) %collective-permute-start) | collective-permute-done | bytes 172064 | tf_op jit(solution)/shard_map/ppermute | solution.py:647
  44.0 0.6 outer_second.1
  44.7 12.8 %all_to_all.11.gathered_ref = f32[16,52,128]{2,1,0:T(8,128)S(1)} all-to-all(f32[16,52,128]{2,1,0:T(8,128)S(1)} %broadcast_in_dim.25), channel_id=1, replica_groups=mesh['sx'=8,'sy'=4,'vel'=16] {'vel'}, dimensions={0} | all-to-all | bytes 851968 | tf_op jit(solution)/shard_map/all_to_all | solution.py:581
  57.4 1.0 %relax.3 = (f32[512,896]{1,0:T(8,128)S(1)}, f32[48,896]{1,0:T(8,128)S(1)}, f32[48,896]{1,0:T(8,128)S(1)}, f32[24,896]{1,0:T(8,128)S(1)}, f32[24,896]{1,0:T(8,128)S(1)}, /*index=5*/f32[128,128]{1,0:T(8,128)S(1)}) custom-call(s32[1]{0:T(128)} %bitcast.1.odd_x_ref, s32[1]{0:T(128)} %bitcast.2.odd_y_ref, f32[16,52,128]{2,1,0:T(8,128)S(1)} %all_to_all.11.gathered_ref, ...), custom_call_target="tpu_custom_call" | custom-call | tf_op jit(solution)/shard_map/relax/pallas_call | solution.py:633
  58.4 4.3 %collective-permute-start.5 = (f32[24,896]{1,0:T(8,128)S(1)}, f32[24,896]{1,0:T(8,128)S(1)}, u32[]{:S(2)}, u32[]{:S(2)}) collective-permute-start(f32[24,896]{1,0:T(8,128)S(1)} %get-tuple-element.53), channel_id=1, source_target_pairs={{0,16},{32,48},{16,0},{48,32},{1,17},{33,49},{17,1},{49,33},{2,18}... | collective-permute-start | bytes 258056 | tf_op jit(solution)/shard_map/ppermute | solution.py:644
  62.7 2.1 %collective-permute-start.6 = (f32[24,896]{1,0:T(8,128)S(1)}, f32[24,896]{1,0:T(8,128)S(1)}, u32[]{:S(2)}, u32[]{:S(2)}) collective-permute-start(f32[24,896]{1,0:T(8,128)S(1)} %get-tuple-element.54), channel_id=1, source_target_pairs={{16,32},{48,0},{32,16},{0,48},{17,33},{49,1},{33,17},{1,49},{18,34... | collective-permute-start | bytes 258056 | tf_op jit(solution)/shard_map/ppermute | solution.py:644
  64.8 2.5 %collective-permute-start.7 = (f32[48,896]{1,0:T(8,128)S(1)}, f32[48,896]{1,0:T(8,128)S(1)}, u32[]{:S(2)}, u32[]{:S(2)}) collective-permute-start(f32[48,896]{1,0:T(8,128)S(1)} %get-tuple-element.57), channel_id=1, source_target_pairs={{0,64},{128,192},{256,320},{384,448},{64,0},{192,128},{320,256},{4... | collective-permute-start | bytes 516104 | tf_op jit(solution)/shard_map/ppermute | solution.py:646
  67.4 1.9 %collective-permute-start.4 = (f32[48,896]{1,0:T(8,128)S(1)}, f32[48,896]{1,0:T(8,128)S(1)}, u32[]{:S(2)}, u32[]{:S(2)}) collective-permute-start(f32[48,896]{1,0:T(8,128)S(1)} %get-tuple-element.52), channel_id=1, source_target_pairs={{64,128},{192,256},{320,384},{448,0},{128,64},{256,192},{384,320},... | collective-permute-start | bytes 516104 | tf_op jit(solution)/shard_map/ppermute | solution.py:647
  69.3 0.0 collective-permute-done.5.first_y_ref
  69.3 1.9 %collective-permute-done.6.second_y_ref = f32[24,896]{1,0:T(8,128)S(1)} collective-permute-done((f32[24,896]{1,0:T(8,128)S(1)}, f32[24,896]{1,0:T(8,128)S(1)}, u32[]{:S(2)}, u32[]{:S(2)}) %collective-permute-start.6) | collective-permute-done | bytes 86048 | tf_op jit(solution)/shard_map/ppermute | solution.py:644
  71.2 3.0 %last_inner.1 = (f32[16,32,864]{2,1,0:T(8,128)}, f32[7,128,128]{2,1,0:T(8,128)S(1)}) custom-call(s32[1]{0:T(128)} %bitcast.2.odd_y_ref, f32[512,896]{1,0:T(8,128)S(1)} %get-tuple-element.51.state_ref, f32[24,896]{1,0:T(8,128)S(1)} %collective-permute-done.5.first_y_ref, f32[24,896]{1,0:T(8,128)S(1)} %collective-permute-done.6.second_y_ref, ...), custom_call_target="tpu_custom_call" | custom-call | flops 1100000000 | bytes 1000 | tf_op jit(solution)/shard_map/last_inner/pallas_call | solution.py:652
  74.3 0.0 collective-permute-done.7.side_x_ref
  74.3 0.4 last_first.1.refs_0_
  74.6 1.2 %collective-permute-done.4.side_x_ref = f32[48,896]{1,0:T(8,128)S(1)} collective-permute-done((f32[48,896]{1,0:T(8,128)S(1)}, f32[48,896]{1,0:T(8,128)S(1)}, u32[]{:S(2)}, u32[]{:S(2)}) %collective-permute-start.4) | collective-permute-done | bytes 172064 | tf_op jit(solution)/shard_map/ppermute | solution.py:647
  75.9 1.0 %last_second.1 = f32[16,32,864]{2,1,0:T(8,128)} custom-call(s32[1]{0:T(128)} %bitcast.1.odd_x_ref, f32[512,896]{1,0:T(8,128)S(1)} %get-tuple-element.51.state_ref, f32[48,896]{1,0:T(8,128)S(1)} %collective-permute-done.4.side_x_ref, f32[7,128,128]{2,1,0:T(8,128)S(1)} %get-tuple-element.56.side_ref, ...), custom_call_target="tpu_custom_call", output_to_operand_aliasing={{}: (6, {})} | custom-call | tf_op jit(solution)/shard_map/last_second/pallas_call | solution.py:673
  (2 shorter events, 0.1 us)
Async XLA Ops:
  0.0 18.7 %copy-start.2 = (f32[16,32]{1,0:T(8,128)S(1)}, f32[16,32]{1,0:T(8,128)}, u32[]{:S(2)}) copy-start(f32[16,32]{1,0:T(8,128)} %knudsen_ref.3) | copy-start | bytes 6148
  0.0 18.7 %copy-start.3 = (s32[16,32]{1,0:T(8,128)S(1)}, s32[16,32]{1,0:T(8,128)}, u32[]{:S(2)}) copy-start(s32[16,32]{1,0:T(8,128)} %kind_ref.3) | copy-start | bytes 6148
  0.3 1.5 %copy-start = (f32[16,32,864]{2,1,0:T(8,128)S(1)}, f32[16,32,864]{2,1,0:T(8,128)}, u32[]{:S(2)}) copy-start(f32[16,32,864]{2,1,0:T(8,128)} %refs_0_.3) | copy-start | bytes 5308420
  1.8 16.9 %copy-start.1 = (f32[16,32,864]{2,1,0:T(8,128)S(1)}, f32[16,32,864]{2,1,0:T(8,128)}, u32[]{:S(2)}) copy-start(f32[16,32,864]{2,1,0:T(8,128)} %refs_0_.3) | copy-start | bytes 5308420
  19.7 17.7 %collective-permute-start.1 = (f32[24,896]{1,0:T(8,128)S(1)}, f32[24,896]{1,0:T(8,128)S(1)}, u32[]{:S(2)}, u32[]{:S(2)}) collective-permute-start(f32[24,896]{1,0:T(8,128)S(1)} %get-tuple-element.39), channel_id=1, source_target_pairs={{0,16},{32,48},{16,0},{48,32},{1,17},{33,49},{17,1},{49,33},{2,18}... | collective-permute-start | bytes 258056 | tf_op jit(solution)/shard_map/ppermute | solution.py:644
  25.8 11.6 %collective-permute-start.2 = (f32[24,896]{1,0:T(8,128)S(1)}, f32[24,896]{1,0:T(8,128)S(1)}, u32[]{:S(2)}, u32[]{:S(2)}) collective-permute-start(f32[24,896]{1,0:T(8,128)S(1)} %get-tuple-element.40), channel_id=1, source_target_pairs={{16,32},{48,0},{32,16},{0,48},{17,33},{49,1},{33,17},{1,49},{18,34... | collective-permute-start | bytes 258056 | tf_op jit(solution)/shard_map/ppermute | solution.py:644
  32.2 7.9 %collective-permute-start.3 = (f32[48,896]{1,0:T(8,128)S(1)}, f32[48,896]{1,0:T(8,128)S(1)}, u32[]{:S(2)}, u32[]{:S(2)}) collective-permute-start(f32[48,896]{1,0:T(8,128)S(1)} %get-tuple-element.44), channel_id=1, source_target_pairs={{0,64},{128,192},{256,320},{384,448},{64,0},{192,128},{320,256},{4... | collective-permute-start | bytes 516104 | tf_op jit(solution)/shard_map/ppermute | solution.py:646
  35.5 8.5 %collective-permute-start = (f32[48,896]{1,0:T(8,128)S(1)}, f32[48,896]{1,0:T(8,128)S(1)}, u32[]{:S(2)}, u32[]{:S(2)}) collective-permute-start(f32[48,896]{1,0:T(8,128)S(1)} %get-tuple-element.38), channel_id=1, source_target_pairs={{64,128},{192,256},{320,384},{448,0},{128,64},{256,192},{384,320},... | collective-permute-start | bytes 516104 | tf_op jit(solution)/shard_map/ppermute | solution.py:647
  58.4 10.9 %collective-permute-start.5 = (f32[24,896]{1,0:T(8,128)S(1)}, f32[24,896]{1,0:T(8,128)S(1)}, u32[]{:S(2)}, u32[]{:S(2)}) collective-permute-start(f32[24,896]{1,0:T(8,128)S(1)} %get-tuple-element.53), channel_id=1, source_target_pairs={{0,16},{32,48},{16,0},{48,32},{1,17},{33,49},{17,1},{49,33},{2,18}... | collective-permute-start | bytes 258056 | tf_op jit(solution)/shard_map/ppermute | solution.py:644
  62.7 8.5 %collective-permute-start.6 = (f32[24,896]{1,0:T(8,128)S(1)}, f32[24,896]{1,0:T(8,128)S(1)}, u32[]{:S(2)}, u32[]{:S(2)}) collective-permute-start(f32[24,896]{1,0:T(8,128)S(1)} %get-tuple-element.54), channel_id=1, source_target_pairs={{16,32},{48,0},{32,16},{0,48},{17,33},{49,1},{33,17},{1,49},{18,34... | collective-permute-start | bytes 258056 | tf_op jit(solution)/shard_map/ppermute | solution.py:644
  64.8 9.4 %collective-permute-start.7 = (f32[48,896]{1,0:T(8,128)S(1)}, f32[48,896]{1,0:T(8,128)S(1)}, u32[]{:S(2)}, u32[]{:S(2)}) collective-permute-start(f32[48,896]{1,0:T(8,128)S(1)} %get-tuple-element.57), channel_id=1, source_target_pairs={{0,64},{128,192},{256,320},{384,448},{64,0},{192,128},{320,256},{4... | collective-permute-start | bytes 516104 | tf_op jit(solution)/shard_map/ppermute | solution.py:646
  67.4 8.5 %collective-permute-start.4 = (f32[48,896]{1,0:T(8,128)S(1)}, f32[48,896]{1,0:T(8,128)S(1)}, u32[]{:S(2)}, u32[]{:S(2)}) collective-permute-start(f32[48,896]{1,0:T(8,128)S(1)} %get-tuple-element.52), channel_id=1, source_target_pairs={{64,128},{192,256},{320,384},{448,0},{128,64},{256,192},{384,320},... | collective-permute-start | bytes 516104 | tf_op jit(solution)/shard_map/ppermute | solution.py:647

commit v8 on v7

--- a/solution.py
+++ b/solution.py
@@ -581,10 +581,13 @@
     return lax.all_to_all(copies, "vel", 0, 0)
 
 
+OFFSETS = {"sx": 0, "sy": 1}
+
+
 def partners(axis):
     devices = lax.axis_size(axis)
     pairs = []
-    for first in (0, 1):
+    for first in (OFFSETS[axis], 1 - OFFSETS[axis]):
         couples = [((i + first) % devices, (i + first + 1) % devices) for i in range(0, devices, 2)]
         pairs.append(couples + [(b, a) for a, b in couples])
     return pairs
@@ -604,8 +607,8 @@
             jnp.full((1,), value, jnp.int32)
             for value in (
                 lax.axis_index("vel") * velocities,
-                lax.axis_index("sx") % 2,
-                lax.axis_index("sy") % 2,
+                (lax.axis_index("sx") + OFFSETS["sx"]) % 2,
+                (lax.axis_index("sy") + OFFSETS["sy"]) % 2,
             )
         )
     )

time: 77.3 us -> 76.7 us (level)
    ppermute x2, starting transfers between devices: 10.4 us -> 12.1 us  [body(): lax.ppermute(first_y, 'sy', to_first)]
    ppermute x2, starting transfers between devices: 8.49 us -> 6.74 us  [body(): lax.ppermute(second_y, 'sy', to_second)]
    ppermute x2, waiting for transfers between devices: 1.93 us -> 1.01 us  [body(): lax.ppermute(second_y, 'sy', to_second)]
  transfers between devices with their start and end apart: 8 -> 8, of which waited for: 3 -> 4; matrix products, arithmetic and copies ran while one was open for 0% -> 0% of each run, Pallas kernels for 9% -> 9%
where the time goes in v8:
time: 76.7 us; the launch traced here: 76.3 us
  blocking collectives  28.9 us (38%)
  starting transfers between devices  28.2 us (37%)
  Pallas kernels  11.2 us (15%)
  waiting for transfers between devices  6.19 us (8%)
  local copies, waits for them, and re-layouts  1.6 us (2%)
    all_to_all x2, blocking collectives, gather(): return lax.all_to_all(copies, 'vel', 0, 0)  28.9 us
    ppermute x2, starting transfers between devices, body(): lax.ppermute(first_y, 'sy', to_first)  12.1 us
    ppermute x2, starting transfers between devices, body(): lax.ppermute(second_y, 'sy', to_second)  6.74 us
    ppermute x2, starting transfers between devices, body(): first_x = lax.ppermute(first_x, 'sx', to_first)  5.18 us
    ppermute x2, waiting for transfers between devices, body(): second_x = lax.ppermute(second_x, 'sx', to_second)  5.17 us
    ppermute x2, starting transfers between devices, body(): second_x = lax.ppermute(second_x, 'sx', to_second)  4.12 us
    pallas_call x1, Pallas kernels, body(): call(functools.partial(inner_kernel, ny, velocities), 'last_inner', (rows...  3.04 us
    pallas_call x1, Pallas kernels, body(): call(functools.partial(inner_kernel, ny, None), 'inner', (rows_of(cells -...  2.67 us
  transfers between devices with their start and end apart: 8, of which 4 were waited for; matrix products, arithmetic and copies ran while one was open for 0% of the time, Pallas kernels for 9%

profile of v8, /device:TPU:56, one launch (start us, length us, event | category | flops | bytes accessed | tf_op | source)
XLA Modules:
  0.0 76.3 jit_solution(9598996176339701698)
XLA Ops:
  0.0 0.0 copy-start.2
  0.0 0.0 copy-start.3
  0.0 0.3 tables.1
  0.3 0.0 copy-start
  0.3 1.5 %copy-done = f32[16,32,864]{2,1,0:T(8,128)S(1)} copy-done((f32[16,32,864]{2,1,0:T(8,128)S(1)}, f32[16,32,864]{2,1,0:T(8,128)}, u32[]{:S(2)}) %copy-start) | copy-done | bytes 1769496
  1.8 0.0 copy-start.1
  1.8 0.7 first_moments.1
  2.5 16.2 %all_to_all.10.gathered_ref = f32[16,52,128]{2,1,0:T(8,128)S(1)} all-to-all(f32[16,52,128]{2,1,0:T(8,128)S(1)} %broadcast_in_dim.24), channel_id=1, replica_groups=mesh['sx'=8,'sy'=4,'vel'=16] {'vel'}, dimensions={0} | all-to-all | bytes 851968 | tf_op jit(solution)/shard_map/all_to_all | solution.py:581
  18.7 0.0 copy-done.2
  18.7 0.0 copy-done.3
  18.7 0.0 copy-done.1
  18.7 1.0 %relax.2 = (f32[512,896]{1,0:T(8,128)S(1)}, f32[48,896]{1,0:T(8,128)S(1)}, f32[48,896]{1,0:T(8,128)S(1)}, f32[24,896]{1,0:T(8,128)S(1)}, f32[24,896]{1,0:T(8,128)S(1)}, /*index=5*/f32[128,128]{1,0:T(8,128)S(1)}) custom-call(s32[1]{0:T(128)} %bitcast.1.odd_x_ref, s32[1]{0:T(128)} %bitcast.2.odd_y_ref, f32[16,52,128]{2,1,0:T(8,128)S(1)} %all_to_all.10.gathered_ref, ...), custom_call_target="tpu_custom_call" | custom-call | tf_op jit(solution)/shard_map/relax/pallas_call | solution.py:636
  19.7 10.0 %collective-permute-start.1 = (f32[24,896]{1,0:T(8,128)S(1)}, f32[24,896]{1,0:T(8,128)S(1)}, u32[]{:S(2)}, u32[]{:S(2)}) collective-permute-start(f32[24,896]{1,0:T(8,128)S(1)} %get-tuple-element.39), channel_id=1, source_target_pairs={{16,32},{48,0},{32,16},{0,48},{17,33},{49,1},{33,17},{1,49},{18,34... | collective-permute-start | bytes 258056 | tf_op jit(solution)/shard_map/ppermute | solution.py:647
  29.7 2.5 %collective-permute-start.2 = (f32[24,896]{1,0:T(8,128)S(1)}, f32[24,896]{1,0:T(8,128)S(1)}, u32[]{:S(2)}, u32[]{:S(2)}) collective-permute-start(f32[24,896]{1,0:T(8,128)S(1)} %get-tuple-element.40), channel_id=1, source_target_pairs={{0,16},{32,48},{16,0},{48,32},{1,17},{33,49},{17,1},{49,33},{2,18}... | collective-permute-start | bytes 258056 | tf_op jit(solution)/shard_map/ppermute | solution.py:647
  32.2 3.3 %collective-permute-start.3 = (f32[48,896]{1,0:T(8,128)S(1)}, f32[48,896]{1,0:T(8,128)S(1)}, u32[]{:S(2)}, u32[]{:S(2)}) collective-permute-start(f32[48,896]{1,0:T(8,128)S(1)} %get-tuple-element.44), channel_id=1, source_target_pairs={{0,64},{128,192},{256,320},{384,448},{64,0},{192,128},{320,256},{4... | collective-permute-start | bytes 516104 | tf_op jit(solution)/shard_map/ppermute | solution.py:649
  35.5 1.9 %collective-permute-start = (f32[48,896]{1,0:T(8,128)S(1)}, f32[48,896]{1,0:T(8,128)S(1)}, u32[]{:S(2)}, u32[]{:S(2)}) collective-permute-start(f32[48,896]{1,0:T(8,128)S(1)} %get-tuple-element.38), channel_id=1, source_target_pairs={{64,128},{192,256},{320,384},{448,0},{128,64},{256,192},{384,320},... | collective-permute-start | bytes 516104 | tf_op jit(solution)/shard_map/ppermute | solution.py:650
  37.4 0.0 collective-permute-done.1.first_y_ref
  37.4 0.6 collective-permute-done.2.second_y_ref
  38.0 2.7 %inner.1 = (f32[384,896]{1,0:T(8,128)S(1)}, f32[64,128]{1,0:T(8,128)S(1)}, f32[7,128,128]{2,1,0:T(8,128)S(1)}) custom-call(s32[1]{0:T(128)} %bitcast.2.odd_y_ref, f32[512,896]{1,0:T(8,128)S(1)} %get-tuple-element.37.state_ref, f32[24,896]{1,0:T(8,128)S(1)} %collective-permute-done.1.first_y_ref, f32[24,896]{1,0:T(8,128)S(1)} %collective-permute-done.2.second_y_ref, ...), custom_call_target="tpu_custom_call" | custom-call | flops 1100000000 | bytes 1000 | tf_op jit(solution)/shard_map/inner/pallas_call | solution.py:685
  40.6 0.0 collective-permute-done.3.side_x_ref
  40.6 0.6 outer_first.1
  41.2 2.7 %collective-permute-done.side_x_ref = f32[48,896]{1,0:T(8,128)S(1)} collective-permute-done((f32[48,896]{1,0:T(8,128)S(1)}, f32[48,896]{1,0:T(8,128)S(1)}, u32[]{:S(2)}, u32[]{:S(2)}) %collective-permute-start) | collective-permute-done | bytes 172064 | tf_op jit(solution)/shard_map/ppermute | solution.py:650
  44.0 0.6 outer_second.1
  44.7 12.8 %all_to_all.11.gathered_ref = f32[16,52,128]{2,1,0:T(8,128)S(1)} all-to-all(f32[16,52,128]{2,1,0:T(8,128)S(1)} %broadcast_in_dim.25), channel_id=1, replica_groups=mesh['sx'=8,'sy'=4,'vel'=16] {'vel'}, dimensions={0} | all-to-all | bytes 851968 | tf_op jit(solution)/shard_map/all_to_all | solution.py:581
  57.4 1.0 %relax.3 = (f32[512,896]{1,0:T(8,128)S(1)}, f32[48,896]{1,0:T(8,128)S(1)}, f32[48,896]{1,0:T(8,128)S(1)}, f32[24,896]{1,0:T(8,128)S(1)}, f32[24,896]{1,0:T(8,128)S(1)}, /*index=5*/f32[128,128]{1,0:T(8,128)S(1)}) custom-call(s32[1]{0:T(128)} %bitcast.1.odd_x_ref, s32[1]{0:T(128)} %bitcast.2.odd_y_ref, f32[16,52,128]{2,1,0:T(8,128)S(1)} %all_to_all.11.gathered_ref, ...), custom_call_target="tpu_custom_call" | custom-call | tf_op jit(solution)/shard_map/relax/pallas_call | solution.py:636
  58.4 2.1 %collective-permute-start.5 = (f32[24,896]{1,0:T(8,128)S(1)}, f32[24,896]{1,0:T(8,128)S(1)}, u32[]{:S(2)}, u32[]{:S(2)}) collective-permute-start(f32[24,896]{1,0:T(8,128)S(1)} %get-tuple-element.53), channel_id=1, source_target_pairs={{16,32},{48,0},{32,16},{0,48},{17,33},{49,1},{33,17},{1,49},{18,34... | collective-permute-start | bytes 258056 | tf_op jit(solution)/shard_map/ppermute | solution.py:647
  60.5 4.3 %collective-permute-start.6 = (f32[24,896]{1,0:T(8,128)S(1)}, f32[24,896]{1,0:T(8,128)S(1)}, u32[]{:S(2)}, u32[]{:S(2)}) collective-permute-start(f32[24,896]{1,0:T(8,128)S(1)} %get-tuple-element.54), channel_id=1, source_target_pairs={{0,16},{32,48},{16,0},{48,32},{1,17},{33,49},{17,1},{49,33},{2,18}... | collective-permute-start | bytes 258056 | tf_op jit(solution)/shard_map/ppermute | solution.py:647
  64.8 1.9 %collective-permute-start.7 = (f32[48,896]{1,0:T(8,128)S(1)}, f32[48,896]{1,0:T(8,128)S(1)}, u32[]{:S(2)}, u32[]{:S(2)}) collective-permute-start(f32[48,896]{1,0:T(8,128)S(1)} %get-tuple-element.57), channel_id=1, source_target_pairs={{0,64},{128,192},{256,320},{384,448},{64,0},{192,128},{320,256},{4... | collective-permute-start | bytes 516104 | tf_op jit(solution)/shard_map/ppermute | solution.py:649
  66.7 2.2 %collective-permute-start.4 = (f32[48,896]{1,0:T(8,128)S(1)}, f32[48,896]{1,0:T(8,128)S(1)}, u32[]{:S(2)}, u32[]{:S(2)}) collective-permute-start(f32[48,896]{1,0:T(8,128)S(1)} %get-tuple-element.52), channel_id=1, source_target_pairs={{64,128},{192,256},{320,384},{448,0},{128,64},{256,192},{384,320},... | collective-permute-start | bytes 516104 | tf_op jit(solution)/shard_map/ppermute | solution.py:650
  69.0 0.0 collective-permute-done.5.first_y_ref
  69.0 0.4 collective-permute-done.6.second_y_ref
  69.4 3.0 %last_inner.1 = (f32[16,32,864]{2,1,0:T(8,128)}, f32[7,128,128]{2,1,0:T(8,128)S(1)}) custom-call(s32[1]{0:T(128)} %bitcast.2.odd_y_ref, f32[512,896]{1,0:T(8,128)S(1)} %get-tuple-element.51.state_ref, f32[24,896]{1,0:T(8,128)S(1)} %collective-permute-done.5.first_y_ref, f32[24,896]{1,0:T(8,128)S(1)} %collective-permute-done.6.second_y_ref, ...), custom_call_target="tpu_custom_call" | custom-call | flops 1100000000 | bytes 1000 | tf_op jit(solution)/shard_map/last_inner/pallas_call | solution.py:655
  72.5 0.0 collective-permute-done.7.side_x_ref
  72.5 0.4 last_first.1.refs_0_
  72.8 2.4 %collective-permute-done.4.side_x_ref = f32[48,896]{1,0:T(8,128)S(1)} collective-permute-done((f32[48,896]{1,0:T(8,128)S(1)}, f32[48,896]{1,0:T(8,128)S(1)}, u32[]{:S(2)}, u32[]{:S(2)}) %collective-permute-start.4) | collective-permute-done | bytes 172064 | tf_op jit(solution)/shard_map/ppermute | solution.py:650
  75.3 1.0 %last_second.1 = f32[16,32,864]{2,1,0:T(8,128)} custom-call(s32[1]{0:T(128)} %bitcast.1.odd_x_ref, f32[512,896]{1,0:T(8,128)S(1)} %get-tuple-element.51.state_ref, f32[48,896]{1,0:T(8,128)S(1)} %collective-permute-done.4.side_x_ref, f32[7,128,128]{2,1,0:T(8,128)S(1)} %get-tuple-element.56.side_ref, ...), custom_call_target="tpu_custom_call", output_to_operand_aliasing={{}: (6, {})} | custom-call | tf_op jit(solution)/shard_map/last_second/pallas_call | solution.py:676
  (2 shorter events, 0.1 us)
Async XLA Ops:
  0.0 18.7 %copy-start.2 = (f32[16,32]{1,0:T(8,128)S(1)}, f32[16,32]{1,0:T(8,128)}, u32[]{:S(2)}) copy-start(f32[16,32]{1,0:T(8,128)} %knudsen_ref.3) | copy-start | bytes 6148
  0.0 18.7 %copy-start.3 = (s32[16,32]{1,0:T(8,128)S(1)}, s32[16,32]{1,0:T(8,128)}, u32[]{:S(2)}) copy-start(s32[16,32]{1,0:T(8,128)} %kind_ref.3) | copy-start | bytes 6148
  0.3 1.5 %copy-start = (f32[16,32,864]{2,1,0:T(8,128)S(1)}, f32[16,32,864]{2,1,0:T(8,128)}, u32[]{:S(2)}) copy-start(f32[16,32,864]{2,1,0:T(8,128)} %refs_0_.3) | copy-start | bytes 5308420
  1.8 16.9 %copy-start.1 = (f32[16,32,864]{2,1,0:T(8,128)S(1)}, f32[16,32,864]{2,1,0:T(8,128)}, u32[]{:S(2)}) copy-start(f32[16,32,864]{2,1,0:T(8,128)} %refs_0_.3) | copy-start | bytes 5308420
  19.7 17.7 %collective-permute-start.1 = (f32[24,896]{1,0:T(8,128)S(1)}, f32[24,896]{1,0:T(8,128)S(1)}, u32[]{:S(2)}, u32[]{:S(2)}) collective-permute-start(f32[24,896]{1,0:T(8,128)S(1)} %get-tuple-element.39), channel_id=1, source_target_pairs={{16,32},{48,0},{32,16},{0,48},{17,33},{49,1},{33,17},{1,49},{18,34... | collective-permute-start | bytes 258056 | tf_op jit(solution)/shard_map/ppermute | solution.py:647
  29.7 8.2 %collective-permute-start.2 = (f32[24,896]{1,0:T(8,128)S(1)}, f32[24,896]{1,0:T(8,128)S(1)}, u32[]{:S(2)}, u32[]{:S(2)}) collective-permute-start(f32[24,896]{1,0:T(8,128)S(1)} %get-tuple-element.40), channel_id=1, source_target_pairs={{0,16},{32,48},{16,0},{48,32},{1,17},{33,49},{17,1},{49,33},{2,18}... | collective-permute-start | bytes 258056 | tf_op jit(solution)/shard_map/ppermute | solution.py:647
  32.2 8.4 %collective-permute-start.3 = (f32[48,896]{1,0:T(8,128)S(1)}, f32[48,896]{1,0:T(8,128)S(1)}, u32[]{:S(2)}, u32[]{:S(2)}) collective-permute-start(f32[48,896]{1,0:T(8,128)S(1)} %get-tuple-element.44), channel_id=1, source_target_pairs={{0,64},{128,192},{256,320},{384,448},{64,0},{192,128},{320,256},{4... | collective-permute-start | bytes 516104 | tf_op jit(solution)/shard_map/ppermute | solution.py:649
  35.5 8.5 %collective-permute-start = (f32[48,896]{1,0:T(8,128)S(1)}, f32[48,896]{1,0:T(8,128)S(1)}, u32[]{:S(2)}, u32[]{:S(2)}) collective-permute-start(f32[48,896]{1,0:T(8,128)S(1)} %get-tuple-element.38), channel_id=1, source_target_pairs={{64,128},{192,256},{320,384},{448,0},{128,64},{256,192},{384,320},... | collective-permute-start | bytes 516104 | tf_op jit(solution)/shard_map/ppermute | solution.py:650
  58.4 10.5 %collective-permute-start.5 = (f32[24,896]{1,0:T(8,128)S(1)}, f32[24,896]{1,0:T(8,128)S(1)}, u32[]{:S(2)}, u32[]{:S(2)}) collective-permute-start(f32[24,896]{1,0:T(8,128)S(1)} %get-tuple-element.53), channel_id=1, source_target_pairs={{16,32},{48,0},{32,16},{0,48},{17,33},{49,1},{33,17},{1,49},{18,34... | collective-permute-start | bytes 258056 | tf_op jit(solution)/shard_map/ppermute | solution.py:647
  60.5 8.9 %collective-permute-start.6 = (f32[24,896]{1,0:T(8,128)S(1)}, f32[24,896]{1,0:T(8,128)S(1)}, u32[]{:S(2)}, u32[]{:S(2)}) collective-permute-start(f32[24,896]{1,0:T(8,128)S(1)} %get-tuple-element.54), channel_id=1, source_target_pairs={{0,16},{32,48},{16,0},{48,32},{1,17},{33,49},{17,1},{49,33},{2,18}... | collective-permute-start | bytes 258056 | tf_op jit(solution)/shard_map/ppermute | solution.py:647
  64.8 7.6 %collective-permute-start.7 = (f32[48,896]{1,0:T(8,128)S(1)}, f32[48,896]{1,0:T(8,128)S(1)}, u32[]{:S(2)}, u32[]{:S(2)}) collective-permute-start(f32[48,896]{1,0:T(8,128)S(1)} %get-tuple-element.57), channel_id=1, source_target_pairs={{0,64},{128,192},{256,320},{384,448},{64,0},{192,128},{320,256},{4... | collective-permute-start | bytes 516104 | tf_op jit(solution)/shard_map/ppermute | solution.py:649
  66.7 8.5 %collective-permute-start.4 = (f32[48,896]{1,0:T(8,128)S(1)}, f32[48,896]{1,0:T(8,128)S(1)}, u32[]{:S(2)}, u32[]{:S(2)}) collective-permute-start(f32[48,896]{1,0:T(8,128)S(1)} %get-tuple-element.52), channel_id=1, source_target_pairs={{64,128},{192,256},{320,384},{448,0},{128,64},{256,192},{384,320},... | collective-permute-start | bytes 516104 | tf_op jit(solution)/shard_map/ppermute | solution.py:650
